TPU v7x, 128 devices: a whole 4x4x4 slice. The times are simulated.
128 devices in a mesh: tm: 4 (over y), height: 16 (over z, x_hi, core), section: 2 (over x_lo).
Axes of the slice: x: 4 (x_hi: 2, x_lo: 2; x = x_hi * 2 + x_lo), y: 4, z: 4, core: 2. Of those that a mesh axis runs over, the one named last changes fastest.
Arguments:
- video: bfloat16 [4, 16, 4, 64, 1280], P('tm', 'height'), may hold values from -6 to 6
- target: bfloat16 [4, 16, 4, 64, 1280], P('tm', 'height'), may hold values from -6 to 6
- gain: float32 [1280], replicated, may hold values from 0.25 to 1.75
- w_qkv: bfloat16 [1280, 3, 1280], P(None, None, 'section')
- w_out: bfloat16 [1280, 1280], P('section'), may hold values from -0.8984375 to 0.8984375
- neighbours: int32 [4, 16, 4, 8], P('tm', 'height'), may hold values from 0 to 255, as said below
- counts: int32 [4, 16, 4], P('tm', 'height'), may hold values from 1 to 64, as said below
Outputs:
- video_grad: bfloat16 [4, 16, 4, 64, 1280], P('tm', 'height', None, None, 'section')
Inputs may be any that keep to these rules, and one draw needn't show every extreme that they name: `neighbours`: row i lists 8 different tube ids; the first is tube i itself, the others lie inside the clip within one tube of i along each of time, height and width. `counts`: tubes in the last height row or the last width column may be partial; all other tubes are full.
All inputs are finite; a program needn't handle non-finite values.
Results may differ from a plain program's by a relative error of at most 0.015.
Values may be sent and summed in bfloat16 or wider, within the bound.
No kernel may reach another device: no remote copies, remote signals or barrier semaphores. Data moves between devices by JAX's collectives and lax.ppermute only.
A program may use at most 192 MiB of HBM per device.

v0:
```python
import jax
import jax.numpy as jnp
from jax import lax
from jax.sharding import PartitionSpec as P

HEAD_DIM = 80


def passed_along(x, axis, by):
    count = lax.axis_size(axis)
    pairs = [(i, i + by) for i in range(count) if 0 <= i + by < count]
    return lax.ppermute(x, axis, pairs)


def with_halo(cells, sides, width):
    for axis, dim in sides:
        count = lax.axis_size(axis)
        ends = count - 1
        head = lax.slice_in_dim(cells, 0, width, axis=dim)
        tail = lax.slice_in_dim(cells, cells.shape[dim] - width, cells.shape[dim], axis=dim)
        cells = jnp.concatenate(
            [
                lax.ppermute(tail, axis, [(i, (i + 1) % count) for i in range(ends)]),
                cells,
                lax.ppermute(head, axis, [((i + 1) % count, i) for i in range(ends)]),
            ],
            axis=dim,
        )
    return cells


def attention_probs(query, keys, near_live):
    scores = jnp.einsum(
        "nqhe,nkhe->nhqk", query, keys, preferred_element_type=jnp.float32
    ) * HEAD_DIM ** (-0.5)
    scores = jnp.where(near_live[:, None, None, :] > 0, scores, -1e30)
    top = jnp.max(scores, axis=-1, keepdims=True)
    expd = jnp.exp(scores - top)
    return expd / jnp.sum(expd, axis=-1, keepdims=True)


def pass_height(piece, step):
    return passed_along(piece.astype(jnp.bfloat16), "height", step).astype(piece.dtype)


def pass_time(piece, step):
    return passed_along(piece.astype(jnp.bfloat16), "tm", step).astype(piece.dtype)


def fold_height(grads):
    inner = grads[:, 1:-1]
    inner = inner.at[:, -1].add(pass_height(grads[:, 0], -1))
    inner = inner.at[:, 0].add(pass_height(grads[:, -1], 1))
    return inner


def fold_time(grads):
    inner = grads[1:-1]
    inner = inner.at[-1].add(pass_time(grads[0], -1))
    inner = inner.at[0].add(pass_time(grads[-1], 1))
    return inner


def per_device(video, target, gain, w_qkv, w_out, neighbours, counts):
    tt, th, tw, tube, width = video.shape
    feats = w_qkv.shape[2]
    heads = feats // HEAD_DIM
    nblist = neighbours.shape[3]
    tubes = tt * th * tw
    rows = tubes * tube
    xf = video.astype(jnp.float32)
    centred_input = xf - jnp.mean(xf, axis=-1, keepdims=True)
    inverse_deviation = lax.rsqrt(
        jnp.mean(centred_input * centred_input, axis=-1, keepdims=True) + 1e-06
    )
    standardized_input = centred_input * inverse_deviation
    normalized_rows = (standardized_input * gain).astype(jnp.bfloat16)
    proj = jnp.einsum(
        "thwpd,dcj->thwpcj", normalized_rows, w_qkv, preferred_element_type=jnp.float32
    ).astype(jnp.bfloat16)
    query = proj[:, :, :, :, 0, :].reshape(tubes, tube, heads, HEAD_DIM)
    keyval = proj[:, :, :, :, 1:, :]
    positions = lax.broadcasted_iota(jnp.int32, (tt, th, tw, tube), 3)
    live_own = positions < counts[..., None]
    live = live_own.astype(jnp.bfloat16)
    ext_kv, ext_live = (
        with_halo(keyval, (("tm", 0), ("height", 1)), 1),
        with_halo(live, (("tm", 0), ("height", 1)), 1),
    )
    t_first = lax.axis_index("tm") * tt
    h_first = lax.axis_index("height") * th
    full_h = th * lax.axis_size("height")
    ids = neighbours.reshape(tubes, nblist)
    t_of = ids // (full_h * tw)
    h_of = ids // tw % full_h
    w_of = ids % tw
    local = ((t_of - t_first + 1) * (th + 2) + (h_of - h_first + 1)) * tw + w_of
    ext_tubes = (tt + 2) * (th + 2) * tw
    flat_kv = ext_kv.reshape(ext_tubes, tube, 2, feats)
    flat_live = ext_live.reshape(ext_tubes, tube)
    near_kv = flat_kv[local]
    keys = near_kv[:, :, :, 0].reshape(tubes, nblist * tube, heads, HEAD_DIM)
    values = near_kv[:, :, :, 1].reshape(tubes, nblist * tube, heads, HEAD_DIM)
    near_live = flat_live[local].reshape(tubes, nblist * tube)
    probs = attention_probs(query, keys, near_live)
    probs_low = probs.astype(jnp.bfloat16)
    attended = jnp.einsum(
        "nhqk,nkhe->nqhe", probs_low, values, preferred_element_type=jnp.float32
    ).astype(jnp.bfloat16)
    partial_out = jnp.dot(attended.reshape(rows, feats), w_out, preferred_element_type=jnp.float32)
    valid = live_own.reshape(rows, 1)
    x_rows = xf.reshape(rows, width)
    goal_rows = target.reshape(rows, width).astype(jnp.float32)
    mixed = lax.psum(partial_out.astype(jnp.bfloat16), "section").astype(jnp.float32)
    grad_feat = jnp.where(valid, 2.0 * (x_rows + mixed - goal_rows), 0.0)
    grad_low = grad_feat.astype(jnp.bfloat16)
    before = 0.5 * grad_feat
    d_att = jnp.einsum("rd,jd->rj", grad_low, w_out, preferred_element_type=jnp.float32).astype(
        jnp.bfloat16
    )
    d_att = d_att.reshape(tubes, tube, heads, HEAD_DIM)
    d_prob = jnp.einsum("nqhe,nkhe->nhqk", d_att, values, preferred_element_type=jnp.float32)
    inner = jnp.sum(d_prob * probs, axis=-1, keepdims=True)
    d_score = (probs * (d_prob - inner) * HEAD_DIM ** (-0.5)).astype(jnp.bfloat16)
    d_query = jnp.einsum(
        "nhqk,nkhe->nqhe", d_score, keys, preferred_element_type=jnp.float32
    ).astype(jnp.bfloat16)
    d_keys = jnp.einsum("nhqk,nqhe->nkhe", d_score, query, preferred_element_type=jnp.float32)
    d_values = jnp.einsum("nhqk,nqhe->nkhe", probs_low, d_att, preferred_element_type=jnp.float32)
    pieces = jnp.stack(
        [d_keys.reshape(tubes, nblist, tube, feats), d_values.reshape(tubes, nblist, tube, feats)],
        axis=3,
    )
    ext_grad = (
        jnp.zeros((ext_tubes, tube, 2, feats), jnp.float32)
        .at[local.reshape(-1)]
        .add(pieces.reshape(tubes * nblist, tube, 2, feats))
    )
    ext_grad = ext_grad.reshape(tt + 2, th + 2, tw, tube, 2, feats)
    own_grad = fold_time(fold_height(ext_grad))
    d_proj = jnp.concatenate(
        [d_query.reshape(tt, th, tw, tube, 1, feats), own_grad.astype(jnp.bfloat16)], axis=4
    )
    d_normed = jnp.einsum("thwpcj,dcj->thwpd", d_proj, w_qkv, preferred_element_type=jnp.float32)
    scaled_gradient = d_normed * gain
    correction_term = (
        scaled_gradient
        - jnp.mean(scaled_gradient, axis=-1, keepdims=True)
        - standardized_input
        * jnp.mean(scaled_gradient * standardized_input, axis=-1, keepdims=True)
    ) * inverse_deviation
    sent = correction_term.reshape(rows, width) + before
    adjoint = lax.psum_scatter(
        sent.astype(jnp.bfloat16), "section", scatter_dimension=1, tiled=True
    ).astype(jnp.float32)
    return adjoint.reshape(tt, th, tw, tube, adjoint.shape[1]).astype(jnp.bfloat16)


def solution(mesh):
    in_specs = (
        P("tm", "height", None, None, None),
        P("tm", "height", None, None, None),
        P(),
        P(None, None, "section"),
        P("section", None),
        P("tm", "height", None, None),
        P("tm", "height", None),
    )
    out_specs = P("tm", "height", None, None, "section")
    return jax.shard_map(
        per_device, mesh=mesh, in_specs=in_specs, out_specs=out_specs, check_vma=False
    )
```

profile of v0, /device:TPU:54, one launch (start us, length us, event | category | flops | bytes accessed | tf_op | source)
XLA Modules:
  0.0 410.5 jit_solution(4523836723646485427)
XLA Ops:
  19.7 12.5 %collective-permute-done.1 = bf16[1,1,4,64,2,640]{5,3,4,2,1,0:T(8,128)(2,1)S(1)} collective-permute-done((bf16[1,1,4,64,2,640]{5,3,4,2,1,0:T(8,128)(2,1)S(1)}, bf16[1,1,4,64,2,640]{5,3,4,2,1,0:T(8,128)(2,1)S(1)}, u32[]{:S(2)}, u32[]{:S(2)}) %collective-permute-start.1) | collective-permute-done | bytes 655392 | tf_op jit(solution)/shard_map/ppermute | solution.py:25
  57.8 20.2 %collective-permute-done.7 = bf16[3,1,4,64]{3,2,1,0:T(4,128)(2,1)S(1)} collective-permute-done((bf16[3,1,4,64]{3,2,1,0:T(4,128)(2,1)S(1)}, bf16[3,1,4,64]{3,2,1,0:T(4,128)(2,1)S(1)}, u32[]{:S(2)}, u32[]{:S(2)}) %collective-permute-start.7) | collective-permute-done | bytes 1568 | tf_op jit(solution)/shard_map/ppermute | solution.py:25
  77.9 6.1 %collective-permute-done.6 = bf16[3,1,4,64]{3,2,1,0:T(4,128)(2,1)S(1)} collective-permute-done((bf16[3,1,4,64]{3,2,1,0:T(4,128)(2,1)S(1)}, bf16[3,1,4,64]{3,2,1,0:T(4,128)(2,1)S(1)}, u32[]{:S(2)}, u32[]{:S(2)}) %collective-permute-start.6) | collective-permute-done | bytes 1568 | tf_op jit(solution)/shard_map/ppermute | solution.py:23
  84.7 6.6 %pad_maximum_fusion.1 = bf16[3,3,4,64,2,640]{5,3,4,2,1,0:T(8,128)(2,1)} fusion(bf16[3,1,4,64,2,640]{5,3,4,2,1,0:T(8,128)(2,1)} %collective-permute-done.3, bf16[1,1,4,64,2,640]{5,3,4,2,1,0:T(8,128)(2,1)S(1)} %collective-permute-done.1, bf16[1,1,4,64,2,640]{5,3,4,2,1,0:T(8,128)(2,1)S(1)} %slice.184, bf16[1,1,4,64,2,640]{5,3,4,2,1,0:T(8,128)(2,1)} %copy-done.5, ...), kind=kLoop, calls=%fused_computation.6 | loop fusion | flops 11796480 | bytes 11796480 | tf_op jit(solution)/shard_map/concatenate | solution.py:21
  91.4 6.2 %gather_fusion = bf16[32,64,2,640]{3,1,2,0:T(8,128)(2,1)} fusion(bf16[36,64,2,640]{3,1,2,0:T(8,128)(2,1)} %bitcast.149, s32[1024]{0:T(1024)S(1)} %pad_clamp_fusion), kind=kCustom, calls=%fused_computation | custom fusion | bytes 10485888 | tf_op jit(solution)/shard_map/gather | solution.py:101
  103.8 7.9 %reshape_squeeze.9 = bf16[4,512,8,80]{3,2,1,0:T(8,128)(2,1)} reshape(bf16[4,8,64,1,640]{4,2,1,0,3:T(8,128)(2,1)} %get-tuple-element.57) | data formatting | bytes 5242880 | tf_op jit(solution)/shard_map/reshape;squeeze | solution.py:102
  111.6 7.2 %copy.40 = bf16[4,512,8,80]{1,3,2,0:T(8,128)(2,1)} copy(bf16[4,512,8,80]{3,2,1,0:T(8,128)(2,1)} %reshape_squeeze.9) | data formatting | bytes 5242880 | tf_op jit(solution)/shard_map/reshape;squeeze | solution.py:102
  118.8 7.9 %reshape_squeeze.11 = bf16[4,512,8,80]{3,2,1,0:T(8,128)(2,1)} reshape(bf16[4,8,64,1,640]{4,2,1,0,3:T(8,128)(2,1)} %get-tuple-element.58) | data formatting | bytes 5242880 | tf_op jit(solution)/shard_map/reshape;squeeze | solution.py:103
  126.6 7.2 %copy.36 = bf16[4,512,8,80]{1,3,2,0:T(8,128)(2,1)} copy(bf16[4,512,8,80]{3,2,1,0:T(8,128)(2,1)} %reshape_squeeze.11) | data formatting | bytes 5242880 | tf_op jit(solution)/shard_map/reshape;squeeze | solution.py:103
  146.4 39.1 %all-reduce.2.cloned.1.call-done = bf16[256,1280]{1,0:T(8,128)(2,1)} async-done(((bf16[256,1280]{1,0:T(8,128)(2,1)}), bf16[256,1280]{1,0:T(8,128)(2,1)}) %all-reduce.2.cloned.1.call-update) | async-done | bytes 655376 | tf_op jit(solution)/shard_map/psum | solution.py:114
  188.2 4.7 %fusion.59 = f32[4,8,64,512]{3,2,1,0:T(8,128)} fusion(bf16[4,512,8,80]{1,3,2,0:T(8,128)(2,1)} %copy.36, bf16[4,64,8,80]{3,2,1,0:T(8,128)(2,1)S(1)} %reshape.776), kind=kOutput, calls=%fused_computation.72 | convolution fusion | flops 167772160 | bytes 7143424 | tf_op jit(solution)/shard_map/nqhe,nkhe->nhqk/dot_general | solution.py:122
  196.2 18.7 %convolution_bitcast_fusion.1 = f32[4,512,8,80]{1,3,2,0:T(8,128)} fusion(f32[4,8,64,512]{3,2,1,0:T(8,128)} %fusion.59, bf16[4,64,8,80]{3,2,1,0:T(8,128)(2,1)S(1)} %reshape_squeeze.10, f32[4,8,64,512]{3,2,1,0:T(8,128)} %copy-done.11, f32[4,8,64]{2,1,0:T(8,128)S(1)} %get-tuple-element.61), kind=kOutput, calls=%fused_computation.24 | convolution fusion | flops 175114752 | bytes 13967360 | tf_op jit(solution)/shard_map/nhqk,nqhe->nkhe/dot_general | solution.py:128
  214.9 8.7 %copy.45 = f32[4,512,8,80]{3,2,1,0:T(8,128)} copy(f32[4,512,8,80]{1,3,2,0:T(8,128)} %convolution_bitcast_fusion) | data formatting | bytes 10485760 | tf_op jit(solution)/shard_map/nhqk,nqhe->nkhe/transpose | solution.py:129
  223.6 8.7 %stack.8 = f32[32,64,1,640]{3,1,0,2:T(8,128)} reshape(f32[4,512,8,80]{3,2,1,0:T(8,128)} %copy.45) | data formatting | bytes 10485760 | tf_op jit(solution)/shard_map/stack | solution.py:130
  232.3 8.7 %copy.43 = f32[4,512,8,80]{3,2,1,0:T(8,128)} copy(f32[4,512,8,80]{1,3,2,0:T(8,128)} %convolution_bitcast_fusion.1) | data formatting | bytes 10485760 | tf_op jit(solution)/shard_map/nhqk,nqhe->nkhe/transpose | solution.py:128
  241.0 8.7 %stack.7 = f32[32,64,1,640]{3,1,0,2:T(8,128)} reshape(f32[4,512,8,80]{3,2,1,0:T(8,128)} %copy.43) | data formatting | bytes 10485760 | tf_op jit(solution)/shard_map/stack | solution.py:130
  249.7 4.7 %pad_maximum_fusion = f32[32,64,2,640]{3,1,0,2:T(8,128)S(1)} fusion(f32[32,64,1,640]{3,1,0,2:T(8,128)} %stack.8, f32[32,64,1,640]{3,1,0,2:T(8,128)} %stack.7), kind=kLoop, calls=%fused_computation.5 | loop fusion | flops 2621440 | bytes 20971520 | tf_op jit(solution)/shard_map/stack | solution.py:130
  259.0 5.9 %broadcast_in_dim.44 = f32[36,64,2,640]{3,1,2,0:T(8,128)} broadcast(f32[]{:T(128)} %constant.155.clone.1), dimensions={} | broadcast | bytes 11796484 | tf_op jit(solution)/shard_map/broadcast_in_dim | solution.py:135
  264.9 21.7 %scatter_fusion = f32[36,64,2,640]{3,1,2,0:T(8,128)} fusion(f32[36,64,2,640]{3,1,2,0:T(8,128)} %broadcast_in_dim.44, s32[32]{0:T(128)S(1)} %fusion.82, f32[32,64,2,640]{3,1,2,0:T(8,128)} %copy.46), kind=kCustom, calls=%fused_computation.2 | custom fusion | flops 2621440 | bytes 31457408 | tf_op jit(solution)/shard_map/scatter-add | solution.py:137
  295.1 36.6 %collective-permute-done.8 = bf16[3,4,64,2,640]{4,2,3,1,0:T(8,128)(2,1)S(1)} collective-permute-done((bf16[3,4,64,2,640]{4,2,3,1,0:T(8,128)(2,1)S(1)}, bf16[3,4,64,2,640]{4,2,3,1,0:T(8,128)(2,1)S(1)}, u32[]{:S(2)}, u32[]{:S(2)}) %collective-permute-start.8) | collective-permute-done | bytes 1966112 | tf_op jit(solution)/shard_map/ppermute | solution.py:12
  331.6 7.3 %collective-permute-done.9 = bf16[3,4,64,2,640]{4,2,3,1,0:T(8,128)(2,1)S(1)} collective-permute-done((bf16[3,4,64,2,640]{4,2,3,1,0:T(8,128)(2,1)S(1)}, bf16[3,4,64,2,640]{4,2,3,1,0:T(8,128)(2,1)S(1)}, u32[]{:S(2)}, u32[]{:S(2)}) %collective-permute-start.9) | collective-permute-done | bytes 1966112 | tf_op jit(solution)/shard_map/ppermute | solution.py:12
  339.0 5.2 %fusion.90 = (bf16[3,1,4,64,2,640]{5,3,4,2,1,0:T(8,128)(2,1)S(1)}, f32[3,1,4,64,2,640]{5,3,4,2,1,0:T(8,128)}) fusion(bf16[3,4,64,2,640]{4,2,3,1,0:T(8,128)(2,1)S(1)} %collective-permute-done.9, bf16[3,4,64,2,640]{4,2,3,1,0:T(8,128)(2,1)S(1)} %collective-permute-done.8, f32[3,3,4,64,2,640]{5,3,4,2,1,0:T(8,128)} %bitcast.148), kind=kLoop, calls=%fused_computation.140 | loop fusion | flops 4915200 | bytes 13762560 | tf_op jit(solution)/shard_map/convert.6
  351.2 18.0 %fusion.44 = bf16[4,64,8,80]{3,1,2,0:T(8,128)(2,1)S(1)} fusion(bf16[4,512,8,80]{1,3,2,0:T(8,128)(2,1)} %copy.40, f32[4,8,64,512]{3,2,1,0:T(8,128)} %fusion.59, f32[4,8,64,512]{3,2,1,0:T(8,128)} %copy-done.11, f32[4,8,64]{2,1,0:T(8,128)S(1)} %get-tuple-element.61), kind=kOutput, calls=%fused_computation.54 | convolution fusion | flops 175278592 | bytes 11345920 | tf_op jit(solution)/shard_map/nhqk,nkhe->nqhe/dot_general | solution.py:125
  382.0 19.8 %reduce-scatter.4.cloned.1.call-done = bf16[640,256]{1,0:T(8,128)(2,1)} async-done(((bf16[1280,256]{1,0:T(8,128)(2,1)}), bf16[640,256]{1,0:T(8,128)(2,1)}) %reduce-scatter.4.cloned.1.call-update) | async-done | bytes 327696
  (100 shorter events, 98.6 us)
Async XLA Ops:
  6.5 136.7 %copy-start = (bf16[640,1280]{1,0:T(8,128)(2,1)S(1)}, bf16[640,1280]{1,0:T(8,128)(2,1)}, u32[]{:S(2)}) copy-start(bf16[640,1280]{1,0:T(8,128)(2,1)} %param.19) | copy-start | bytes 4915204
  6.5 178.9 %all-reduce.2.cloned.1.call-start = ((), (), s32[]{:S(2)}) async-start(), calls=%async_computation.1 | async-start | bytes 1310720 | tf_op jit(solution)/shard_map/psum | solution.py:114
  13.6 18.6 %copy-start.7 = (bf16[1,1,4,64,3,640]{5,3,4,2,1,0:T(8,128)(2,1)}, bf16[1,1,4,64,3,640]{5,3,4,2,1,0:T(8,128)(2,1)S(1)}, u32[]{:S(2)}) copy-start(bf16[1,1,4,64,3,640]{5,3,4,2,1,0:T(8,128)(2,1)S(1)} %fusion.31) | copy-start | bytes 2949124
  13.6 27.4 %copy-start.9 = (s32[1,1,4]{2,1,0:T(1,128)S(1)}, s32[1,1,4]{2,1,0:T(1,128)}, u32[]{:S(2)}) copy-start(s32[1,1,4]{2,1,0:T(1,128)} %param.21) | copy-start | bytes 52
  13.6 33.3 %copy-start.8 = (s32[1,1,4,8]{3,2,1,0:T(4,128)S(1)}, s32[1,1,4,8]{3,2,1,0:T(4,128)}, u32[]{:S(2)}) copy-start(s32[1,1,4,8]{3,2,1,0:T(4,128)} %param.20) | copy-start | bytes 388
  13.7 18.5 %collective-permute-start.1 = (bf16[1,1,4,64,2,640]{5,3,4,2,1,0:T(8,128)(2,1)S(1)}, bf16[1,1,4,64,2,640]{5,3,4,2,1,0:T(8,128)(2,1)S(1)}, u32[]{:S(2)}, u32[]{:S(2)}) collective-permute-start(bf16[1,1,4,64,2,640]{5,3,4,2,1,0:T(8,128)(2,1)S(1)} %slice.184), channel_id=1, source_target_pairs={{32,0},{64,32},{96,64},{33,1},{65,33},{97,65},{34,2},{66,34},{98,6... | collective-permute-start | bytes 1966088 | tf_op jit(solution)/shard_map/ppermute | solution.py:25
  16.2 18.1 %collective-permute-start = (bf16[1,1,4,64,2,640]{5,3,4,2,1,0:T(8,128)(2,1)S(1)}, bf16[1,1,4,64,2,640]{5,3,4,2,1,0:T(8,128)(2,1)S(1)}, u32[]{:S(2)}, u32[]{:S(2)}) collective-permute-start(bf16[1,1,4,64,2,640]{5,3,4,2,1,0:T(8,128)(2,1)S(1)} %slice.184), channel_id=1, source_target_pairs={{0,32},{32,64},{64,96},{1,33},{33,65},{65,97},{2,34},{34,66},{66,9... | collective-permute-start | bytes 1966088 | tf_op jit(solution)/shard_map/ppermute | solution.py:23
  36.7 48.1 %collective-permute-start.3 = (bf16[3,1,4,64,2,640]{5,3,4,2,1,0:T(8,128)(2,1)}, bf16[3,1,4,64,2,640]{5,3,4,2,1,0:T(8,128)(2,1)}, u32[]{:S(2)}, u32[]{:S(2)}) collective-permute-start(bf16[3,1,4,64,2,640]{5,3,4,2,1,0:T(8,128)(2,1)} %pad_maximum_fusion.2), channel_id=1, source_target_pairs={{2,0},{4,2},{6,4},{8,6},{10,8},{12,10},{14,12},{16,14},{18,16},{20... | collective-permute-start | bytes 5898248 | tf_op jit(solution)/shard_map/ppermute | solution.py:25
  38.6 46.1 %collective-permute-start.2 = (bf16[3,1,4,64,2,640]{5,3,4,2,1,0:T(8,128)(2,1)}, bf16[3,1,4,64,2,640]{5,3,4,2,1,0:T(8,128)(2,1)}, u32[]{:S(2)}, u32[]{:S(2)}) collective-permute-start(bf16[3,1,4,64,2,640]{5,3,4,2,1,0:T(8,128)(2,1)} %pad_maximum_fusion.2), channel_id=1, source_target_pairs={{0,2},{2,4},{4,6},{6,8},{8,10},{10,12},{12,14},{14,16},{16,18},{18... | collective-permute-start | bytes 5898248 | tf_op jit(solution)/shard_map/ppermute | solution.py:23
  41.1 6.0 %collective-permute-start.5 = (bf16[1,1,4,64]{3,2,1,0:T(4,128)(2,1)S(1)}, bf16[1,1,4,64]{3,2,1,0:T(4,128)(2,1)S(1)}, u32[]{:S(2)}, u32[]{:S(2)}) collective-permute-start(bf16[1,1,4,64]{3,2,1,0:T(4,128)(2,1)S(1)} %fusion.75), channel_id=1, source_target_pairs={{32,0},{64,32},{96,64},{33,1},{65,33},{97,65},{34,2},{66,34},{98,6... | collective-permute-start | bytes 1544 | tf_op jit(solution)/shard_map/ppermute | solution.py:25
  43.4 5.5 %collective-permute-start.4 = (bf16[1,1,4,64]{3,2,1,0:T(4,128)(2,1)S(1)}, bf16[1,1,4,64]{3,2,1,0:T(4,128)(2,1)S(1)}, u32[]{:S(2)}, u32[]{:S(2)}) collective-permute-start(bf16[1,1,4,64]{3,2,1,0:T(4,128)(2,1)S(1)} %fusion.75), channel_id=1, source_target_pairs={{0,32},{32,64},{64,96},{1,33},{33,65},{65,97},{2,34},{34,66},{66,9... | collective-permute-start | bytes 1544 | tf_op jit(solution)/shard_map/ppermute | solution.py:23
  48.9 29.0 %collective-permute-start.7 = (bf16[3,1,4,64]{3,2,1,0:T(4,128)(2,1)S(1)}, bf16[3,1,4,64]{3,2,1,0:T(4,128)(2,1)S(1)}, u32[]{:S(2)}, u32[]{:S(2)}) collective-permute-start(bf16[3,1,4,64]{3,2,1,0:T(4,128)(2,1)S(1)} %pad_maximum_fusion.4), channel_id=1, source_target_pairs={{2,0},{4,2},{6,4},{8,6},{10,8},{12,10},{14,12},{16,14},{18,16},{20... | collective-permute-start | bytes 4616 | tf_op jit(solution)/shard_map/ppermute | solution.py:25
  52.5 31.5 %collective-permute-start.6 = (bf16[3,1,4,64]{3,2,1,0:T(4,128)(2,1)S(1)}, bf16[3,1,4,64]{3,2,1,0:T(4,128)(2,1)S(1)}, u32[]{:S(2)}, u32[]{:S(2)}) collective-permute-start(bf16[3,1,4,64]{3,2,1,0:T(4,128)(2,1)S(1)} %pad_maximum_fusion.4), channel_id=1, source_target_pairs={{0,2},{2,4},{4,6},{6,8},{8,10},{10,12},{12,14},{14,16},{16,18},{18... | collective-permute-start | bytes 4616 | tf_op jit(solution)/shard_map/ppermute | solution.py:23
  137.9 2.0 copy-start.11
  139.9 45.5 %copy-start.2 = (bf16[1,1,4,64,1280]{4,3,2,1,0:T(8,128)(2,1)S(1)}, bf16[1,1,4,64,1280]{4,3,2,1,0:T(8,128)(2,1)}, u32[]{:S(2)}) copy-start(bf16[1,1,4,64,1280]{4,3,2,1,0:T(8,128)(2,1)} %param.15) | copy-start | bytes 1966084
  139.9 45.5 %copy-start.6 = (bf16[1,1,4,64,1280]{4,3,2,1,0:T(8,128)(2,1)S(1)}, bf16[1,1,4,64,1280]{4,3,2,1,0:T(8,128)(2,1)}, u32[]{:S(2)}) copy-start(bf16[1,1,4,64,1280]{4,3,2,1,0:T(8,128)(2,1)} %param.16) | copy-start | bytes 1966084
  145.8 256.0 %reduce-scatter.4.cloned.1.call-start = ((), (), s32[]{:S(2)}) async-start(), calls=%async_computation.2 | async-start | bytes 983040
  188.2 4.7 %copy-start.12 = (f32[4,8,64,512]{3,2,1,0:T(8,128)S(1)}, f32[4,8,64,512]{3,2,1,0:T(8,128)}, u32[]{:S(2)}) copy-start(f32[4,8,64,512]{3,2,1,0:T(8,128)} %copy-done.11) | copy-start | bytes 12582916
  290.5 41.1 %collective-permute-start.8 = (bf16[3,4,64,2,640]{4,2,3,1,0:T(8,128)(2,1)S(1)}, bf16[3,4,64,2,640]{4,2,3,1,0:T(8,128)(2,1)S(1)}, u32[]{:S(2)}, u32[]{:S(2)}) collective-permute-start(bf16[3,4,64,2,640]{4,2,3,1,0:T(8,128)(2,1)S(1)} %get-tuple-element.55), channel_id=1, source_target_pairs={{2,0},{4,2},{6,4},{8,6},{10,8},{12,10},{14,12},{16,14},{18,16},{20... | collective-permute-start | bytes 5898248 | tf_op jit(solution)/shard_map/ppermute | solution.py:12
  293.1 45.8 %collective-permute-start.9 = (bf16[3,4,64,2,640]{4,2,3,1,0:T(8,128)(2,1)S(1)}, bf16[3,4,64,2,640]{4,2,3,1,0:T(8,128)(2,1)S(1)}, u32[]{:S(2)}, u32[]{:S(2)}) collective-permute-start(bf16[3,4,64,2,640]{4,2,3,1,0:T(8,128)(2,1)S(1)} %get-tuple-element.56), channel_id=1, source_target_pairs={{0,2},{2,4},{4,6},{6,8},{8,10},{10,12},{12,14},{14,16},{16,18},{18... | collective-permute-start | bytes 5898248 | tf_op jit(solution)/shard_map/ppermute | solution.py:12
  344.3 25.7 %collective-permute-start.10 = (bf16[1,4,64,2,640]{4,2,3,1,0:T(8,128)(2,1)S(1)}, bf16[1,4,64,2,640]{4,2,3,1,0:T(8,128)(2,1)}, u32[]{:S(2)}, u32[]{:S(2)}) collective-permute-start(bf16[1,4,64,2,640]{4,2,3,1,0:T(8,128)(2,1)S(1)} %get-tuple-element.59), channel_id=1, source_target_pairs={{32,0},{64,32},{96,64},{33,1},{65,33},{97,65},{34,2},{66,34},{98,6... | collective-permute-start | bytes 1966088 | tf_op jit(solution)/shard_map/ppermute | solution.py:12
  347.0 23.1 %collective-permute-start.11 = (bf16[1,4,64,2,640]{4,2,3,1,0:T(8,128)(2,1)S(1)}, bf16[1,4,64,2,640]{4,2,3,1,0:T(8,128)(2,1)}, u32[]{:S(2)}, u32[]{:S(2)}) collective-permute-start(bf16[1,4,64,2,640]{4,2,3,1,0:T(8,128)(2,1)S(1)} %get-tuple-element.60), channel_id=1, source_target_pairs={{0,32},{32,64},{64,96},{1,33},{33,65},{65,97},{2,34},{34,66},{66,9... | collective-permute-start | bytes 1966088 | tf_op jit(solution)/shard_map/ppermute | solution.py:12
  369.3 2.7 copy-start.10
  377.3 26.4 %copy-start.1 = (bf16[640,1280]{1,0:T(8,128)(2,1)S(1)}, bf16[640,1280]{1,0:T(8,128)(2,1)}, u32[]{:S(2)}) copy-start(bf16[640,1280]{1,0:T(8,128)(2,1)} %param.19) | copy-start | bytes 4915204
  (3 other events, 3.6 us)
Sparse Core Ops, SparseCore 0:
  145.9 39.5 all-reduce.1
  382.1 19.6 reduce-scatter.3
where the time goes:
time: 415 us; the launch traced here: 411 us
  waiting for transfers between devices  145 us (35%)
  local copies, waits for them, and re-layouts  107 us (26%)
  matrix products  59.6 us (14%)
  other arithmetic  51.6 us (12%)
  starting transfers between devices  33.4 us (8%)
  between operations  13.8 us (3%)
    ppermute x4, waiting for transfers between devices, passed_along(): return lax.ppermute(x, axis, pairs)  43.9 us
    psum x1, waiting for transfers between devices, per_device(): lax.psum(partial_out.astype(jnp.bfloat16), 'section').astype(jnp.float32)  39.1 us
    ppermute x4, waiting for transfers between devices, with_halo(): lax.ppermute(head, axis, [((i + 1) % count, i) for i in range(ends)])  32.6 us
    another operation x3, local copies, waits for them, and re-layouts, per_device(): jnp.stack([d_keys.reshape(tubes, nblist, tube, feats), d_values.reshape(t...  21.9 us
    scatter-add x1, other arithmetic, per_device(): ext_grad = jnp.zeros((ext_tubes, tube, 2, feats), jnp.float32).at[local.r...  21.7 us
    unnamed x3, waiting for transfers between devices  19.8 us
    dot_general x1, matrix products, per_device(): jnp.einsum('nhqk,nqhe->nkhe', d_score, query, preferred_element_type=jnp....  18.7 us
    dot_general x1, matrix products, per_device(): jnp.einsum('nhqk,nkhe->nqhe', d_score, keys, preferred_element_type=jnp.f...  18 us
  transfers between devices with their start and end apart: 14, of which 9 were waited for; matrix products, arithmetic and copies ran while one was open for 6% of the time, Pallas kernels for 0%

commit v1 on v0

v1 whole, which is shorter than its diff:
```python
import functools
import math

import jax
import jax.numpy as jnp
from jax import lax
from jax.experimental import pallas as pl
from jax.experimental.pallas import tpu as pltpu
from jax.sharding import PartitionSpec as P

HEAD_DIM = 80
SCALE = HEAD_DIM ** (-0.5)
LOG2_SCALE = SCALE * math.log2(math.e)
BF16 = jnp.bfloat16
F32 = jnp.float32
MIB = 1 << 20
GROUPS = ((0, 3, 0, 256), (3, 2, 128, 384), (5, 3, 384, 256))
CHUNK = 4
STAT_ROWS = 32

NT_DIMS = (((1,), (1,)), ((), ()))


def dot(a, b):
    return jnp.dot(a, b, preferred_element_type=F32)


def dot_nt(a, b):
    return lax.dot_general(a, b, NT_DIMS, preferred_element_type=F32)


def head_mask(head, first_lane, rows, lanes):
    lane = lax.broadcasted_iota(jnp.int32, (rows, lanes), 1) + first_lane
    return (lane >= head * HEAD_DIM) & (lane < (head + 1) * HEAD_DIM)


def spread(x, group):
    h0, nh, l0, wd = group
    zero = jnp.zeros_like(x)
    return jnp.concatenate(
        [jnp.where(head_mask(h, l0, x.shape[0], wd), x, zero) for h in range(h0, h0 + nh)], axis=0
    )


def gather_heads(y, group, rows):
    h0, nh, l0, wd = group
    total = jnp.zeros((rows, wd), y.dtype)
    for k in range(nh):
        total = jnp.where(head_mask(h0 + k, l0, rows, wd), y[k * rows : (k + 1) * rows], total)
    return total


def add_group(ref, rows, value, group):
    h0, nh, l0, wd = group
    ref[rows, l0 : l0 + wd] = ref[rows, l0 : l0 + wd] + value


def project_body(n, aliased, *refs):
    xs = refs[:n]
    gain_ref, w_ref = refs[n : n + 2]
    out_ref, x_scr = refs[n + 2 + aliased :]
    step = pl.program_id(0)
    for k in range(n):

        @pl.when(step == k)
        def _():
            x_scr[...] = xs[k][...]

    x = x_scr[...].astype(F32)
    centred = x - jnp.mean(x, axis=-1, keepdims=True)
    inverse = lax.rsqrt(jnp.mean(centred * centred, axis=-1, keepdims=True) + 1e-06)
    normed = (centred * inverse * gain_ref[...]).astype(BF16)
    feats = w_ref.shape[1] // 3
    for c in range(3):
        cols = slice(c * feats, (c + 1) * feats)
        out_ref[0, :, cols] = dot(normed, w_ref[:, cols]).astype(BF16)


def project(blocks, first, gain, w, buf=None):
    n = len(blocks)
    rows, width = blocks[0].shape
    cols = w.shape[1]
    aliased = int(buf is not None)
    whole = lambda a: pl.BlockSpec(a.shape, lambda i: (0,) * a.ndim)
    return pl.pallas_call(
        functools.partial(project_body, n, aliased),
        grid=(n,),
        in_specs=[whole(b) for b in blocks]
        + [whole(gain), whole(w)]
        + [pl.BlockSpec(memory_space=pl.ANY)] * aliased,
        out_specs=pl.BlockSpec((1, rows, cols), lambda i: (i + first, 0, 0)),
        out_shape=jax.ShapeDtypeStruct((9, rows, cols), BF16),
        scratch_shapes=[pltpu.VMEM((rows, width), BF16)],
        input_output_aliases={n + 2: 0} if aliased else {},
        compiler_params=pltpu.CompilerParams(vmem_limit_bytes=32 * MIB),
        cost_estimate=pl.CostEstimate(
            flops=2 * n * rows * width * cols, bytes_accessed=2 * width * cols + 4 * n * rows * width, transcendentals=0
        ),
        name=f"project{first}",
    )(*blocks, gain, w, *([buf] if aliased else []))


def start_kv(local_ref, qkv_ref, kv_scr, sem, tubes, nb):
    feats = kv_scr.shape[2] // 2

    @pl.when(pl.program_id(0) == 0)
    def _():
        for i in range(tubes):
            for n in range(nb):
                pltpu.make_async_copy(
                    qkv_ref.at[local_ref[i * nb + n], :, feats:],
                    kv_scr.at[i, n * 64 : (n + 1) * 64, :],
                    sem.at[i],
                ).start()


def wait_kv(kv_scr, sem, i):
    pltpu.make_async_copy(kv_scr.at[i], kv_scr.at[i], sem.at[i]).wait()


def forward_body(local_ref, count_ref, qkv_ref, q_ref, w_out_ref, part_ref, o_ref, p_ref, lse_ref, kv_scr, att_scr, sem):
    tubes, keys, feats2 = kv_scr.shape
    feats = feats2 // 2
    nb = keys // 64
    i = pl.program_id(0)
    start_kv(local_ref, qkv_ref, kv_scr, sem, tubes, nb)
    lane = lax.broadcasted_iota(jnp.int32, (1, keys), 1)
    slot, place = lane // 64, lane % 64
    limit = jnp.zeros((1, keys), jnp.int32)
    for n in range(nb):
        limit = jnp.where(slot == n, count_ref[local_ref[i * nb + n]], limit)
    live = place < limit
    wait_kv(kv_scr, sem, i)
    o_ref[...] = jnp.zeros_like(o_ref)
    pick = lax.broadcasted_iota(jnp.int32, (64, 128), 0) == lax.broadcasted_iota(jnp.int32, (64, 128), 1) % 64
    for group in GROUPS:
        h0, nh, l0, wd = group
        window = slice(l0, l0 + wd)
        q = spread(q_ref[:, window], group)
        s = dot_nt(q, kv_scr[i, :, window]) * LOG2_SCALE
        s = jnp.where(live, s, -1e30)
        top = jnp.max(s, axis=-1, keepdims=True)
        e = jnp.exp2(s - top)
        total = jnp.sum(e, axis=-1, keepdims=True)
        p = (e * (1.0 / total)).astype(BF16)
        p_ref[0, h0 * 64 : (h0 + nh) * 64, :] = p
        o = dot(p, kv_scr[i, :, feats + l0 : feats + l0 + wd])
        add_group(o_ref, slice(None), gather_heads(o, group, 64), group)
        lse = top + jnp.log2(total)
        for k in range(nh):
            column = jnp.broadcast_to(lse[k * 64 : (k + 1) * 64], (64, 128))
            lse_ref[0, h0 + k : h0 + k + 1, :] = jnp.sum(jnp.where(pick, column, 0.0), axis=0, keepdims=True)
    att_scr[pl.ds(i * 64, 64), :] = o_ref[...].astype(BF16)

    @pl.when(i == tubes - 1)
    def _():
        part_ref[...] = dot(att_scr[...], w_out_ref[...]).astype(BF16)


def attend_forward(local, counts, qkv, w_out):
    slots, _, cols = qkv.shape
    feats = cols // 3
    tubes, nb = 4, local.shape[0] // 4
    keys = nb * 64
    rows = tubes * 64
    heads = feats // HEAD_DIM
    width = w_out.shape[1]
    return pl.pallas_call(
        forward_body,
        grid_spec=pltpu.PrefetchScalarGridSpec(
            num_scalar_prefetch=2,
            grid=(tubes,),
            in_specs=[
                pl.BlockSpec(memory_space=pl.ANY),
                pl.BlockSpec((pl.squeezed, 64, feats), lambda i, *_: (i, 0, 0)),
                pl.BlockSpec((feats, width), lambda i, *_: (0, 0)),
            ],
            out_specs=[
                pl.BlockSpec((rows, width), lambda i, *_: (0, 0)),
                pl.BlockSpec((64, feats), lambda i, *_: (i, 0)),
                pl.BlockSpec((1, heads * 64, keys), lambda i, *_: (i, 0, 0)),
                pl.BlockSpec((1, heads, 128), lambda i, *_: (i, 0, 0)),
            ],
            scratch_shapes=[
                pltpu.VMEM((tubes, keys, 2 * feats), BF16),
                pltpu.VMEM((rows, feats), BF16),
                pltpu.SemaphoreType.DMA((tubes,)),
            ],
        ),
        out_shape=[
            jax.ShapeDtypeStruct((rows, width), BF16),
            jax.ShapeDtypeStruct((rows, feats), F32),
            jax.ShapeDtypeStruct((tubes, heads * 64, keys), BF16),
            jax.ShapeDtypeStruct((tubes, heads, 128), F32),
        ],
        compiler_params=pltpu.CompilerParams(vmem_limit_bytes=32 * MIB),
        cost_estimate=pl.CostEstimate(
            flops=4 * rows * heads * keys * 256, bytes_accessed=10 * MIB, transcendentals=rows * heads * keys
        ),
        name="attend_forward",
    )(local, counts, qkv, qkv, w_out)


def parts_of(x, n):
    out = []
    for _ in range(n):
        piece = x.astype(BF16)
        out.append(piece)
        x = x - piece.astype(F32)
    return out


def middle_body(count_ref, sec_ref, mine_ref, other_ref, video_ref, target_ref, w_out_ref, o_ref, lse_ref, pay_ref, g_ref):
    rows, width = video_ref.shape
    feats = w_out_ref.shape[0]
    heads = feats // HEAD_DIM
    tubes = rows // 64
    row = lax.broadcasted_iota(jnp.int32, (rows, 1), 0)
    limit = jnp.zeros((rows, 1), jnp.int32)
    for i in range(tubes):
        limit = jnp.where(row // 64 == i, count_ref[i], limit)
    valid = row % 64 < limit
    mixed = mine_ref[...].astype(F32) + other_ref[...].astype(F32)
    g = jnp.where(valid, 2.0 * (video_ref[...].astype(F32) + mixed - target_ref[...].astype(F32)), 0.0)
    half = width // 2
    g_ref[...] = jnp.where(sec_ref[0] == 0, g[:, :half], g[:, half:])
    d_att = dot_nt(g.astype(BF16), w_out_ref[...]).astype(BF16)
    pay_ref[:rows] = d_att
    prod = d_att.astype(F32) * o_ref[...]
    head = lax.broadcasted_iota(jnp.int32, (heads, feats), 0)
    lane = lax.broadcasted_iota(jnp.int32, (heads, feats), 1)
    ones = ((lane >= head * HEAD_DIM) & (lane < (head + 1) * HEAD_DIM)).astype(F32)
    inner = []
    for i in range(tubes):
        one = prod[i * 64 : (i + 1) * 64]
        inner.append(
            lax.dot_general(
                ones,
                jnp.concatenate([one, one], axis=0),
                NT_DIMS,
                precision=lax.Precision.HIGHEST,
                preferred_element_type=F32,
            )
        )
    inner = jnp.concatenate(inner, axis=0)
    lse = lse_ref[...].reshape(tubes * heads, 128)
    for k, piece in enumerate(parts_of(lse, 3) + parts_of(inner, 2)):
        pay_ref[rows:, k * 128 : (k + 1) * 128] = piece


def middle(counts, sec, mine, other, video, target, w_out, o, lse):
    rows, width = video.shape
    feats = w_out.shape[0]
    vmem = pl.BlockSpec(memory_space=pltpu.VMEM)
    smem = pl.BlockSpec(memory_space=pltpu.SMEM)
    return pl.pallas_call(
        middle_body,
        in_specs=[smem, smem] + [vmem] * 7,
        out_specs=[vmem, vmem],
        out_shape=[
            jax.ShapeDtypeStruct((rows + STAT_ROWS, feats), BF16),
            jax.ShapeDtypeStruct((rows, width // 2), F32),
        ],
        compiler_params=pltpu.CompilerParams(vmem_limit_bytes=32 * MIB),
        cost_estimate=pl.CostEstimate(flops=2 * rows * width * feats, bytes_accessed=6 * MIB, transcendentals=0),
        name="middle",
    )(counts, sec, mine, other, video, target, w_out, o, lse)


def query_body(local_ref, qkv_ref, p_ref, pay_ref, dq_ref, kv_scr, dq_scr, sem):
    tubes, keys, feats2 = kv_scr.shape
    feats = feats2 // 2
    i = pl.program_id(0)
    start_kv(local_ref, qkv_ref, kv_scr, sem, tubes, keys // 64)
    wait_kv(kv_scr, sem, i)
    dq_scr[...] = jnp.zeros_like(dq_scr)
    for group in GROUPS:
        h0, nh, l0, wd = group
        window = slice(l0, l0 + wd)
        d_att = spread(pay_ref[pl.ds(i * 64, 64), window], group)
        d_prob = dot_nt(d_att, kv_scr[i, :, feats + l0 : feats + l0 + wd])
        p = p_ref[0, h0 * 64 : (h0 + nh) * 64, :].astype(F32)
        inner = jnp.sum(d_prob * p, axis=-1, keepdims=True)
        d_score = (p * (d_prob - inner) * SCALE).astype(BF16)
        add_group(dq_scr, slice(None), gather_heads(dot(d_score, kv_scr[i, :, window]), group, 64), group)
    dq_ref[...] = dq_scr[...].astype(BF16)


def query_grad(local, qkv, p, pay):
    cols = qkv.shape[2]
    feats = cols // 3
    tubes, rows_h, keys = p.shape
    return pl.pallas_call(
        query_body,
        grid_spec=pltpu.PrefetchScalarGridSpec(
            num_scalar_prefetch=1,
            grid=(tubes,),
            in_specs=[
                pl.BlockSpec(memory_space=pl.ANY),
                pl.BlockSpec((1, rows_h, keys), lambda i, *_: (i, 0, 0)),
                pl.BlockSpec(pay.shape, lambda i, *_: (0, 0)),
            ],
            out_specs=pl.BlockSpec((64, feats), lambda i, *_: (i, 0)),
            scratch_shapes=[
                pltpu.VMEM((tubes, keys, 2 * feats), BF16),
                pltpu.VMEM((64, feats), F32),
                pltpu.SemaphoreType.DMA((tubes,)),
            ],
        ),
        out_shape=jax.ShapeDtypeStruct((tubes * 64, feats), BF16),
        compiler_params=pltpu.CompilerParams(vmem_limit_bytes=32 * MIB),
        cost_estimate=pl.CostEstimate(flops=4 * tubes * rows_h * keys * 256, bytes_accessed=10 * MIB, transcendentals=0),
        name="query_grad",
    )(local, qkv, p, pay)


def key_body(
    list_ref, n_ref, count_ref, sec_ref, qkv_ref, w_ref, *rest
):
    pays = rest[:9]
    video_ref, gain_ref, dq_ref, g_ref, send_ref, keep_ref = rest[9:15]
    q_scr, kv_scr, pay_scr, w_scr, lse_scr, inner_scr, qc_scr, dc_scr, grad_scr, dproj_scr, sem = rest[15:]
    tubes = kv_scr.shape[0]
    feats = q_scr.shape[2]
    rows = tubes * 64
    most = list_ref.shape[0] // tubes
    w_copy = pltpu.make_async_copy(w_ref, w_scr, sem.at[0])
    q_copy = pltpu.make_async_copy(qkv_ref.at[:, :, :feats], q_scr, sem.at[1])
    kv_copy = pltpu.make_async_copy(qkv_ref.at[:tubes, :, feats:], kv_scr, sem.at[2])
    pay_copies = [pltpu.make_async_copy(pays[k], pay_scr.at[k], sem.at[3 + k]) for k in range(9)]
    for c in pay_copies + [q_copy, kv_copy, w_copy]:
        c.start()
    for k, c in enumerate(pay_copies):
        c.wait()
        parts = [pay_scr[k, rows:, j * 128 : (j + 1) * 128].astype(F32) for j in range(5)]
        lse_scr[k * tubes : (k + 1) * tubes] = (parts[0] + parts[1] + parts[2]).reshape(tubes, -1, 128)
        inner_scr[k * tubes : (k + 1) * tubes] = (parts[3] + parts[4]).reshape(tubes, -1, 128)
    q_copy.wait()
    kv_copy.wait()
    low = lax.broadcasted_iota(jnp.int32, (8, 128), 1) < 64
    key_row = lax.broadcasted_iota(jnp.int32, (64, 1), 0)
    grad_scr[...] = jnp.zeros_like(grad_scr)

    def tube(j, carry):
        alive = key_row < count_ref[j]

        def chunk(c, carry):
            lses, inners = [], []
            for t in range(CHUNK):
                place = c * CHUNK + t
                i = list_ref[j * most + jnp.minimum(place, most - 1)]
                slot, w = i // tubes, i % tubes
                qc_scr[t * 64 : (t + 1) * 64, :] = q_scr[i]
                dc_scr[t * 64 : (t + 1) * 64, :] = pay_scr[slot, pl.ds(pl.multiple_of(w * 64, 64), 64), :]
                lses.append(jnp.where(place < n_ref[j], lse_scr[i], 1e30))
                inners.append(inner_scr[i])
            lse = jnp.concatenate([jnp.where(low, lses[t], lses[t + 1]) for t in range(0, CHUNK, 2)], axis=1)
            inner = jnp.concatenate([jnp.where(low, inners[t], inners[t + 1]) for t in range(0, CHUNK, 2)], axis=1)
            for group in GROUPS:
                h0, nh, l0, wd = group
                window = slice(l0, l0 + wd)
                k = spread(kv_scr[j, :, window], group)
                v = spread(kv_scr[j, :, feats + l0 : feats + l0 + wd], group)
                qc, dc = qc_scr[:, window], dc_scr[:, window]
                s = dot_nt(k, qc) * LOG2_SCALE
                d_prob = dot_nt(v, dc)
                p, d_score = [], []
                for m in range(nh):
                    part = slice(m * 64, (m + 1) * 64)
                    head = slice(h0 + m, h0 + m + 1)
                    one = jnp.where(alive, jnp.exp2(s[part] - lse[head]), 0.0)
                    p.append(one.astype(BF16))
                    d_score.append((one * (d_prob[part] - inner[head]) * SCALE).astype(BF16))
                d_key = dot(jnp.concatenate(d_score, axis=0), qc)
                d_value = dot(jnp.concatenate(p, axis=0), dc)
                block = pl.ds(pl.multiple_of(j * 64, 64), 64)
                grad_scr[block, window] += gather_heads(d_key, group, 64)
                there = slice(feats + l0, feats + l0 + wd)
                grad_scr[block, there] += gather_heads(d_value, group, 64)
            return carry

        return lax.fori_loop(0, (n_ref[j] + CHUNK - 1) // CHUNK, chunk, carry)

    lax.fori_loop(0, tubes, tube, 0)
    dproj_scr[:, :feats] = dq_ref[...]
    dproj_scr[:, feats:] = grad_scr[...].astype(BF16)
    w_copy.wait()
    x = video_ref[...].astype(F32)
    centred = x - jnp.mean(x, axis=-1, keepdims=True)
    inverse = lax.rsqrt(jnp.mean(centred * centred, axis=-1, keepdims=True) + 1e-06)
    xhat = centred * inverse
    scaled = dot_nt(dproj_scr[...], w_scr[...]) * gain_ref[...]
    out = (
        scaled
        - jnp.mean(scaled, axis=-1, keepdims=True)
        - xhat * jnp.mean(scaled * xhat, axis=-1, keepdims=True)
    ) * inverse
    half = out.shape[1] // 2
    first = sec_ref[0] == 0
    send_ref[...] = jnp.where(first, out[:, half:], out[:, :half]).astype(BF16)
    keep_ref[...] = jnp.where(first, out[:, :half], out[:, half:]) + g_ref[...]


def key_grad(lists, lengths, counts, sec, qkv, w, pays, video, gain, dq, g):
    cols = qkv.shape[2]
    feats = cols // 3
    rows, width = video.shape
    tubes = rows // 64
    heads = feats // HEAD_DIM
    vmem = pl.BlockSpec(memory_space=pltpu.VMEM)
    smem = pl.BlockSpec(memory_space=pltpu.SMEM)
    hbm = pl.BlockSpec(memory_space=pl.ANY)
    return pl.pallas_call(
        key_body,
        in_specs=[smem] * 4 + [hbm] * 11 + [vmem] * 4,
        out_specs=[vmem, vmem],
        out_shape=[
            jax.ShapeDtypeStruct((rows, width // 2), BF16),
            jax.ShapeDtypeStruct((rows, width // 2), F32),
        ],
        scratch_shapes=[
            pltpu.VMEM((9 * tubes, 64, feats), BF16),
            pltpu.VMEM((tubes, 64, 2 * feats), BF16),
            pltpu.VMEM((9, rows + STAT_ROWS, feats), BF16),
            pltpu.VMEM(w.shape, BF16),
            pltpu.VMEM((9 * tubes, heads, 128), F32),
            pltpu.VMEM((9 * tubes, heads, 128), F32),
            pltpu.VMEM((CHUNK * 64, feats), BF16),
            pltpu.VMEM((CHUNK * 64, feats), BF16),
            pltpu.VMEM((rows, 2 * feats), F32),
            pltpu.VMEM((rows, 3 * feats), BF16),
            pltpu.SemaphoreType.DMA((12,)),
        ],
        compiler_params=pltpu.CompilerParams(vmem_limit_bytes=40 * MIB),
        cost_estimate=pl.CostEstimate(flops=12 * 10**9, bytes_accessed=16 * MIB, transcendentals=10**6),
        name="key_grad",
    )(lists, lengths, counts, sec, qkv, w, *pays, video, gain, dq, g)


def per_device(video, target, gain, w_qkv, w_out, neighbours, counts):
    tt, th, tw, tube, width = video.shape
    feats = w_qkv.shape[2]
    nb = neighbours.shape[3]
    rows = tt * th * tw * tube
    n_t, n_h = lax.axis_size("tm"), lax.axis_size("height")
    t_here, h_here, sec = lax.axis_index("tm"), lax.axis_index("height"), lax.axis_index("section")
    later = [(i, i + 1) for i in range(n_t - 1)]
    earlier = [(i + 1, i) for i in range(n_t - 1)]
    off_chip = [p for h in range(1, n_h - 1, 2) for p in ((h, h + 1), (h + 1, h))]
    on_chip = [(h, h ^ 1) for h in range(n_h)]
    swap = [(0, 1), (1, 0)]

    def from_before(x):
        return lax.ppermute(x, "tm", later)

    def from_after(x):
        return lax.ppermute(x, "tm", earlier)

    def from_off(x):
        return lax.ppermute(x, "height", off_chip)

    def from_mate(x):
        return lax.ppermute(x, "height", on_chip)

    def halo(x):
        off = from_off(x)
        before, after = from_before(x), from_after(x)
        return (x, before, after, off), (from_mate(x), from_mate(before), from_mate(after)), (from_before(off), from_after(off))

    video = video.reshape(rows, width)
    target = target.reshape(rows, width)
    gain = gain.reshape(1, width)
    w = w_qkv.reshape(width, 3 * feats)

    near, mates, corners = halo(video)
    qkv = project([near[0]], 0, gain, w)
    qkv = project([*near[1:], mates[0]], 1, gain, w, qkv)
    qkv = project([*mates[1:], *corners], 5, gain, w, qkv)
    qkv = qkv.reshape(9 * tw, tube, 3 * feats)

    meta = jnp.concatenate(
        [neighbours.reshape(tw, nb) + 1, counts.reshape(tw, 1), jnp.zeros((tw, 16 - nb - 1), jnp.int32)], axis=1
    )
    three = jnp.stack([meta, from_before(meta), from_after(meta)])
    off_meta, mate_meta = from_off(three), from_mate(three)
    meta = jnp.concatenate([three, off_meta[:1], mate_meta, off_meta[1:]]).reshape(9 * tw, 16)
    listed = meta[:, :nb] - 1
    count_all = meta[:, nb]

    ids = listed[:tw]
    t_of, h_of, w_of = ids // (n_h * tw), ids // tw % n_h, ids % tw
    step = jnp.where(t_of == t_here, 0, jnp.where(t_of < t_here, 1, 2))
    slot = jnp.where(
        h_of == h_here, step, jnp.where(h_of == h_here + 1 - 2 * (h_here % 2), 4 + step, jnp.where(step == 0, 3, 6 + step))
    )
    local = (slot * tw + w_of).reshape(tw * nb)
    own_ids = (t_here * n_h + h_here) * tw + jnp.arange(tw, dtype=jnp.int32)
    names = jnp.any(listed[None] == own_ids[:, None, None], axis=2)
    where = jnp.arange(9 * tw, dtype=jnp.int32)
    rank = jnp.sum(names[:, None, :] & (where[None, :] < where[:, None])[None], axis=2)
    lengths = jnp.sum(names, axis=1).astype(jnp.int32)
    most = 28
    hit = names[:, None, :] & (rank[:, None, :] == jnp.arange(most)[None, :, None])
    lists = jnp.sum(jnp.where(hit, where, 0), axis=2).astype(jnp.int32).reshape(tw * most)
    sec = sec.reshape(1).astype(jnp.int32)
    own_counts = count_all[:tw]

    part, o, p, lse = attend_forward(local, count_all, qkv, w_out)
    other = lax.ppermute(part, "section", swap)
    pay, g = middle(own_counts, sec, part, other, video, target, w_out, o, lse)
    near, mates, corners = halo(pay)
    dq = query_grad(local, qkv, p, pay)
    send, keep = key_grad(lists, lengths, own_counts, sec, qkv, w, [*near, *mates, *corners], video, gain, dq, g)
    got = lax.ppermute(send, "section", swap)
    return (keep + got.astype(F32)).astype(BF16).reshape(tt, th, tw, tube, width // 2)


def solution(mesh):
    in_specs = (
        P("tm", "height", None, None, None),
        P("tm", "height", None, None, None),
        P(),
        P(None, None, "section"),
        P("section", None),
        P("tm", "height", None, None),
        P("tm", "height", None),
    )
    out_specs = P("tm", "height", None, None, "section")
    return jax.shard_map(
        per_device, mesh=mesh, in_specs=in_specs, out_specs=out_specs, check_vma=False
    )
```

time: 415 us -> 188 us (0.45)
  the two profiles are of different devices: /device:TPU:54 before, /device:TPU:105 now
where the time goes in v1:
time: 188 us; the launch traced here: 186 us
  Pallas kernels  57.3 us (30%)
  local copies, waits for them, and re-layouts  48.8 us (26%)
  starting transfers between devices  48.7 us (26%)
  waiting for transfers between devices  27.4 us (15%)
  other arithmetic  3.04 us (2%)
    unnamed x47, local copies, waits for them, and re-layouts  39.1 us
    pallas_call x3, Pallas kernels, project(): pl.pallas_call(functools.partial(project_body, n, aliased), grid=(n,), in...  22 us
    pallas_call x1, Pallas kernels, key_grad(): pl.pallas_call(key_body, in_specs=[smem] * 4 + [hbm] * 11 + [vmem] * 4, o...  17.3 us
    ppermute x5, starting transfers between devices, from_before(): return lax.ppermute(x, 'tm', later)  16.2 us
    ppermute x1, waiting for transfers between devices, per_device(): other = lax.ppermute(part, 'section', swap)  14.7 us
    ppermute x5, starting transfers between devices, from_after(): return lax.ppermute(x, 'tm', earlier)  11.8 us
    ppermute x3, starting transfers between devices, from_off(): return lax.ppermute(x, 'height', off_chip)  10.6 us
    ppermute x7, starting transfers between devices, from_mate(): return lax.ppermute(x, 'height', on_chip)  9.5 us
  transfers between devices with their start and end apart: 22, of which 5 were waited for; matrix products, arithmetic and copies ran while one was open for 10% of the time, Pallas kernels for 10%

profile of v1, /device:TPU:105, one launch (start us, length us, event | category | flops | bytes accessed | tf_op | source)
XLA Modules:
  0.0 185.7 jit_solution(13883036260286332815)
XLA Ops:
  1.6 3.2 %collective-permute-start = (s32[4,16]{1,0:T(4,128)S(1)}, s32[4,16]{1,0:T(4,128)S(1)}, u32[]{:S(2)}, u32[]{:S(2)}) collective-permute-start(s32[4,16]{1,0:T(4,128)S(1)} %get-tuple-element.22), channel_id=1, source_target_pairs={{0,32},{32,64},{64,96},{1,33},{33,65},{65,97},{2,34},{34,66},{66,9... | collective-permute-start | bytes 776 | tf_op jit(solution)/shard_map/ppermute | solution.py:454
  6.9 5.8 %collective-permute-start.8 = (bf16[256,1280]{1,0:T(8,128)(2,1)}, bf16[256,1280]{1,0:T(8,128)(2,1)S(1)}, u32[]{:S(2)}, u32[]{:S(2)}) collective-permute-start(bf16[256,1280]{1,0:T(8,128)(2,1)} %bitcast.21), channel_id=1, source_target_pairs={{2,4},{4,2},{6,8},{8,6},{10,12},{12,10},{14,16},{16,14},{18,20},{2... | collective-permute-start | bytes 1966088 | tf_op jit(solution)/shard_map/ppermute | solution.py:460
  12.6 3.2 %collective-permute-start.4 = (bf16[256,1280]{1,0:T(8,128)(2,1)}, bf16[256,1280]{1,0:T(8,128)(2,1)}, u32[]{:S(2)}, u32[]{:S(2)}) collective-permute-start(bf16[256,1280]{1,0:T(8,128)(2,1)} %bitcast.22), channel_id=1, source_target_pairs={{0,32},{32,64},{64,96},{1,33},{33,65},{65,97},{2,34},{34,66},{66,9... | collective-permute-start | bytes 1966088 | tf_op jit(solution)/shard_map/ppermute | solution.py:454
  15.9 2.9 %collective-permute-start.6 = (bf16[256,1280]{1,0:T(8,128)(2,1)}, bf16[256,1280]{1,0:T(8,128)(2,1)}, u32[]{:S(2)}, u32[]{:S(2)}) collective-permute-start(bf16[256,1280]{1,0:T(8,128)(2,1)} %bitcast.23), channel_id=1, source_target_pairs={{32,0},{64,32},{96,64},{33,1},{65,33},{97,65},{34,2},{66,34},{98,6... | collective-permute-start | bytes 1966088 | tf_op jit(solution)/shard_map/ppermute | solution.py:457
  18.8 8.2 %copy.29 = bf16[1280,3,640]{0,2,1:T(8,128)(2,1)} copy(bf16[1280,3,640]{2,0,1:T(8,128)(2,1)} %param.10) | data formatting | bytes 9830400 | tf_op args[3]
  27.0 8.1 %copy.32.refs_2_.refs_5_.w_ref = bf16[1280,1920]{1,0:T(8,128)(2,1)} copy(bf16[1280,1920]{0,1:T(8,128)(2,1)} %bitcast.29) | data formatting | bytes 9830400 | tf_op jit(solution)/shard_map/reshape | solution.py:473
  39.5 3.4 %copy-done = bf16[9,256,1920]{2,1,0:T(8,128)(2,1)} copy-done((bf16[9,256,1920]{2,1,0:T(8,128)(2,1)}, bf16[9,256,1920]{2,1,0:T(8,128)(2,1)S(1)}, u32[]{:S(2)}) %copy-start) | copy-done | bytes 8847384
  45.5 3.9 %collective-permute-done.2 = s32[3,4,16]{2,1,0:T(4,128)S(1)} collective-permute-done((s32[3,4,16]{2,1,0:T(4,128)S(1)}, s32[3,4,16]{2,1,0:T(4,128)S(1)}, u32[]{:S(2)}, u32[]{:S(2)}) %collective-permute-start.2) | collective-permute-done | bytes 800 | tf_op jit(solution)/shard_map/ppermute | solution.py:460
  53.6 3.4 %collective-permute-start.9 = (bf16[256,1280]{1,0:T(8,128)(2,1)S(1)}, bf16[256,1280]{1,0:T(8,128)(2,1)}, u32[]{:S(2)}, u32[]{:S(2)}) collective-permute-start(bf16[256,1280]{1,0:T(8,128)(2,1)S(1)} %collective-permute-done.8.refs_2_), channel_id=1, source_target_pairs={{0,32},{32,64},{64,96},{1,33},{33,65},{65,97},{2,34},{34,66},{66,9... | collective-permute-start | bytes 1966088 | tf_op jit(solution)/shard_map/ppermute | solution.py:454
  58.4 3.5 %copy-done.1 = bf16[9,256,1920]{2,1,0:T(8,128)(2,1)S(1)} copy-done((bf16[9,256,1920]{2,1,0:T(8,128)(2,1)S(1)}, bf16[9,256,1920]{2,1,0:T(8,128)(2,1)}, u32[]{:S(2)}) %copy-start.1) | copy-done | bytes 8847384
  64.3 9.7 %project1.1.refs_6_ = bf16[9,256,1920]{2,1,0:T(8,128)(2,1)S(1)} custom-call(bf16[256,1280]{1,0:T(8,128)(2,1)} %collective-permute-done.4.refs_0_, bf16[256,1280]{1,0:T(8,128)(2,1)} %collective-permute-done.6.refs_1_, bf16[256,1280]{1,0:T(8,128)(2,1)S(1)} %collective-permute-done.8.refs_2_, ...), custom_call_target="tpu_custom_call", output_to_operand_aliasing={{}: (6, {})} | custom-call | flops 5033164800 | bytes 10158080 | tf_op jit(solution)/shard_map/project1/pallas_call | solution.py:85
  74.1 10.2 %project5.1 = bf16[9,256,1920]{2,1,0:T(8,128)(2,1)S(1)} custom-call(bf16[256,1280]{1,0:T(8,128)(2,1)} %collective-permute-done.5.refs_0_, bf16[256,1280]{1,0:T(8,128)(2,1)} %collective-permute-done.7.refs_1_, bf16[256,1280]{1,0:T(8,128)(2,1)} %collective-permute-done.9.refs_2_, ...), custom_call_target="tpu_custom_call", output_to_operand_aliasing={{}: (6, {})} | custom-call | flops 5033164800 | bytes 10158080 | tf_op jit(solution)/shard_map/project5/pallas_call | solution.py:85
  84.3 3.4 %copy-done.2 = bf16[9,256,1920]{2,1,0:T(8,128)(2,1)} copy-done((bf16[9,256,1920]{2,1,0:T(8,128)(2,1)}, bf16[9,256,1920]{2,1,0:T(8,128)(2,1)S(1)}, u32[]{:S(2)}) %copy-start.2) | copy-done | bytes 8847384
  87.7 3.5 %copy-done.3 = bf16[9,256,1920]{2,1,0:T(8,128)(2,1)S(1)} copy-done((bf16[9,256,1920]{2,1,0:T(8,128)(2,1)S(1)}, bf16[9,256,1920]{2,1,0:T(8,128)(2,1)}, u32[]{:S(2)}) %copy-start.3) | copy-done | bytes 8847384
  91.2 8.3 %attend_forward.1 = (bf16[256,1280]{1,0:T(8,128)(2,1)S(1)}, f32[256,640]{1,0:T(8,128)S(1)}, bf16[4,512,512]{2,1,0:T(8,128)(2,1)S(1)}, f32[4,8,128]{2,1,0:T(8,128)S(1)}) custom-call(s32[32]{0:T(128)S(1)} %reshape.64.local_ref, s32[36]{0:T(128)S(1)} %slice_reduce_fusion.count_ref, bf16[36,64,1920]{2,1,0:T(8,128)(2,1)S(1)} %bitcast.16, ...), custom_call_target="tpu_custom_call" | custom-call | flops 1073741824 | bytes 10485760 | tf_op jit(solution)/shard_map/attend_forward/pallas_call | solution.py:168
  103.1 14.7 %collective-permute-done.12.other_ref = bf16[256,1280]{1,0:T(8,128)(2,1)} collective-permute-done((bf16[256,1280]{1,0:T(8,128)(2,1)S(1)}, bf16[256,1280]{1,0:T(8,128)(2,1)}, u32[]{:S(2)}, u32[]{:S(2)}) %collective-permute-start.12) | collective-permute-done | bytes 655392 | tf_op jit(solution)/shard_map/ppermute | solution.py:509
  121.0 3.3 %middle.1 = (bf16[288,640]{1,0:T(8,128)(2,1)S(1)}, f32[256,640]{1,0:T(8,128)S(1)}) custom-call(s32[4]{0:T(128)S(1)} %slice_reduce_fusion.1.count_ref, s32[1]{0:T(128)} %bitcast.5.sec_ref, bf16[256,1280]{1,0:T(8,128)(2,1)S(1)} %copy-done.13, bf16[256,1280]{1,0:T(8,128)(2,1)} %collective-permute-done.12.other_ref, bf16[256,1280]{1,0:T(8,128)(2,1)S(1)} %bitcast.26, ...), custom_call_target="tpu_custom_call" | custom-call | flops 419430400 | bytes 6291456 | tf_op jit(solution)/shard_map/middle/pallas_call | solution.py:256
  127.5 3.2 %collective-permute-start.13 = (bf16[288,640]{1,0:T(8,128)(2,1)S(1)}, bf16[288,640]{1,0:T(8,128)(2,1)S(1)}, u32[]{:S(2)}, u32[]{:S(2)}) collective-permute-start(bf16[288,640]{1,0:T(8,128)(2,1)S(1)} %get-tuple-element.16.pay_ref.rest_0_), channel_id=1, source_target_pairs={{0,32},{32,64},{64,96},{1,33},{33,65},{65,97},{2,34},{34,66},{66,9... | collective-permute-start | bytes 1105928 | tf_op jit(solution)/shard_map/ppermute | solution.py:454
  135.8 3.2 %collective-permute-start.19 = (bf16[288,640]{1,0:T(8,128)(2,1)S(1)}, bf16[288,640]{1,0:T(8,128)(2,1)}, u32[]{:S(2)}, u32[]{:S(2)}) collective-permute-start(bf16[288,640]{1,0:T(8,128)(2,1)S(1)} %collective-permute-done.15.rest_3_), channel_id=1, source_target_pairs={{0,32},{32,64},{64,96},{1,33},{33,65},{65,97},{2,34},{34,66},{66,9... | collective-permute-start | bytes 1105928 | tf_op jit(solution)/shard_map/ppermute | solution.py:454
  141.8 4.8 %collective-permute-start.17 = (bf16[288,640]{1,0:T(8,128)(2,1)S(1)}, bf16[288,640]{1,0:T(8,128)(2,1)}, u32[]{:S(2)}, u32[]{:S(2)}) collective-permute-start(bf16[288,640]{1,0:T(8,128)(2,1)S(1)} %collective-permute-done.13.rest_1_), channel_id=1, source_target_pairs={{0,2},{2,0},{4,6},{6,4},{8,10},{10,8},{12,14},{14,12},{16,18},{18,... | collective-permute-start | bytes 1105928 | tf_op jit(solution)/shard_map/ppermute | solution.py:463
  148.4 3.5 %copy-done.4 = bf16[9,256,1920]{2,1,0:T(8,128)(2,1)S(1)} copy-done((bf16[9,256,1920]{2,1,0:T(8,128)(2,1)S(1)}, bf16[9,256,1920]{2,1,0:T(8,128)(2,1)}, u32[]{:S(2)}) %copy-start.4) | copy-done | bytes 8847384
  153.5 6.5 %query_grad.1.rest_11_ = bf16[256,640]{1,0:T(8,128)(2,1)S(1)} custom-call(s32[32]{0:T(128)S(1)} %reshape.64.local_ref, bf16[36,64,1920]{2,1,0:T(8,128)(2,1)S(1)} %bitcast.18, bf16[4,512,512]{2,1,0:T(8,128)(2,1)S(1)} %copy-done.10, bf16[288,640]{1,0:T(8,128)(2,1)S(1)} %get-tuple-element.16.pay_ref.rest_0_), custom_call_target="tpu_custom_call" | custom-call | flops 1073741824 | bytes 10485760 | tf_op jit(solution)/shard_map/query_grad/pallas_call | solution.py:293
  160.1 17.3 %key_grad.1 = (bf16[256,640]{1,0:T(8,128)(2,1)S(1)}, f32[256,640]{1,0:T(8,128)S(1)}) custom-call(s32[112]{0:T(128)S(1)} %reshape.58.list_ref, s32[4]{0:T(128)S(1)} %convert_reduce_fusion.1.n_ref, s32[4]{0:T(128)S(1)} %slice_reduce_fusion.1.count_ref, s32[1]{0:T(128)} %bitcast.5.sec_ref, bf16[36,64,1920]{2,1,0:T(8,128)(2,1)} %bitcast.15, ...), custom_call_target="tpu_custom_call" | custom-call | flops 12000000000 | bytes 16777216 | tf_op jit(solution)/shard_map/key_grad/pallas_call | solution.py:413
  177.7 7.2 %collective-permute-done.21 = bf16[256,640]{1,0:T(8,128)(2,1)S(1)} collective-permute-done((bf16[256,640]{1,0:T(8,128)(2,1)S(1)}, bf16[256,640]{1,0:T(8,128)(2,1)S(1)}, u32[]{:S(2)}, u32[]{:S(2)}) %collective-permute-start.21) | collective-permute-done | bytes 327712 | tf_op jit(solution)/shard_map/ppermute | solution.py:514
  (101 shorter events, 40.9 us)
Async XLA Ops:
  1.6 41.4 %collective-permute-start = (s32[4,16]{1,0:T(4,128)S(1)}, s32[4,16]{1,0:T(4,128)S(1)}, u32[]{:S(2)}, u32[]{:S(2)}) collective-permute-start(s32[4,16]{1,0:T(4,128)S(1)} %get-tuple-element.22), channel_id=1, source_target_pairs={{0,32},{32,64},{64,96},{1,33},{33,65},{65,97},{2,34},{34,66},{66,9... | collective-permute-start | bytes 776 | tf_op jit(solution)/shard_map/ppermute | solution.py:454
  4.8 38.2 %collective-permute-start.1 = (s32[4,16]{1,0:T(4,128)S(1)}, s32[4,16]{1,0:T(4,128)S(1)}, u32[]{:S(2)}, u32[]{:S(2)}) collective-permute-start(s32[4,16]{1,0:T(4,128)S(1)} %get-tuple-element.22), channel_id=1, source_target_pairs={{32,0},{64,32},{96,64},{33,1},{65,33},{97,65},{34,2},{66,34},{98,6... | collective-permute-start | bytes 776 | tf_op jit(solution)/shard_map/ppermute | solution.py:457
  6.9 44.8 %collective-permute-start.8 = (bf16[256,1280]{1,0:T(8,128)(2,1)}, bf16[256,1280]{1,0:T(8,128)(2,1)S(1)}, u32[]{:S(2)}, u32[]{:S(2)}) collective-permute-start(bf16[256,1280]{1,0:T(8,128)(2,1)} %bitcast.21), channel_id=1, source_target_pairs={{2,4},{4,2},{6,8},{8,6},{10,12},{12,10},{14,16},{16,14},{18,20},{2... | collective-permute-start | bytes 1966088 | tf_op jit(solution)/shard_map/ppermute | solution.py:460
  12.6 44.4 %collective-permute-start.4 = (bf16[256,1280]{1,0:T(8,128)(2,1)}, bf16[256,1280]{1,0:T(8,128)(2,1)}, u32[]{:S(2)}, u32[]{:S(2)}) collective-permute-start(bf16[256,1280]{1,0:T(8,128)(2,1)} %bitcast.22), channel_id=1, source_target_pairs={{0,32},{32,64},{64,96},{1,33},{33,65},{65,97},{2,34},{34,66},{66,9... | collective-permute-start | bytes 1966088 | tf_op jit(solution)/shard_map/ppermute | solution.py:454
  15.9 42.1 %collective-permute-start.6 = (bf16[256,1280]{1,0:T(8,128)(2,1)}, bf16[256,1280]{1,0:T(8,128)(2,1)}, u32[]{:S(2)}, u32[]{:S(2)}) collective-permute-start(bf16[256,1280]{1,0:T(8,128)(2,1)} %bitcast.23), channel_id=1, source_target_pairs={{32,0},{64,32},{96,64},{33,1},{65,33},{97,65},{34,2},{66,34},{98,6... | collective-permute-start | bytes 1966088 | tf_op jit(solution)/shard_map/ppermute | solution.py:457
  43.0 15.4 %collective-permute-start.11 = (bf16[256,1280]{1,0:T(8,128)(2,1)S(1)}, bf16[256,1280]{1,0:T(8,128)(2,1)S(1)}, u32[]{:S(2)}, u32[]{:S(2)}) collective-permute-start(bf16[256,1280]{1,0:T(8,128)(2,1)S(1)} %bitcast.25), channel_id=1, source_target_pairs={{0,2},{2,0},{4,6},{6,4},{8,10},{10,8},{12,14},{14,12},{16,18},{18,... | collective-permute-start | bytes 1966088 | tf_op jit(solution)/shard_map/ppermute | solution.py:463
  43.0 6.5 %collective-permute-start.2 = (s32[3,4,16]{2,1,0:T(4,128)S(1)}, s32[3,4,16]{2,1,0:T(4,128)S(1)}, u32[]{:S(2)}, u32[]{:S(2)}) collective-permute-start(s32[3,4,16]{2,1,0:T(4,128)S(1)} %pad_add_fusion), channel_id=1, source_target_pairs={{2,4},{4,2},{6,8},{8,6},{10,12},{12,10},{14,16},{16,14},{18,20},{2... | collective-permute-start | bytes 2312 | tf_op jit(solution)/shard_map/ppermute | solution.py:460
  49.4 2.2 %collective-permute-start.3 = (s32[3,4,16]{2,1,0:T(4,128)S(1)}, s32[3,4,16]{2,1,0:T(4,128)S(1)}, u32[]{:S(2)}, u32[]{:S(2)}) collective-permute-start(s32[3,4,16]{2,1,0:T(4,128)S(1)} %pad_add_fusion), channel_id=1, source_target_pairs={{0,2},{2,0},{4,6},{6,4},{8,10},{10,8},{12,14},{14,12},{16,18},{18,... | collective-permute-start | bytes 2312 | tf_op jit(solution)/shard_map/ppermute | solution.py:463
  51.7 22.3 %collective-permute-start.10 = (bf16[256,1280]{1,0:T(8,128)(2,1)S(1)}, bf16[256,1280]{1,0:T(8,128)(2,1)}, u32[]{:S(2)}, u32[]{:S(2)}) collective-permute-start(bf16[256,1280]{1,0:T(8,128)(2,1)S(1)} %collective-permute-done.8.refs_2_), channel_id=1, source_target_pairs={{32,0},{64,32},{96,64},{33,1},{65,33},{97,65},{34,2},{66,34},{98,6... | collective-permute-start | bytes 1966088 | tf_op jit(solution)/shard_map/ppermute | solution.py:457
  53.6 20.4 %collective-permute-start.9 = (bf16[256,1280]{1,0:T(8,128)(2,1)S(1)}, bf16[256,1280]{1,0:T(8,128)(2,1)}, u32[]{:S(2)}, u32[]{:S(2)}) collective-permute-start(bf16[256,1280]{1,0:T(8,128)(2,1)S(1)} %collective-permute-done.8.refs_2_), channel_id=1, source_target_pairs={{0,32},{32,64},{64,96},{1,33},{33,65},{65,97},{2,34},{34,66},{66,9... | collective-permute-start | bytes 1966088 | tf_op jit(solution)/shard_map/ppermute | solution.py:454
  57.0 17.0 %collective-permute-start.5 = (bf16[256,1280]{1,0:T(8,128)(2,1)}, bf16[256,1280]{1,0:T(8,128)(2,1)}, u32[]{:S(2)}, u32[]{:S(2)}) collective-permute-start(bf16[256,1280]{1,0:T(8,128)(2,1)} %collective-permute-done.4.refs_0_), channel_id=1, source_target_pairs={{0,2},{2,0},{4,6},{6,4},{8,10},{10,8},{12,14},{14,12},{16,18},{18,... | collective-permute-start | bytes 1966088 | tf_op jit(solution)/shard_map/ppermute | solution.py:463
  58.0 16.0 %collective-permute-start.7 = (bf16[256,1280]{1,0:T(8,128)(2,1)}, bf16[256,1280]{1,0:T(8,128)(2,1)}, u32[]{:S(2)}, u32[]{:S(2)}) collective-permute-start(bf16[256,1280]{1,0:T(8,128)(2,1)} %collective-permute-done.6.refs_1_), channel_id=1, source_target_pairs={{0,2},{2,0},{4,6},{6,4},{8,10},{10,8},{12,14},{14,12},{16,18},{18,... | collective-permute-start | bytes 1966088 | tf_op jit(solution)/shard_map/ppermute | solution.py:463
  74.0 13.7 %copy-start.7 = (bf16[640,1280]{1,0:T(8,128)(2,1)S(1)}, bf16[640,1280]{1,0:T(8,128)(2,1)}, u32[]{:S(2)}) copy-start(bf16[640,1280]{1,0:T(8,128)(2,1)} %w_out_ref.3) | copy-start | bytes 4915204
  101.7 16.0 %collective-permute-start.12 = (bf16[256,1280]{1,0:T(8,128)(2,1)S(1)}, bf16[256,1280]{1,0:T(8,128)(2,1)}, u32[]{:S(2)}, u32[]{:S(2)}) collective-permute-start(bf16[256,1280]{1,0:T(8,128)(2,1)S(1)} %get-tuple-element.13.mine_ref), channel_id=1, source_target_pairs={{0,1},{1,0},{2,3},{3,2},{4,5},{5,4},{6,7},{7,6},{8,9},{9,8},{10,11... | collective-permute-start | bytes 1966088 | tf_op jit(solution)/shard_map/ppermute | solution.py:509
  121.0 39.0 %slice-start = ((s8[4915200]{0:T(1024)(128)(4,1)}), s8[720896]{0:T(1024)(128)(4,1)S(1)}, s32[]{:S(2)}) async-start(s8[4915200]{0:T(1024)(128)(4,1)} %bitcast.19), calls=%async_computation | async-start | bytes 1441792
  125.2 10.6 %collective-permute-start.15 = (bf16[288,640]{1,0:T(8,128)(2,1)S(1)}, bf16[288,640]{1,0:T(8,128)(2,1)S(1)}, u32[]{:S(2)}, u32[]{:S(2)}) collective-permute-start(bf16[288,640]{1,0:T(8,128)(2,1)S(1)} %get-tuple-element.16.pay_ref.rest_0_), channel_id=1, source_target_pairs={{2,4},{4,2},{6,8},{8,6},{10,12},{12,10},{14,16},{16,14},{18,20},{2... | collective-permute-start | bytes 1105928 | tf_op jit(solution)/shard_map/ppermute | solution.py:460
  127.5 14.3 %collective-permute-start.13 = (bf16[288,640]{1,0:T(8,128)(2,1)S(1)}, bf16[288,640]{1,0:T(8,128)(2,1)S(1)}, u32[]{:S(2)}, u32[]{:S(2)}) collective-permute-start(bf16[288,640]{1,0:T(8,128)(2,1)S(1)} %get-tuple-element.16.pay_ref.rest_0_), channel_id=1, source_target_pairs={{0,32},{32,64},{64,96},{1,33},{33,65},{65,97},{2,34},{34,66},{66,9... | collective-permute-start | bytes 1105928 | tf_op jit(solution)/shard_map/ppermute | solution.py:454
  130.7 15.9 %collective-permute-start.14 = (bf16[288,640]{1,0:T(8,128)(2,1)S(1)}, bf16[288,640]{1,0:T(8,128)(2,1)S(1)}, u32[]{:S(2)}, u32[]{:S(2)}) collective-permute-start(bf16[288,640]{1,0:T(8,128)(2,1)S(1)} %get-tuple-element.16.pay_ref.rest_0_), channel_id=1, source_target_pairs={{32,0},{64,32},{96,64},{33,1},{65,33},{97,65},{34,2},{66,34},{98,6... | collective-permute-start | bytes 1105928 | tf_op jit(solution)/shard_map/ppermute | solution.py:457
  133.0 27.0 %collective-permute-start.16 = (bf16[288,640]{1,0:T(8,128)(2,1)S(1)}, bf16[288,640]{1,0:T(8,128)(2,1)S(1)}, u32[]{:S(2)}, u32[]{:S(2)}) collective-permute-start(bf16[288,640]{1,0:T(8,128)(2,1)S(1)} %get-tuple-element.16.pay_ref.rest_0_), channel_id=1, source_target_pairs={{0,2},{2,0},{4,6},{6,4},{8,10},{10,8},{12,14},{14,12},{16,18},{18,... | collective-permute-start | bytes 1105928 | tf_op jit(solution)/shard_map/ppermute | solution.py:463
  135.8 24.2 %collective-permute-start.19 = (bf16[288,640]{1,0:T(8,128)(2,1)S(1)}, bf16[288,640]{1,0:T(8,128)(2,1)}, u32[]{:S(2)}, u32[]{:S(2)}) collective-permute-start(bf16[288,640]{1,0:T(8,128)(2,1)S(1)} %collective-permute-done.15.rest_3_), channel_id=1, source_target_pairs={{0,32},{32,64},{64,96},{1,33},{33,65},{65,97},{2,34},{34,66},{66,9... | collective-permute-start | bytes 1105928 | tf_op jit(solution)/shard_map/ppermute | solution.py:454
  139.0 21.0 %collective-permute-start.20 = (bf16[288,640]{1,0:T(8,128)(2,1)S(1)}, bf16[288,640]{1,0:T(8,128)(2,1)}, u32[]{:S(2)}, u32[]{:S(2)}) collective-permute-start(bf16[288,640]{1,0:T(8,128)(2,1)S(1)} %collective-permute-done.15.rest_3_), channel_id=1, source_target_pairs={{32,0},{64,32},{96,64},{33,1},{65,33},{97,65},{34,2},{66,34},{98,6... | collective-permute-start | bytes 1105928 | tf_op jit(solution)/shard_map/ppermute | solution.py:457
  141.8 18.2 %collective-permute-start.17 = (bf16[288,640]{1,0:T(8,128)(2,1)S(1)}, bf16[288,640]{1,0:T(8,128)(2,1)}, u32[]{:S(2)}, u32[]{:S(2)}) collective-permute-start(bf16[288,640]{1,0:T(8,128)(2,1)S(1)} %collective-permute-done.13.rest_1_), channel_id=1, source_target_pairs={{0,2},{2,0},{4,6},{6,4},{8,10},{10,8},{12,14},{14,12},{16,18},{18,... | collective-permute-start | bytes 1105928 | tf_op jit(solution)/shard_map/ppermute | solution.py:463
  146.6 13.4 %collective-permute-start.18 = (bf16[288,640]{1,0:T(8,128)(2,1)S(1)}, bf16[288,640]{1,0:T(8,128)(2,1)}, u32[]{:S(2)}, u32[]{:S(2)}) collective-permute-start(bf16[288,640]{1,0:T(8,128)(2,1)S(1)} %collective-permute-done.14.rest_2_), channel_id=1, source_target_pairs={{0,2},{2,0},{4,6},{6,4},{8,10},{10,8},{12,14},{14,12},{16,18},{18,... | collective-permute-start | bytes 1105928 | tf_op jit(solution)/shard_map/ppermute | solution.py:463
  177.3 7.6 %collective-permute-start.21 = (bf16[256,640]{1,0:T(8,128)(2,1)S(1)}, bf16[256,640]{1,0:T(8,128)(2,1)S(1)}, u32[]{:S(2)}, u32[]{:S(2)}) collective-permute-start(bf16[256,640]{1,0:T(8,128)(2,1)S(1)} %get-tuple-element.20), channel_id=1, source_target_pairs={{0,1},{1,0},{2,3},{3,2},{4,5},{5,4},{6,7},{7,6},{8,9},{9,8},{10,11... | collective-permute-start | bytes 983048 | tf_op jit(solution)/shard_map/ppermute | solution.py:514
  (19 other events, 60.2 us)

commit v2 on v1

v2 whole, which is shorter than its diff:
```python
import functools
import math

import jax
import jax.numpy as jnp
from jax import lax
from jax.experimental import pallas as pl
from jax.experimental.pallas import tpu as pltpu
from jax.sharding import PartitionSpec as P

HEAD_DIM = 80
SCALE = HEAD_DIM ** (-0.5)
LOG2_SCALE = SCALE * math.log2(math.e)
BF16 = jnp.bfloat16
F32 = jnp.float32
MIB = 1 << 20
GROUPS = ((0, 3, 0, 256), (3, 2, 128, 384), (5, 3, 384, 256))
NEAR_CHUNK, LAST_CHUNK = 8, 2
STAT_ROWS = 32
BLOCKS = 12
SMALL = pl.CostEstimate(flops=1, bytes_accessed=1, transcendentals=0)
VMEM_LIMIT = 60 * MIB

NT_DIMS = (((1,), (1,)), ((), ()))


def dot(a, b):
    return jnp.dot(a, b, preferred_element_type=F32)


def dot_nt(a, b):
    return lax.dot_general(a, b, NT_DIMS, preferred_element_type=F32)


def head_row(head, first_lane, lanes):
    lane = lax.broadcasted_iota(jnp.int32, (1, lanes), 1) + first_lane
    return jnp.where((lane >= head * HEAD_DIM) & (lane < (head + 1) * HEAD_DIM), 1.0, 0.0).astype(F32)


def spread(x, group):
    h0, nh, l0, wd = group
    out = []
    for h in range(h0, h0 + nh):
        mask = jnp.broadcast_to(head_row(h, l0, wd), (16, wd)).astype(BF16)
        out += [x[r : r + 16] * mask for r in range(0, x.shape[0], 16)]
    return jnp.concatenate(out, axis=0)


def gather_heads(y, group, rows):
    h0, nh, l0, wd = group
    total = y[:rows] * head_row(h0, l0, wd)
    for k in range(1, nh):
        total = total + y[k * rows : (k + 1) * rows] * head_row(h0 + k, l0, wd)
    return total


def add_group(ref, rows, value, group):
    h0, nh, l0, wd = group
    ref[rows, l0 : l0 + wd] = ref[rows, l0 : l0 + wd] + value


def normalize(x):
    centred = x - jnp.mean(x, axis=-1, keepdims=True)
    inverse = lax.rsqrt(jnp.mean(centred * centred, axis=-1, keepdims=True) + 1e-06)
    return centred * inverse, inverse


def project_near_body(n, *refs):
    xs = refs[:n]
    gain_ref, w_ref = refs[n : n + 2]
    kv_ref, q_ref, x_scr = refs[n + 3 :]
    rows = xs[0].shape[0]
    step = pl.program_id(0)

    @pl.when(step == 0)
    def _():
        for k in range(n):
            x_scr[k * rows : (k + 1) * rows] = (normalize(xs[k][...].astype(F32))[0] * gain_ref[...]).astype(BF16)

    @pl.when(step > 0)
    def _():
        kv_ref[...] = dot(x_scr[...], w_ref[...]).astype(BF16).reshape(q_ref.shape)

    @pl.when(step == 0)
    def _():
        q_ref[...] = dot(x_scr[...], w_ref[...]).astype(BF16).reshape(q_ref.shape)


def whole(a):
    return pl.BlockSpec(a.shape, lambda i: (0,) * a.ndim)


def project_near(blocks, first, gain, w, buf):
    n = len(blocks)
    rows, width = blocks[0].shape
    feats = w.shape[2]
    return pl.pallas_call(
        functools.partial(project_near_body, n),
        grid=(3,),
        in_specs=[whole(b) for b in blocks]
        + [whole(gain), pl.BlockSpec((pl.squeezed, width, feats), lambda i: (i, 0, 0))]
        + [pl.BlockSpec(memory_space=pl.ANY)],
        out_specs=[
            pl.BlockSpec((n, rows, feats), lambda i: (first // n, 0, jnp.maximum(i - 1, 0))),
            pl.BlockSpec((n, rows, feats), lambda i: (0, 0, 0)),
        ],
        out_shape=[jax.ShapeDtypeStruct(buf.shape, BF16), jax.ShapeDtypeStruct((n, rows, feats), BF16)],
        scratch_shapes=[pltpu.VMEM((n * rows, width), BF16)],
        input_output_aliases={n + 2: 0},
        compiler_params=pltpu.CompilerParams(vmem_limit_bytes=VMEM_LIMIT),
        cost_estimate=SMALL,
        name="project_near",
    )(*blocks, gain, w, buf)


def project_own_body(x_ref, gain_ref, w_ref, kv_ref, q_ref, x_scr):
    step = pl.program_id(0)

    @pl.when(step == 0)
    def _():
        x_scr[...] = (normalize(x_ref[...].astype(F32))[0] * gain_ref[...]).astype(BF16)

    @pl.when(step < 2)
    def _():
        kv_ref[0] = dot(x_scr[...], w_ref[...]).astype(BF16)

    @pl.when(step == 2)
    def _():
        q_ref[...] = dot(x_scr[...], w_ref[...]).astype(BF16)


def project_own(x, gain, w):
    rows, width = x.shape
    feats = w.shape[2]
    return pl.pallas_call(
        project_own_body,
        grid=(3,),
        in_specs=[whole(x), whole(gain), pl.BlockSpec((pl.squeezed, width, feats), lambda i: ((i + 1) % 3, 0, 0))],
        out_specs=[
            pl.BlockSpec((1, rows, feats), lambda i: (0, 0, jnp.minimum(i, 1))),
            pl.BlockSpec((rows, feats), lambda i: (0, 0)),
        ],
        out_shape=[
            jax.ShapeDtypeStruct((BLOCKS, rows, 2 * feats), BF16),
            jax.ShapeDtypeStruct((rows, feats), BF16),
        ],
        scratch_shapes=[pltpu.VMEM((rows, width), BF16)],
        compiler_params=pltpu.CompilerParams(vmem_limit_bytes=VMEM_LIMIT),
        cost_estimate=SMALL,
        name="project_own",
    )(x, gain, w)


def project_queries_body(n, *refs):
    xs = refs[:n]
    gain_ref, w_ref, out_ref, x_scr = refs[n:]
    step = pl.program_id(0)
    for k in range(n):

        @pl.when(step == k)
        def _():
            x_scr[...] = xs[k][...]

    normed = (normalize(x_scr[...].astype(F32))[0] * gain_ref[...]).astype(BF16)
    out_ref[0] = dot(normed, w_ref[...]).astype(BF16)


def project_queries(blocks, gain, w):
    n = len(blocks)
    rows, width = blocks[0].shape
    feats = w.shape[2]
    return pl.pallas_call(
        functools.partial(project_queries_body, n),
        grid=(n,),
        in_specs=[whole(b) for b in blocks] + [whole(gain), pl.BlockSpec((pl.squeezed, width, feats), lambda i: (0, 0, 0))],
        out_specs=pl.BlockSpec((1, rows, feats), lambda i: (i, 0, 0)),
        out_shape=jax.ShapeDtypeStruct((n, rows, feats), BF16),
        scratch_shapes=[pltpu.VMEM((rows, width), BF16)],
        compiler_params=pltpu.CompilerParams(vmem_limit_bytes=VMEM_LIMIT),
        cost_estimate=SMALL,
        name="project_queries",
    )(*blocks, gain, w)


def lay_out_keys(local_ref, all_scr, kv_scr, i):
    nb = kv_scr.shape[1] // 64
    for n in range(nb):
        kv_scr[i, n * 64 : (n + 1) * 64, :] = all_scr[local_ref[i * nb + n]]


def forward_body(
    local_ref, count_ref, x0_ref, x1_ref, gain_ref, w_ref, kv_ref, q_ref, w_out_ref,
    part_ref, o_ref, lse_ref, p_ref, far_ref,
    x_scr, n_scr, w_scr, wo_scr, q_scr, all_scr, kv_scr, p_scr, sem, p_sem,
):
    tubes, keys, feats2 = kv_scr.shape
    feats = feats2 // 2
    nb = keys // 64
    rows = tubes * 64
    copies = [
        pltpu.make_async_copy(x0_ref, x_scr.at[:rows], sem.at[0]),
        pltpu.make_async_copy(x1_ref, x_scr.at[rows:], sem.at[1]),
        pltpu.make_async_copy(w_ref.at[1], w_scr.at[0], sem.at[2]),
        pltpu.make_async_copy(w_ref.at[2], w_scr.at[1], sem.at[3]),
        pltpu.make_async_copy(q_ref, q_scr, sem.at[4]),
        pltpu.make_async_copy(w_out_ref, wo_scr, sem.at[5]),
        pltpu.make_async_copy(kv_ref.at[:tubes], all_scr.at[:tubes], sem.at[6]),
        pltpu.make_async_copy(kv_ref.at[6 * tubes :], all_scr.at[tubes : 7 * tubes], sem.at[7]),
    ]
    for k in (0, 1, 2, 3, 6, 7, 4, 5):
        copies[k].start()
    for k in range(2):
        copies[k].wait()
        half = slice(k * rows, (k + 1) * rows)
        n_scr[half] = (normalize(x_scr[half].astype(F32))[0] * gain_ref[...]).astype(BF16)
    for k in range(2):
        copies[2 + k].wait()
        out = dot(n_scr[...], w_scr[k]).astype(BF16).reshape(2 * tubes, 64, feats)
        all_scr[7 * tubes :, :, k * feats : (k + 1) * feats] = out
    far_copy = pltpu.make_async_copy(all_scr.at[7 * tubes :], far_ref, sem.at[8])
    far_copy.start()
    for k in (6, 7, 4):
        copies[k].wait()
    lane = lax.broadcasted_iota(jnp.int32, (1, keys), 1)
    slot, place = lane // 64, lane % 64
    pick = lax.broadcasted_iota(jnp.int32, (64, 128), 0) == lax.broadcasted_iota(jnp.int32, (64, 128), 1) % 64
    o_ref[...] = jnp.zeros_like(o_ref)

    def tube(i):
        limit = jnp.zeros((1, keys), jnp.int32)
        for n in range(nb):
            limit = jnp.where(slot == n, count_ref[local_ref[i * nb + n]], limit)
        live = place < limit
        here = slice(i * 64, (i + 1) * 64)
        lay_out_keys(local_ref, all_scr, kv_scr, i)
        for group in GROUPS:
            h0, nh, l0, wd = group
            window = slice(l0, l0 + wd)
            q = spread(q_scr[here, window], group)
            s = dot_nt(q, kv_scr[i, :, window]) * LOG2_SCALE
            s = jnp.where(live, s, -1e30)
            top = jnp.max(s, axis=-1, keepdims=True)
            e = jnp.exp2(s - top)
            total = jnp.sum(e, axis=-1, keepdims=True)
            p = (e * (1.0 / total)).astype(BF16)
            p_scr[i, h0 * 64 : (h0 + nh) * 64, :] = p
            o = dot(p, kv_scr[i, :, feats + l0 : feats + l0 + wd])
            o_ref[here, window] += gather_heads(o, group, 64)
            lse = top + jnp.log2(total)
            for k in range(nh):
                column = jnp.broadcast_to(lse[k * 64 : (k + 1) * 64], (64, 128))
                lse_ref[i, h0 + k : h0 + k + 1, :] = jnp.sum(jnp.where(pick, column, 0.0), axis=0, keepdims=True)
        pltpu.make_async_copy(p_scr.at[i], p_ref.at[i], p_sem.at[i]).start()

    for i in range(tubes):
        tube(i)
    copies[5].wait()
    part_ref[...] = dot(o_ref[...].astype(BF16), wo_scr[...]).astype(BF16)
    far_copy.wait()
    for i in range(tubes):
        pltpu.make_async_copy(p_scr.at[i], p_ref.at[i], p_sem.at[i]).wait()


def attend_forward(local, counts, x0, x1, gain, w, kv, q, w_out):
    rows, feats = q.shape
    tubes = rows // 64
    nb = local.shape[0] // tubes
    keys = nb * 64
    heads = feats // HEAD_DIM
    width = w_out.shape[1]
    vmem = pl.BlockSpec(memory_space=pltpu.VMEM)
    smem = pl.BlockSpec(memory_space=pltpu.SMEM)
    hbm = pl.BlockSpec(memory_space=pl.ANY)
    return pl.pallas_call(
        forward_body,
        in_specs=[smem, smem, hbm, hbm, vmem, hbm, hbm, hbm, hbm],
        out_specs=[vmem, vmem, vmem, hbm, hbm],
        out_shape=[
            jax.ShapeDtypeStruct((rows, width), BF16),
            jax.ShapeDtypeStruct((rows, feats), F32),
            jax.ShapeDtypeStruct((tubes, heads, 128), F32),
            jax.ShapeDtypeStruct((tubes, heads * 64, keys), BF16),
            jax.ShapeDtypeStruct((2 * tubes, 64, 2 * feats), BF16),
        ],
        scratch_shapes=[
            pltpu.VMEM((2 * rows, width), BF16),
            pltpu.VMEM((2 * rows, width), BF16),
            pltpu.VMEM((2, width, feats), BF16),
            pltpu.VMEM((feats, width), BF16),
            pltpu.VMEM((rows, feats), BF16),
            pltpu.VMEM((9 * tubes, 64, 2 * feats), BF16),
            pltpu.VMEM((tubes, keys, 2 * feats), BF16),
            pltpu.VMEM((tubes, heads * 64, keys), BF16),
            pltpu.SemaphoreType.DMA((9,)),
            pltpu.SemaphoreType.DMA((tubes,)),
        ],
        compiler_params=pltpu.CompilerParams(vmem_limit_bytes=VMEM_LIMIT),
        cost_estimate=SMALL,
        name="attend_forward",
    )(local, counts, x0, x1, gain, w, kv, q, w_out)


def parts_of(x, n):
    out = []
    for _ in range(n):
        piece = x.astype(BF16)
        out.append(piece)
        x = x - piece.astype(F32)
    return out


def middle_body(
    count_ref, sec_ref, mine_hbm, other_hbm, video_hbm, target_hbm, w_out_hbm, o_hbm, lse_ref, pay_ref, g_ref,
    mine_ref, other_ref, video_ref, target_ref, w_out_ref, o_ref, sem,
):
    rows, width = video_ref.shape
    feats = w_out_ref.shape[0]
    pairs = [
        (mine_hbm, mine_ref),
        (other_hbm, other_ref),
        (video_hbm, video_ref),
        (target_hbm, target_ref),
        (w_out_hbm, w_out_ref),
        (o_hbm, o_ref),
    ]
    copies = [pltpu.make_async_copy(*pair, sem.at[k]) for k, pair in enumerate(pairs)]
    for c in copies:
        c.start()
    heads = feats // HEAD_DIM
    tubes = rows // 64
    row = lax.broadcasted_iota(jnp.int32, (rows, 1), 0)
    limit = jnp.zeros((rows, 1), jnp.int32)
    for i in range(tubes):
        limit = jnp.where(row // 64 == i, count_ref[i], limit)
    valid = row % 64 < limit
    for c in copies[:4]:
        c.wait()
    mixed = mine_ref[...].astype(F32) + other_ref[...].astype(F32)
    g = jnp.where(valid, 2.0 * (video_ref[...].astype(F32) + mixed - target_ref[...].astype(F32)), 0.0)
    half = width // 2
    g_ref[...] = jnp.where(sec_ref[0] == 0, g[:, :half], g[:, half:])
    copies[4].wait()
    d_att = dot_nt(g.astype(BF16), w_out_ref[...]).astype(BF16)
    copies[5].wait()
    pay_ref[:rows] = d_att
    prod = d_att.astype(F32) * o_ref[...]
    head = lax.broadcasted_iota(jnp.int32, (heads, feats), 0)
    lane = lax.broadcasted_iota(jnp.int32, (heads, feats), 1)
    ones = ((lane >= head * HEAD_DIM) & (lane < (head + 1) * HEAD_DIM)).astype(F32)
    inner = []
    for i in range(tubes):
        one = prod[i * 64 : (i + 1) * 64]
        inner.append(
            lax.dot_general(
                ones,
                jnp.concatenate([one, one], axis=0),
                NT_DIMS,
                precision=lax.Precision.HIGHEST,
                preferred_element_type=F32,
            )
        )
    inner = jnp.concatenate(inner, axis=0)
    lse = lse_ref[...].reshape(tubes * heads, 128)
    for k, piece in enumerate(parts_of(lse, 3) + parts_of(inner, 2)):
        pay_ref[rows:, k * 128 : (k + 1) * 128] = piece


def middle(counts, sec, mine, other, video, target, w_out, o, lse):
    rows, width = video.shape
    feats = w_out.shape[0]
    vmem = pl.BlockSpec(memory_space=pltpu.VMEM)
    smem = pl.BlockSpec(memory_space=pltpu.SMEM)
    return pl.pallas_call(
        middle_body,
        in_specs=[smem, smem] + [pl.BlockSpec(memory_space=pl.ANY)] * 6 + [vmem],
        out_specs=[vmem, vmem],
        out_shape=[
            jax.ShapeDtypeStruct((rows + STAT_ROWS, feats), BF16),
            jax.ShapeDtypeStruct((rows, width // 2), F32),
        ],
        scratch_shapes=[pltpu.VMEM((rows, width), BF16)] * 4
        + [pltpu.VMEM((feats, width), BF16), pltpu.VMEM((rows, feats), F32), pltpu.SemaphoreType.DMA((6,))],
        compiler_params=pltpu.CompilerParams(vmem_limit_bytes=VMEM_LIMIT),
        cost_estimate=SMALL,
        name="middle",
    )(counts, sec, mine, other, video, target, w_out, o, lse)


def key_pass(
    list_ref, n_ref, count_ref, q_scr, kv_scr, pay_scr, lse_scr, inner_scr, qc_scr, dc_scr, km_scr, vm_scr, dk_scr, dv_scr, grad_scr
):
    tubes = kv_scr.shape[0]
    size = qc_scr.shape[0] // 64
    feats = q_scr.shape[2]
    most = list_ref.shape[0] // tubes
    low = lax.broadcasted_iota(jnp.int32, (8, 128), 1) < 64
    key_row = lax.broadcasted_iota(jnp.int32, (64, 1), 0)

    def tube(j, carry):
        alive = key_row < count_ref[j]
        block = pl.ds(pl.multiple_of(j * 64, 64), 64)
        for group in GROUPS:
            h0, nh, l0, wd = group
            these = slice(h0 * 64, (h0 + nh) * 64)
            km_scr[these, :wd] = spread(kv_scr[j, :, l0 : l0 + wd], group)
            vm_scr[these, :wd] = spread(kv_scr[j, :, feats + l0 : feats + l0 + wd], group)
        dk_scr[...] = jnp.zeros_like(dk_scr)
        dv_scr[...] = jnp.zeros_like(dv_scr)

        def chunk(c, carry):
            lses, inners = [], []
            for t in range(size):
                place = c * size + t
                i = list_ref[j * most + jnp.minimum(place, most - 1)]
                slot, w = i // tubes, i % tubes
                qc_scr[t * 64 : (t + 1) * 64, :] = q_scr[i]
                dc_scr[t * 64 : (t + 1) * 64, :] = pay_scr[slot, pl.ds(pl.multiple_of(w * 64, 64), 64), :]
                lses.append(jnp.where(place < n_ref[j], lse_scr[i], 1e30))
                inners.append(inner_scr[i])
            lse = jnp.concatenate([jnp.where(low, lses[t], lses[t + 1]) for t in range(0, size, 2)], axis=1)
            inner = jnp.concatenate([jnp.where(low, inners[t], inners[t + 1]) for t in range(0, size, 2)], axis=1)
            for group in GROUPS:
                h0, nh, l0, wd = group
                window = slice(l0, l0 + wd)
                these = slice(h0 * 64, (h0 + nh) * 64)
                qc, dc = qc_scr[:, window], dc_scr[:, window]
                s = dot_nt(km_scr[these, :wd], qc)
                d_prob = dot_nt(vm_scr[these, :wd], dc)
                p, d_score = [], []
                for m in range(nh):
                    part = slice(m * 64, (m + 1) * 64)
                    head = slice(h0 + m, h0 + m + 1)
                    one = jnp.where(alive, jnp.exp2(s[part] * LOG2_SCALE - lse[head]), 0.0)
                    p.append(one.astype(BF16))
                    d_score.append((one * (d_prob[part] - inner[head])).astype(BF16))
                dk_scr[these, :wd] += dot(jnp.concatenate(d_score, axis=0), qc)
                dv_scr[these, :wd] += dot(jnp.concatenate(p, axis=0), dc)
            return carry

        lax.fori_loop(0, (n_ref[j] + size - 1) // size, chunk, carry)
        for group in GROUPS:
            h0, nh, l0, wd = group
            these = slice(h0 * 64, (h0 + nh) * 64)
            grad_scr[block, l0 : l0 + wd] += gather_heads(dk_scr[these, :wd], group, 64) * SCALE
            grad_scr[block, feats + l0 : feats + l0 + wd] += gather_heads(dv_scr[these, :wd], group, 64)
        return carry

    lax.fori_loop(0, tubes, tube, 0)


def stats_of(pay_scr, k, rows, tubes, lse_scr, inner_scr):
    parts = [pay_scr[k, rows:, j * 128 : (j + 1) * 128].astype(F32) for j in range(5)]
    lse_scr[k * tubes : (k + 1) * tubes] = (parts[0] + parts[1] + parts[2]).reshape(tubes, -1, 128)
    inner_scr[k * tubes : (k + 1) * tubes] = (parts[3] + parts[4]).reshape(tubes, -1, 128)


def query_body(local_ref, pay_ref, kv_ref, far_ref, p_ref, dq_ref, all_scr, kv_scr, p_scr, pay_scr, dq_scr, sem, p_sem):
    tubes, keys, feats2 = kv_scr.shape
    feats = feats2 // 2
    pay_copy = pltpu.make_async_copy(pay_ref, pay_scr, sem.at[0])
    p_copies = [pltpu.make_async_copy(p_ref.at[i], p_scr.at[i], p_sem.at[i]) for i in range(tubes)]
    copies = [
        pltpu.make_async_copy(kv_ref.at[:tubes], all_scr.at[:tubes], sem.at[1]),
        pltpu.make_async_copy(kv_ref.at[6 * tubes :], all_scr.at[tubes : 7 * tubes], sem.at[2]),
        pltpu.make_async_copy(far_ref, all_scr.at[7 * tubes :], sem.at[3]),
    ]
    for c in copies + [pay_copy] + p_copies:
        c.start()
    for c in copies:
        c.wait()
    dq_scr[...] = jnp.zeros_like(dq_scr)
    pay_copy.wait()
    for i in range(tubes):
        here = slice(i * 64, (i + 1) * 64)
        lay_out_keys(local_ref, all_scr, kv_scr, i)
        p_copies[i].wait()
        for group in GROUPS:
            h0, nh, l0, wd = group
            window = slice(l0, l0 + wd)
            d_att = spread(pay_scr[here, window], group)
            d_prob = dot_nt(d_att, kv_scr[i, :, feats + l0 : feats + l0 + wd])
            p = p_scr[i, h0 * 64 : (h0 + nh) * 64, :].astype(F32)
            inner = jnp.sum(d_prob * p, axis=-1, keepdims=True)
            d_score = (p * (d_prob - inner)).astype(BF16)
            dq_scr[here, window] += gather_heads(dot(d_score, kv_scr[i, :, window]), group, 64)
    dq_ref[...] = (dq_scr[...] * SCALE).astype(BF16)


def query_grad(local, pay, kv, far, p):
    feats = pay.shape[1]
    tubes, _, keys = p.shape
    vmem = pl.BlockSpec(memory_space=pltpu.VMEM)
    smem = pl.BlockSpec(memory_space=pltpu.SMEM)
    hbm = pl.BlockSpec(memory_space=pl.ANY)
    return pl.pallas_call(
        query_body,
        in_specs=[smem] + [hbm] * 4,
        out_specs=vmem,
        out_shape=jax.ShapeDtypeStruct((tubes * 64, feats), BF16),
        scratch_shapes=[
            pltpu.VMEM((9 * tubes, 64, 2 * feats), BF16),
            pltpu.VMEM((tubes, keys, 2 * feats), BF16),
            pltpu.VMEM(p.shape, BF16),
            pltpu.VMEM(pay.shape, BF16),
            pltpu.VMEM((tubes * 64, feats), F32),
            pltpu.SemaphoreType.DMA((4,)),
            pltpu.SemaphoreType.DMA((tubes,)),
        ],
        compiler_params=pltpu.CompilerParams(vmem_limit_bytes=VMEM_LIMIT),
        cost_estimate=SMALL,
        name="query_grad",
    )(local, pay, kv, far, p)


def key_near_body(n, list_ref, n_ref, count_ref, own_q_ref, q_ref, kv_ref, w_ref, dq_ref, *rest):
    pays = rest[:n]
    grad_ref, base_ref, w_scr, dq_scr, q_scr, kv_scr, pay_scr, *scr, sem = rest[n:]
    lse_scr, inner_scr = scr[:2]
    tubes = kv_scr.shape[0]
    rows = tubes * 64
    pay_copies = [pltpu.make_async_copy(pays[k], pay_scr.at[k], sem.at[k]) for k in range(n)]
    first = [
        pltpu.make_async_copy(dq_ref, dq_scr, sem.at[n + 4]),
        pltpu.make_async_copy(w_ref.at[0], w_scr, sem.at[n]),
    ]
    copies = [
        pltpu.make_async_copy(own_q_ref, q_scr.at[:tubes], sem.at[n + 1]),
        pltpu.make_async_copy(q_ref.at[: (n - 1) * tubes], q_scr.at[tubes:], sem.at[n + 2]),
        pltpu.make_async_copy(kv_ref.at[:tubes], kv_scr, sem.at[n + 3]),
    ]
    for c in first + pay_copies + copies:
        c.start()
    grad_ref[...] = jnp.zeros_like(grad_ref)
    for c in first:
        c.wait()
    base_ref[...] = dot_nt(dq_scr[...], w_scr[...])
    for k in range(n):
        pay_copies[k].wait()
        stats_of(pay_scr, k, rows, tubes, lse_scr, inner_scr)
    for c in copies:
        c.wait()
    key_pass(list_ref, n_ref, count_ref, q_scr, kv_scr, pay_scr, *scr, grad_ref)


def key_scratch(n, tubes, feats, size):
    rows = tubes * 64
    heads = feats // HEAD_DIM
    return [
        pltpu.VMEM((n * tubes, 64, feats), BF16),
        pltpu.VMEM((tubes, 64, 2 * feats), BF16),
        pltpu.VMEM((n, rows + STAT_ROWS, feats), BF16),
        pltpu.VMEM((n * tubes, heads, 128), F32),
        pltpu.VMEM((n * tubes, heads, 128), F32),
        pltpu.VMEM((size * 64, feats), BF16),
        pltpu.VMEM((size * 64, feats), BF16),
        pltpu.VMEM((heads * 64, 384), BF16),
        pltpu.VMEM((heads * 64, 384), BF16),
        pltpu.VMEM((heads * 64, 384), F32),
        pltpu.VMEM((heads * 64, 384), F32),
    ]


def key_near(lists, lengths, counts, own_q, q, kv, w, dq, pays):
    rows, feats = dq.shape
    width = w.shape[1]
    tubes = rows // 64
    n = len(pays)
    vmem = pl.BlockSpec(memory_space=pltpu.VMEM)
    smem = pl.BlockSpec(memory_space=pltpu.SMEM)
    hbm = pl.BlockSpec(memory_space=pl.ANY)
    return pl.pallas_call(
        functools.partial(key_near_body, n),
        in_specs=[smem] * 3 + [hbm] * (5 + n),
        out_specs=[vmem, vmem],
        out_shape=[
            jax.ShapeDtypeStruct((rows, 2 * feats), F32),
            jax.ShapeDtypeStruct((rows, width), F32),
        ],
        scratch_shapes=[pltpu.VMEM((width, feats), BF16), pltpu.VMEM((rows, feats), BF16)]
        + key_scratch(n, tubes, feats, NEAR_CHUNK)
        + [pltpu.SemaphoreType.DMA((n + 5,))],
        compiler_params=pltpu.CompilerParams(vmem_limit_bytes=VMEM_LIMIT),
        cost_estimate=SMALL,
        name="key_near",
    )(lists, lengths, counts, own_q, q, kv, w, dq, *pays)


def key_last_body(n, first, list_ref, n_ref, count_ref, sec_ref, q_ref, kv_ref, w_ref, acc_ref, *rest):
    pays = rest[:n]
    video_ref, gain_ref, base_ref, g_ref, send_ref, keep_ref = rest[n : n + 6]
    q_scr, kv_scr, pay_scr, *scr, w_scr, grad_scr, x_scr, base_scr, g_scr, sem = rest[n + 6 :]
    lse_scr, inner_scr = scr[:2]
    tubes = kv_scr.shape[0]
    rows = tubes * 64
    feats = q_scr.shape[2]
    q_copy = pltpu.make_async_copy(q_ref.at[first * tubes : (first + n) * tubes], q_scr, sem.at[0])
    kv_copy = pltpu.make_async_copy(kv_ref.at[:tubes], kv_scr, sem.at[1])
    acc_copy = pltpu.make_async_copy(acc_ref, grad_scr, sem.at[2])
    w_copy = pltpu.make_async_copy(w_ref.at[1:], w_scr, sem.at[3])
    x_copy = pltpu.make_async_copy(video_ref, x_scr, sem.at[4])
    base_copy = pltpu.make_async_copy(base_ref, base_scr, sem.at[5])
    g_copy = pltpu.make_async_copy(g_ref, g_scr, sem.at[6])
    pay_copies = [pltpu.make_async_copy(pays[k], pay_scr.at[k], sem.at[7 + k]) for k in range(n)]
    for c in pay_copies + [q_copy, kv_copy, acc_copy, w_copy, x_copy, base_copy, g_copy]:
        c.start()
    for k, c in enumerate(pay_copies):
        c.wait()
        stats_of(pay_scr, k, rows, tubes, lse_scr, inner_scr)
    q_copy.wait()
    kv_copy.wait()
    acc_copy.wait()
    key_pass(list_ref, n_ref, count_ref, q_scr, kv_scr, pay_scr, *scr, grad_scr)
    d_proj = grad_scr[...].astype(BF16)
    x_copy.wait()
    xhat, inverse = normalize(x_scr[...].astype(F32))
    w_copy.wait()
    base_copy.wait()
    g_copy.wait()
    d_normed = base_scr[...] + dot_nt(d_proj[:, :feats], w_scr[0]) + dot_nt(d_proj[:, feats:], w_scr[1])
    scaled = d_normed * gain_ref[...]
    out = (
        scaled
        - jnp.mean(scaled, axis=-1, keepdims=True)
        - xhat * jnp.mean(scaled * xhat, axis=-1, keepdims=True)
    ) * inverse
    half = out.shape[1] // 2
    lower = sec_ref[0] == 0
    send_ref[...] = jnp.where(lower, out[:, half:], out[:, :half]).astype(BF16)
    keep_ref[...] = jnp.where(lower, out[:, :half], out[:, half:]) + g_scr[...]


def key_last(first, lists, lengths, counts, sec, q, kv, w, acc, pays, video, gain, base, g):
    rows, width = video.shape
    feats = q.shape[2]
    tubes = rows // 64
    n = len(pays)
    vmem = pl.BlockSpec(memory_space=pltpu.VMEM)
    smem = pl.BlockSpec(memory_space=pltpu.SMEM)
    hbm = pl.BlockSpec(memory_space=pl.ANY)
    return pl.pallas_call(
        functools.partial(key_last_body, n, first),
        in_specs=[smem] * 4 + [hbm] * (5 + n) + [vmem] + [hbm] * 2,
        out_specs=[vmem, vmem],
        out_shape=[
            jax.ShapeDtypeStruct((rows, width // 2), BF16),
            jax.ShapeDtypeStruct((rows, width // 2), F32),
        ],
        scratch_shapes=key_scratch(n, tubes, feats, LAST_CHUNK)
        + [
            pltpu.VMEM((2, width, feats), BF16),
            pltpu.VMEM((rows, 2 * feats), F32),
            pltpu.VMEM((rows, width), BF16),
            pltpu.VMEM((rows, width), F32),
            pltpu.VMEM((rows, width // 2), F32),
            pltpu.SemaphoreType.DMA((7 + n,)),
        ],
        compiler_params=pltpu.CompilerParams(vmem_limit_bytes=VMEM_LIMIT),
        cost_estimate=SMALL,
        name="key_last",
    )(lists, lengths, counts, sec, q, kv, w, acc, *pays, video, gain, base, g)


def per_device(video, target, gain, w_qkv, w_out, neighbours, counts):
    tt, th, tw, tube, width = video.shape
    feats = w_qkv.shape[2]
    nb = neighbours.shape[3]
    rows = tt * th * tw * tube
    n_t, n_h = lax.axis_size("tm"), lax.axis_size("height")
    t_here, h_here, sec = lax.axis_index("tm"), lax.axis_index("height"), lax.axis_index("section")
    off_chip = [p for h in range(1, n_h - 1, 2) for p in ((h, h + 1), (h + 1, h))]
    on_chip = [(h, h ^ 1) for h in range(n_h)]
    pair_times = [(t, t ^ 1) for t in range(n_t)]
    other_times = [p for t in range(1, n_t - 1, 2) for p in ((t, t + 1), (t + 1, t))]
    swap = [(0, 1), (1, 0)]

    def from_pair(x):
        return lax.ppermute(x, "tm", pair_times)

    def from_other(x):
        return lax.ppermute(x, "tm", other_times)

    def from_off(x):
        return lax.ppermute(x, "height", off_chip)

    def from_mate(x):
        return lax.ppermute(x, "height", on_chip)

    video = video.reshape(rows, width)
    target = target.reshape(rows, width)
    gain = gain.reshape(1, width)
    w = jnp.transpose(w_qkv, (1, 0, 2))

    off, mate, pair, other = from_off(video), from_mate(video), from_pair(video), from_other(video)
    meta = jnp.concatenate(
        [neighbours.reshape(tw, nb) + 1, counts.reshape(tw, 1), jnp.zeros((tw, 16 - nb - 1), jnp.int32)], axis=1
    )
    own_video, meta, _ = lax.optimization_barrier((video, meta, mate))
    kv, own_q = project_own(own_video, gain, w)
    three = jnp.stack([meta, from_pair(meta), from_other(meta)])
    off_meta, mate_meta = from_off(three), from_mate(three)
    off, off_meta, mate_meta, kv = lax.optimization_barrier((off, off_meta, mate_meta, kv))
    corners = from_pair(off), from_other(off)
    mates = mate, from_mate(pair), from_mate(other)
    kv, near_q = project_near((pair, other, off, *mates), 6, gain, w, kv)
    kv = kv.reshape(BLOCKS * tw, tube, 2 * feats)

    meta = jnp.concatenate([three, off_meta[:1], mate_meta, off_meta[1:]]).reshape(9 * tw, 16)
    listed = meta[:, :nb] - 1
    count_q = meta[:, nb].reshape(9, tw)
    count_all = count_q.reshape(9 * tw)

    ids = neighbours.reshape(tw, nb)
    t_of, h_of, w_of = ids // (n_h * tw), ids // tw % n_h, ids % tw
    step = jnp.where(t_of == t_here, 0, jnp.where(t_of == t_here + 1 - 2 * (t_here % 2), 1, 2))
    slot = jnp.where(
        h_of == h_here,
        step,
        jnp.where(h_of == h_here + 1 - 2 * (h_here % 2), 4 + step, jnp.where(step == 0, 3, 6 + step)),
    )
    local = (slot * tw + w_of).reshape(tw * nb)
    own_ids = (t_here * n_h + h_here) * tw + jnp.arange(tw, dtype=jnp.int32)
    names = jnp.any(listed[None] == own_ids[:, None, None], axis=2)

    def listing(first, last, most):
        named = names[:, first:last]
        where = jnp.arange(last - first, dtype=jnp.int32)
        rank = jnp.sum(named[:, None, :] & (where[None, :] < where[:, None])[None], axis=2)
        hit = named[:, None, :] & (rank[:, None, :] == jnp.arange(most)[None, :, None])
        places = jnp.sum(jnp.where(hit, where, 0), axis=2).astype(jnp.int32).reshape(tw * most)
        return places, jnp.sum(named, axis=1).astype(jnp.int32)

    near_list, near_n = listing(0, 7 * tw, 24)
    last_list, last_n = listing(7 * tw, 9 * tw, 8)
    sec = sec.reshape(1).astype(jnp.int32)
    own_counts = counts.reshape(tw)

    part, o, lse, p, far = attend_forward(local, count_all, *corners, gain, w, kv, own_q, w_out)
    other = lax.ppermute(part, "section", swap)
    part, videos = lax.optimization_barrier((part, corners))
    far_q = project_queries(videos, gain, w).reshape(2 * tw, tube, feats)
    other, far_q, near_list, near_n, last_list, last_n = lax.optimization_barrier(
        (other, far_q, near_list, near_n, last_list, last_n)
    )
    pay, g = middle(own_counts, sec, part, other, video, target, w_out, o, lse)
    off, mate = from_off(pay), from_mate(pay)
    pair, after = from_pair(pay), from_other(pay)
    dq = query_grad(local, pay, kv, far, p)
    dq, off = lax.optimization_barrier((dq, off))
    near, mates, corners = (pay, pair, after, off), (mate, from_mate(pair), from_mate(after)), (from_pair(off), from_other(off))
    acc, base = key_near(
        near_list, near_n, own_counts, own_q.reshape(tw, tube, feats), near_q.reshape(6 * tw, tube, feats), kv, w, dq, [*near, *mates]
    )
    send, keep = key_last(0, last_list, last_n, own_counts, sec, far_q, kv, w, acc, corners, video, gain, base, g)
    got = lax.ppermute(send, "section", swap)
    return (keep + got.astype(F32)).astype(BF16).reshape(tt, th, tw, tube, width // 2)


def solution(mesh):
    in_specs = (
        P("tm", "height", None, None, None),
        P("tm", "height", None, None, None),
        P(),
        P(None, None, "section"),
        P("section", None),
        P("tm", "height", None, None),
        P("tm", "height", None),
    )
    out_specs = P("tm", "height", None, None, "section")
    return jax.shard_map(
        per_device, mesh=mesh, in_specs=in_specs, out_specs=out_specs, check_vma=False
    )
```

time: 188 us -> 156 us (0.83)
  the two profiles are of different devices: /device:TPU:105 before, /device:TPU:54 now
where the time goes in v2:
time: 156 us; the launch traced here: 155 us
  Pallas kernels  80.3 us (51%)
  starting transfers between devices  29.7 us (19%)
  waiting for transfers between devices  29.4 us (19%)
  local copies, waits for them, and re-layouts  9.79 us (6%)
  other arithmetic  5.69 us (4%)
    pallas_call x1, Pallas kernels, project_near(): pl.pallas_call(functools.partial(project_near_body, n), grid=(3,), in_spe...  16.9 us
    ppermute x5, starting transfers between devices, from_other(): return lax.ppermute(x, 'tm', other_times)  14.1 us
    pallas_call x1, Pallas kernels, key_near(): pl.pallas_call(functools.partial(key_near_body, n), in_specs=[smem] * 3 +...  12.9 us
    pallas_call x1, Pallas kernels, attend_forward(): pl.pallas_call(forward_body, in_specs=[smem, smem, hbm, hbm, vmem, hbm, h...  12.2 us
    pallas_call x1, Pallas kernels, key_last(): pl.pallas_call(functools.partial(key_last_body, n, first), in_specs=[smem...  12.1 us
    pallas_call x1, Pallas kernels, query_grad(): pl.pallas_call(query_body, in_specs=[smem] + [hbm] * 4, out_specs=vmem, o...  10 us
    ppermute x1, waiting for transfers between devices, per_device(): got = lax.ppermute(send, 'section', swap)  9.79 us
    ppermute x1, waiting for transfers between devices, per_device(): other = lax.ppermute(part, 'section', swap)  9.01 us
  transfers between devices with their start and end apart: 22, of which 7 were waited for; matrix products, arithmetic and copies ran while one was open for 6% of the time, Pallas kernels for 32%

profile of v2, /device:TPU:54, one launch (start us, length us, event | category | flops | bytes accessed | tf_op | source)
XLA Modules:
  0.0 155.3 jit_solution(9211657357147385107)
XLA Ops:
  0.0 3.4 %collective-permute-start.3 = (bf16[256,1280]{1,0:T(8,128)(2,1)}, bf16[256,1280]{1,0:T(8,128)(2,1)S(1)}, u32[]{:S(2)}, u32[]{:S(2)}) collective-permute-start(bf16[256,1280]{1,0:T(8,128)(2,1)} %bitcast.32), channel_id=1, source_target_pairs={{2,4},{4,2},{6,8},{8,6},{10,12},{12,10},{14,16},{16,14},{18,20},{2... | collective-permute-start | bytes 1966088 | tf_op jit(solution)/shard_map/ppermute | solution.py:683
  4.8 1.9 %collective-permute-start.9 = (bf16[256,1280]{1,0:T(8,128)(2,1)}, bf16[256,1280]{1,0:T(8,128)(2,1)}, u32[]{:S(2)}, u32[]{:S(2)}) collective-permute-start(bf16[256,1280]{1,0:T(8,128)(2,1)} %bitcast.34), channel_id=1, source_target_pairs={{32,64},{64,32},{33,65},{65,33},{34,66},{66,34},{35,67},{67,35},{3... | collective-permute-start | bytes 1966088 | tf_op jit(solution)/shard_map/ppermute | solution.py:680
  11.3 3.6 %collective-permute-start.2 = (s32[4,16]{1,0:T(4,128)S(1)}, s32[4,16]{1,0:T(4,128)S(1)}, u32[]{:S(2)}, u32[]{:S(2)}) collective-permute-start(s32[4,16]{1,0:T(4,128)S(1)} %add_add_fusion), channel_id=1, source_target_pairs={{32,64},{64,32},{33,65},{65,33},{34,66},{66,34},{35,67},{67,35},{3... | collective-permute-start | bytes 776 | tf_op jit(solution)/shard_map/ppermute | solution.py:680
  14.9 5.8 %project_own.1 = (bf16[12,256,1280]{2,1,0:T(8,128)(2,1)}, bf16[256,640]{1,0:T(8,128)(2,1)}) custom-call(bf16[256,1280]{1,0:T(8,128)(2,1)} %bitcast.35, f32[1,1280]{1,0:T(1,128)} %reshape.86.gain_ref.refs_6_.refs_2_.rest_3_, bf16[3,1280,640]{2,1,0:T(8,128)(2,1)} %bitcast.25), custom_call_target="tpu_custom_call" | custom-call | flops 1 | bytes 1 | tf_op jit(solution)/shard_map/project_own/pallas_call | solution.py:135
  21.6 2.9 %collective-permute-done.9.refs_1_ = bf16[256,1280]{1,0:T(8,128)(2,1)} collective-permute-done((bf16[256,1280]{1,0:T(8,128)(2,1)}, bf16[256,1280]{1,0:T(8,128)(2,1)}, u32[]{:S(2)}, u32[]{:S(2)}) %collective-permute-start.9) | collective-permute-done | bytes 655392 | tf_op jit(solution)/shard_map/ppermute | solution.py:680
  24.6 2.9 %collective-permute-start.4 = (s32[3,4,16]{2,1,0:T(4,128)S(1)}, s32[3,4,16]{2,1,0:T(4,128)S(1)}, u32[]{:S(2)}, u32[]{:S(2)}) collective-permute-start(s32[3,4,16]{2,1,0:T(4,128)S(1)} %pad_add_fusion), channel_id=1, source_target_pairs={{2,4},{4,2},{6,8},{8,6},{10,12},{12,10},{14,16},{16,14},{18,20},{2... | collective-permute-start | bytes 2312 | tf_op jit(solution)/shard_map/ppermute | solution.py:683
  29.0 2.1 %collective-permute-done.4 = s32[3,4,16]{2,1,0:T(4,128)S(1)} collective-permute-done((s32[3,4,16]{2,1,0:T(4,128)S(1)}, s32[3,4,16]{2,1,0:T(4,128)S(1)}, u32[]{:S(2)}, u32[]{:S(2)}) %collective-permute-start.4) | collective-permute-done | bytes 800 | tf_op jit(solution)/shard_map/ppermute | solution.py:683
  31.1 2.1 %collective-permute-start.7 = (bf16[256,1280]{1,0:T(8,128)(2,1)S(1)}, bf16[256,1280]{1,0:T(8,128)(2,1)S(1)}, u32[]{:S(2)}, u32[]{:S(2)}) collective-permute-start(bf16[256,1280]{1,0:T(8,128)(2,1)S(1)} %collective-permute-done.3.refs_2_), channel_id=1, source_target_pairs={{32,64},{64,32},{33,65},{65,33},{34,66},{66,34},{35,67},{67,35},{3... | collective-permute-start | bytes 1966088 | tf_op jit(solution)/shard_map/ppermute | solution.py:680
  35.0 16.9 %project_near.1 = (bf16[12,256,1280]{2,1,0:T(8,128)(2,1)}, bf16[6,256,640]{2,1,0:T(8,128)(2,1)}) custom-call(bf16[256,1280]{1,0:T(8,128)(2,1)} %copy-done.4, bf16[256,1280]{1,0:T(8,128)(2,1)} %collective-permute-done.9.refs_1_, bf16[256,1280]{1,0:T(8,128)(2,1)} %copy-done.2, bf16[256,1280]{1,0:T(8,128)(2,1)} %copy-done.3, ...), custom_call_target="tpu_custom_call", output_to_operand_aliasing={{0}: (8, {})} | custom-call | flops 1 | bytes 1 | tf_op jit(solution)/shard_map/project_near/pallas_call | solution.py:97
  53.0 12.2 %attend_forward.1 = (bf16[256,1280]{1,0:T(8,128)(2,1)}, f32[256,640]{1,0:T(8,128)}, f32[4,8,128]{2,1,0:T(8,128)}, bf16[4,512,512]{2,1,0:T(8,128)(2,1)}, bf16[8,64,1280]{2,1,0:T(8,128)(2,1)}) custom-call(s32[32]{0:T(128)} %fusion.2.local_ref, s32[36]{0:T(128)} %slice_reduce_fusion.count_ref, bf16[256,1280]{1,0:T(8,128)(2,1)} %copy-done, ...), custom_call_target="tpu_custom_call" | custom-call | flops 1 | bytes 1 | tf_op jit(solution)/shard_map/attend_forward/pallas_call | solution.py:274
  69.2 4.6 %project_queries.1 = bf16[2,256,640]{2,1,0:T(8,128)(2,1)} custom-call(bf16[256,1280]{1,0:T(8,128)(2,1)} %copy-done, bf16[256,1280]{1,0:T(8,128)(2,1)} %copy-done.1, f32[1,1280]{1,0:T(1,128)} %reshape.86.gain_ref.refs_6_.refs_2_.rest_3_, bf16[3,1280,640]{2,1,0:T(8,128)(2,1)} %bitcast.28), custom_call_target="tpu_custom_call" | custom-call | flops 1 | bytes 1 | tf_op jit(solution)/shard_map/project_queries/pallas_call | solution.py:172
  73.8 9.0 %collective-permute-done.12.other_hbm = bf16[256,1280]{1,0:T(8,128)(2,1)S(1)} collective-permute-done((bf16[256,1280]{1,0:T(8,128)(2,1)}, bf16[256,1280]{1,0:T(8,128)(2,1)S(1)}, u32[]{:S(2)}, u32[]{:S(2)}) %collective-permute-start.12) | collective-permute-done | bytes 655392 | tf_op jit(solution)/shard_map/ppermute | solution.py:738
  83.7 5.8 %middle.1 = (bf16[288,640]{1,0:T(8,128)(2,1)}, f32[256,640]{1,0:T(8,128)}) custom-call(s32[4]{0:T(128)} %bitcast.45, s32[1]{0:T(128)} %bitcast.10.sec_ref, bf16[256,1280]{1,0:T(8,128)(2,1)} %get-tuple-element.55.mine_hbm, bf16[256,1280]{1,0:T(8,128)(2,1)} %copy-done.6, bf16[256,1280]{1,0:T(8,128)(2,1)} %bitcast.36, bf16[256,1280]{1,0:T(8,128)(2,1)} %bitcast.41, ...), custom_call_target="tpu_custom_call" | custom-call | flops 1 | bytes 1 | tf_op jit(solution)/shard_map/middle/pallas_call | solution.py:373
  90.6 3.1 %collective-permute-start.15 = (bf16[288,640]{1,0:T(8,128)(2,1)}, bf16[288,640]{1,0:T(8,128)(2,1)S(1)}, u32[]{:S(2)}, u32[]{:S(2)}) collective-permute-start(bf16[288,640]{1,0:T(8,128)(2,1)} %get-tuple-element.59.pay_ref.rest_0_), channel_id=1, source_target_pairs={{32,64},{64,32},{33,65},{65,33},{34,66},{66,34},{35,67},{67,35},{3... | collective-permute-start | bytes 1105928 | tf_op jit(solution)/shard_map/ppermute | solution.py:680
  93.8 1.9 %collective-permute-start.13 = (bf16[288,640]{1,0:T(8,128)(2,1)}, bf16[288,640]{1,0:T(8,128)(2,1)S(1)}, u32[]{:S(2)}, u32[]{:S(2)}) collective-permute-start(bf16[288,640]{1,0:T(8,128)(2,1)} %get-tuple-element.59.pay_ref.rest_0_), channel_id=1, source_target_pairs={{2,4},{4,2},{6,8},{8,6},{10,12},{12,10},{14,16},{16,14},{18,20},{2... | collective-permute-start | bytes 1105928 | tf_op jit(solution)/shard_map/ppermute | solution.py:683
  95.7 2.0 %collective-permute-start.16 = (bf16[288,640]{1,0:T(8,128)(2,1)}, bf16[288,640]{1,0:T(8,128)(2,1)S(1)}, u32[]{:S(2)}, u32[]{:S(2)}) collective-permute-start(bf16[288,640]{1,0:T(8,128)(2,1)} %get-tuple-element.59.pay_ref.rest_0_), channel_id=1, source_target_pairs={{0,2},{2,0},{4,6},{6,4},{8,10},{10,8},{12,14},{14,12},{16,18},{18,... | collective-permute-start | bytes 1105928 | tf_op jit(solution)/shard_map/ppermute | solution.py:686
  97.7 2.7 %collective-permute-done.14.rest_1_ = bf16[288,640]{1,0:T(8,128)(2,1)S(1)} collective-permute-done((bf16[288,640]{1,0:T(8,128)(2,1)}, bf16[288,640]{1,0:T(8,128)(2,1)S(1)}, u32[]{:S(2)}, u32[]{:S(2)}) %collective-permute-start.14) | collective-permute-done | bytes 368672 | tf_op jit(solution)/shard_map/ppermute | solution.py:677
  100.4 2.6 %collective-permute-done.15.rest_2_ = bf16[288,640]{1,0:T(8,128)(2,1)S(1)} collective-permute-done((bf16[288,640]{1,0:T(8,128)(2,1)}, bf16[288,640]{1,0:T(8,128)(2,1)S(1)}, u32[]{:S(2)}, u32[]{:S(2)}) %collective-permute-start.15) | collective-permute-done | bytes 368672 | tf_op jit(solution)/shard_map/ppermute | solution.py:680
  103.1 10.0 %query_grad.1.dq_ref = bf16[256,640]{1,0:T(8,128)(2,1)} custom-call(s32[32]{0:T(128)} %fusion.2.local_ref, bf16[288,640]{1,0:T(8,128)(2,1)} %get-tuple-element.59.pay_ref.rest_0_, bf16[48,64,1280]{2,1,0:T(8,128)(2,1)} %bitcast.22, bf16[8,64,1280]{2,1,0:T(8,128)(2,1)} %get-tuple-element.60.far_ref, bf16[4,512,512]{2,1,0:T(8,128)(2,1)} %get-tuple-element.61.p_ref), custom_call_target="tpu_custom_call" | custom-call | flops 1 | bytes 1 | tf_op jit(solution)/shard_map/query_grad/pallas_call | solution.py:495
  113.2 3.4 %collective-permute-start.20 = (bf16[288,640]{1,0:T(8,128)(2,1)S(1)}, bf16[288,640]{1,0:T(8,128)(2,1)S(1)}, u32[]{:S(2)}, u32[]{:S(2)}) collective-permute-start(bf16[288,640]{1,0:T(8,128)(2,1)S(1)} %collective-permute-done.13.rest_3_), channel_id=1, source_target_pairs={{32,64},{64,32},{33,65},{65,33},{34,66},{66,34},{35,67},{67,35},{3... | collective-permute-start | bytes 1105928 | tf_op jit(solution)/shard_map/ppermute | solution.py:680
  117.7 12.9 %key_near.1 = (f32[256,1280]{1,0:T(8,128)}, f32[256,1280]{1,0:T(8,128)}) custom-call(s32[96]{0:T(128)} %reshape.90.list_ref, s32[4]{0:T(128)} %convert_reduce_fusion.3.n_ref, s32[4]{0:T(128)} %bitcast.46, bf16[4,64,640]{2,1,0:T(8,128)(2,1)} %bitcast.40, bf16[24,64,640]{2,1,0:T(8,128)(2,1)} %bitcast.39, bf16[48,64,1280]{2,1,0:T(8,128)(2,1)} %bitcast.23, ...), custom_call_target="tpu_custom_call" | custom-call | flops 1 | bytes 1 | tf_op jit(solution)/shard_map/key_near/pallas_call | solution.py:571
  131.5 12.1 %key_last.1 = (bf16[256,640]{1,0:T(8,128)(2,1)}, f32[256,640]{1,0:T(8,128)}) custom-call(s32[32]{0:T(128)} %reshape.91.list_ref, s32[4]{0:T(128)} %convert_reduce_fusion.2.n_ref, s32[4]{0:T(128)} %bitcast.47, s32[1]{0:T(128)} %bitcast.10.sec_ref, bf16[8,64,640]{2,1,0:T(8,128)(2,1)} %bitcast.38, bf16[48,64,1280]{2,1,0:T(8,128)(2,1)} %bitcast.24, ...), custom_call_target="tpu_custom_call" | custom-call | flops 1 | bytes 1 | tf_op jit(solution)/shard_map/key_last/pallas_call | solution.py:640
  143.7 9.8 %collective-permute-done.21 = bf16[256,640]{1,0:T(8,128)(2,1)S(1)} collective-permute-done((bf16[256,640]{1,0:T(8,128)(2,1)}, bf16[256,640]{1,0:T(8,128)(2,1)S(1)}, u32[]{:S(2)}, u32[]{:S(2)}) %collective-permute-start.21) | collective-permute-done | bytes 327712 | tf_op jit(solution)/shard_map/ppermute | solution.py:754
  153.4 1.9 %add_convert_fusion = bf16[256,640]{1,0:T(8,128)(2,1)} fusion(f32[256,640]{1,0:T(8,128)} %get-tuple-element.67, bf16[256,640]{1,0:T(8,128)(2,1)S(1)} %collective-permute-done.21), kind=kLoop, calls=%fused_computation | loop fusion | flops 491520 | bytes 1310720 | tf_op jit(solution)/shard_map/convert_element_type | solution.py:755
  (92 shorter events, 19.2 us)
Async XLA Ops:
  0.0 10.9 %collective-permute-start = (bf16[256,1280]{1,0:T(8,128)(2,1)}, bf16[256,1280]{1,0:T(8,128)(2,1)S(1)}, u32[]{:S(2)}, u32[]{:S(2)}) collective-permute-start(bf16[256,1280]{1,0:T(8,128)(2,1)} %bitcast.31), channel_id=1, source_target_pairs={{0,2},{2,0},{4,6},{6,4},{8,10},{10,8},{12,14},{14,12},{16,18},{18,... | collective-permute-start | bytes 1966088 | tf_op jit(solution)/shard_map/ppermute | solution.py:686
  0.0 29.0 %collective-permute-start.3 = (bf16[256,1280]{1,0:T(8,128)(2,1)}, bf16[256,1280]{1,0:T(8,128)(2,1)S(1)}, u32[]{:S(2)}, u32[]{:S(2)}) collective-permute-start(bf16[256,1280]{1,0:T(8,128)(2,1)} %bitcast.32), channel_id=1, source_target_pairs={{2,4},{4,2},{6,8},{8,6},{10,12},{12,10},{14,16},{16,14},{18,20},{2... | collective-permute-start | bytes 1966088 | tf_op jit(solution)/shard_map/ppermute | solution.py:683
  3.4 17.6 %collective-permute-start.8 = (bf16[256,1280]{1,0:T(8,128)(2,1)}, bf16[256,1280]{1,0:T(8,128)(2,1)S(1)}, u32[]{:S(2)}, u32[]{:S(2)}) collective-permute-start(bf16[256,1280]{1,0:T(8,128)(2,1)} %bitcast.33), channel_id=1, source_target_pairs={{0,32},{32,0},{64,96},{96,64},{1,33},{33,1},{65,97},{97,65},{2,34}... | collective-permute-start | bytes 1966088 | tf_op jit(solution)/shard_map/ppermute | solution.py:677
  4.8 19.7 %collective-permute-start.9 = (bf16[256,1280]{1,0:T(8,128)(2,1)}, bf16[256,1280]{1,0:T(8,128)(2,1)}, u32[]{:S(2)}, u32[]{:S(2)}) collective-permute-start(bf16[256,1280]{1,0:T(8,128)(2,1)} %bitcast.34), channel_id=1, source_target_pairs={{32,64},{64,32},{33,65},{65,33},{34,66},{66,34},{35,67},{67,35},{3... | collective-permute-start | bytes 1966088 | tf_op jit(solution)/shard_map/ppermute | solution.py:680
  10.9 13.7 %collective-permute-start.1 = (s32[4,16]{1,0:T(4,128)S(1)}, s32[4,16]{1,0:T(4,128)S(1)}, u32[]{:S(2)}, u32[]{:S(2)}) collective-permute-start(s32[4,16]{1,0:T(4,128)S(1)} %add_add_fusion), channel_id=1, source_target_pairs={{0,32},{32,0},{64,96},{96,64},{1,33},{33,1},{65,97},{97,65},{2,34}... | collective-permute-start | bytes 776 | tf_op jit(solution)/shard_map/ppermute | solution.py:677
  11.3 13.3 %collective-permute-start.2 = (s32[4,16]{1,0:T(4,128)S(1)}, s32[4,16]{1,0:T(4,128)S(1)}, u32[]{:S(2)}, u32[]{:S(2)}) collective-permute-start(s32[4,16]{1,0:T(4,128)S(1)} %add_add_fusion), channel_id=1, source_target_pairs={{32,64},{64,32},{33,65},{65,33},{34,66},{66,34},{35,67},{67,35},{3... | collective-permute-start | bytes 776 | tf_op jit(solution)/shard_map/ppermute | solution.py:680
  21.0 13.2 %copy-start.4 = (bf16[256,1280]{1,0:T(8,128)(2,1)}, bf16[256,1280]{1,0:T(8,128)(2,1)S(1)}, u32[]{:S(2)}) copy-start(bf16[256,1280]{1,0:T(8,128)(2,1)S(1)} %collective-permute-done.8.refs_0_) | copy-start | bytes 1966084
  21.0 13.2 %collective-permute-start.10 = (bf16[256,1280]{1,0:T(8,128)(2,1)S(1)}, bf16[256,1280]{1,0:T(8,128)(2,1)S(1)}, u32[]{:S(2)}, u32[]{:S(2)}) collective-permute-start(bf16[256,1280]{1,0:T(8,128)(2,1)S(1)} %collective-permute-done.8.refs_0_), channel_id=1, source_target_pairs={{0,2},{2,0},{4,6},{6,4},{8,10},{10,8},{12,14},{14,12},{16,18},{18,... | collective-permute-start | bytes 1966088 | tf_op jit(solution)/shard_map/ppermute | solution.py:686
  24.5 9.7 %collective-permute-start.11 = (bf16[256,1280]{1,0:T(8,128)(2,1)}, bf16[256,1280]{1,0:T(8,128)(2,1)}, u32[]{:S(2)}, u32[]{:S(2)}) collective-permute-start(bf16[256,1280]{1,0:T(8,128)(2,1)} %collective-permute-done.9.refs_1_), channel_id=1, source_target_pairs={{0,2},{2,0},{4,6},{6,4},{8,10},{10,8},{12,14},{14,12},{16,18},{18,... | collective-permute-start | bytes 1966088 | tf_op jit(solution)/shard_map/ppermute | solution.py:686
  24.6 6.5 %collective-permute-start.4 = (s32[3,4,16]{2,1,0:T(4,128)S(1)}, s32[3,4,16]{2,1,0:T(4,128)S(1)}, u32[]{:S(2)}, u32[]{:S(2)}) collective-permute-start(s32[3,4,16]{2,1,0:T(4,128)S(1)} %pad_add_fusion), channel_id=1, source_target_pairs={{2,4},{4,2},{6,8},{8,6},{10,12},{12,10},{14,16},{16,14},{18,20},{2... | collective-permute-start | bytes 2312 | tf_op jit(solution)/shard_map/ppermute | solution.py:683
  27.5 3.5 %collective-permute-start.5 = (s32[3,4,16]{2,1,0:T(4,128)S(1)}, s32[3,4,16]{2,1,0:T(4,128)S(1)}, u32[]{:S(2)}, u32[]{:S(2)}) collective-permute-start(s32[3,4,16]{2,1,0:T(4,128)S(1)} %pad_add_fusion), channel_id=1, source_target_pairs={{0,2},{2,0},{4,6},{6,4},{8,10},{10,8},{12,14},{14,12},{16,18},{18,... | collective-permute-start | bytes 2312 | tf_op jit(solution)/shard_map/ppermute | solution.py:686
  31.1 20.8 %collective-permute-start.6 = (bf16[256,1280]{1,0:T(8,128)(2,1)S(1)}, bf16[256,1280]{1,0:T(8,128)(2,1)S(1)}, u32[]{:S(2)}, u32[]{:S(2)}) collective-permute-start(bf16[256,1280]{1,0:T(8,128)(2,1)S(1)} %collective-permute-done.3.refs_2_), channel_id=1, source_target_pairs={{0,32},{32,0},{64,96},{96,64},{1,33},{33,1},{65,97},{97,65},{2,34}... | collective-permute-start | bytes 1966088 | tf_op jit(solution)/shard_map/ppermute | solution.py:677
  31.1 20.9 %collective-permute-start.7 = (bf16[256,1280]{1,0:T(8,128)(2,1)S(1)}, bf16[256,1280]{1,0:T(8,128)(2,1)S(1)}, u32[]{:S(2)}, u32[]{:S(2)}) collective-permute-start(bf16[256,1280]{1,0:T(8,128)(2,1)S(1)} %collective-permute-done.3.refs_2_), channel_id=1, source_target_pairs={{32,64},{64,32},{33,65},{65,33},{34,66},{66,34},{35,67},{67,35},{3... | collective-permute-start | bytes 1966088 | tf_op jit(solution)/shard_map/ppermute | solution.py:680
  65.2 17.6 %collective-permute-start.12 = (bf16[256,1280]{1,0:T(8,128)(2,1)}, bf16[256,1280]{1,0:T(8,128)(2,1)S(1)}, u32[]{:S(2)}, u32[]{:S(2)}) collective-permute-start(bf16[256,1280]{1,0:T(8,128)(2,1)} %get-tuple-element.55.mine_hbm), channel_id=1, source_target_pairs={{0,1},{1,0},{2,3},{3,2},{4,5},{5,4},{6,7},{7,6},{8,9},{9,8},{10,11... | collective-permute-start | bytes 1966088 | tf_op jit(solution)/shard_map/ppermute | solution.py:738
  89.5 10.9 %collective-permute-start.14 = (bf16[288,640]{1,0:T(8,128)(2,1)}, bf16[288,640]{1,0:T(8,128)(2,1)S(1)}, u32[]{:S(2)}, u32[]{:S(2)}) collective-permute-start(bf16[288,640]{1,0:T(8,128)(2,1)} %get-tuple-element.59.pay_ref.rest_0_), channel_id=1, source_target_pairs={{0,32},{32,0},{64,96},{96,64},{1,33},{33,1},{65,97},{97,65},{2,34}... | collective-permute-start | bytes 1105928 | tf_op jit(solution)/shard_map/ppermute | solution.py:677
  90.6 12.4 %collective-permute-start.15 = (bf16[288,640]{1,0:T(8,128)(2,1)}, bf16[288,640]{1,0:T(8,128)(2,1)S(1)}, u32[]{:S(2)}, u32[]{:S(2)}) collective-permute-start(bf16[288,640]{1,0:T(8,128)(2,1)} %get-tuple-element.59.pay_ref.rest_0_), channel_id=1, source_target_pairs={{32,64},{64,32},{33,65},{65,33},{34,66},{66,34},{35,67},{67,35},{3... | collective-permute-start | bytes 1105928 | tf_op jit(solution)/shard_map/ppermute | solution.py:680
  93.8 19.3 %collective-permute-start.13 = (bf16[288,640]{1,0:T(8,128)(2,1)}, bf16[288,640]{1,0:T(8,128)(2,1)S(1)}, u32[]{:S(2)}, u32[]{:S(2)}) collective-permute-start(bf16[288,640]{1,0:T(8,128)(2,1)} %get-tuple-element.59.pay_ref.rest_0_), channel_id=1, source_target_pairs={{2,4},{4,2},{6,8},{8,6},{10,12},{12,10},{14,16},{16,14},{18,20},{2... | collective-permute-start | bytes 1105928 | tf_op jit(solution)/shard_map/ppermute | solution.py:683
  95.7 20.9 %collective-permute-start.16 = (bf16[288,640]{1,0:T(8,128)(2,1)}, bf16[288,640]{1,0:T(8,128)(2,1)S(1)}, u32[]{:S(2)}, u32[]{:S(2)}) collective-permute-start(bf16[288,640]{1,0:T(8,128)(2,1)} %get-tuple-element.59.pay_ref.rest_0_), channel_id=1, source_target_pairs={{0,2},{2,0},{4,6},{6,4},{8,10},{10,8},{12,14},{14,12},{16,18},{18,... | collective-permute-start | bytes 1105928 | tf_op jit(solution)/shard_map/ppermute | solution.py:686
  100.4 12.7 %copy-start.8 = (bf16[288,640]{1,0:T(8,128)(2,1)}, bf16[288,640]{1,0:T(8,128)(2,1)S(1)}, u32[]{:S(2)}) copy-start(bf16[288,640]{1,0:T(8,128)(2,1)S(1)} %collective-permute-done.14.rest_1_) | copy-start | bytes 1105924
  100.4 16.2 %collective-permute-start.17 = (bf16[288,640]{1,0:T(8,128)(2,1)S(1)}, bf16[288,640]{1,0:T(8,128)(2,1)S(1)}, u32[]{:S(2)}, u32[]{:S(2)}) collective-permute-start(bf16[288,640]{1,0:T(8,128)(2,1)S(1)} %collective-permute-done.14.rest_1_), channel_id=1, source_target_pairs={{0,2},{2,0},{4,6},{6,4},{8,10},{10,8},{12,14},{14,12},{16,18},{18,... | collective-permute-start | bytes 1105928 | tf_op jit(solution)/shard_map/ppermute | solution.py:686
  103.1 13.6 %collective-permute-start.18 = (bf16[288,640]{1,0:T(8,128)(2,1)S(1)}, bf16[288,640]{1,0:T(8,128)(2,1)S(1)}, u32[]{:S(2)}, u32[]{:S(2)}) collective-permute-start(bf16[288,640]{1,0:T(8,128)(2,1)S(1)} %collective-permute-done.15.rest_2_), channel_id=1, source_target_pairs={{0,2},{2,0},{4,6},{6,4},{8,10},{10,8},{12,14},{14,12},{16,18},{18,... | collective-permute-start | bytes 1105928 | tf_op jit(solution)/shard_map/ppermute | solution.py:686
  113.1 17.5 %collective-permute-start.19 = (bf16[288,640]{1,0:T(8,128)(2,1)S(1)}, bf16[288,640]{1,0:T(8,128)(2,1)S(1)}, u32[]{:S(2)}, u32[]{:S(2)}) collective-permute-start(bf16[288,640]{1,0:T(8,128)(2,1)S(1)} %collective-permute-done.13.rest_3_), channel_id=1, source_target_pairs={{0,32},{32,0},{64,96},{96,64},{1,33},{33,1},{65,97},{97,65},{2,34}... | collective-permute-start | bytes 1105928 | tf_op jit(solution)/shard_map/ppermute | solution.py:677
  113.2 17.4 %collective-permute-start.20 = (bf16[288,640]{1,0:T(8,128)(2,1)S(1)}, bf16[288,640]{1,0:T(8,128)(2,1)S(1)}, u32[]{:S(2)}, u32[]{:S(2)}) collective-permute-start(bf16[288,640]{1,0:T(8,128)(2,1)S(1)} %collective-permute-done.13.rest_3_), channel_id=1, source_target_pairs={{32,64},{64,32},{33,65},{65,33},{34,66},{66,34},{35,67},{67,35},{3... | collective-permute-start | bytes 1105928 | tf_op jit(solution)/shard_map/ppermute | solution.py:680
  143.6 9.9 %collective-permute-start.21 = (bf16[256,640]{1,0:T(8,128)(2,1)}, bf16[256,640]{1,0:T(8,128)(2,1)S(1)}, u32[]{:S(2)}, u32[]{:S(2)}) collective-permute-start(bf16[256,640]{1,0:T(8,128)(2,1)} %get-tuple-element.68), channel_id=1, source_target_pairs={{0,1},{1,0},{2,3},{3,2},{4,5},{5,4},{6,7},{7,6},{8,9},{9,8},{10,11... | collective-permute-start | bytes 983048 | tf_op jit(solution)/shard_map/ppermute | solution.py:754
  (13 other events, 36.4 us)

commit v3 on v2

--- a/solution.py
+++ b/solution.py
@@ -19,7 +19,7 @@
 STAT_ROWS = 32
 BLOCKS = 12
 SMALL = pl.CostEstimate(flops=1, bytes_accessed=1, transcendentals=0)
-VMEM_LIMIT = 60 * MIB
+VMEM_LIMIT = 52 * MIB
 
 NT_DIMS = (((1,), (1,)), ((), ()))
 
@@ -59,6 +59,10 @@
     ref[rows, l0 : l0 + wd] = ref[rows, l0 : l0 + wd] + value
 
 
+def gain_of(gain_ref):
+    return gain_ref[...].reshape(1, -1)
+
+
 def normalize(x):
     centred = x - jnp.mean(x, axis=-1, keepdims=True)
     inverse = lax.rsqrt(jnp.mean(centred * centred, axis=-1, keepdims=True) + 1e-06)
@@ -68,22 +72,15 @@
 def project_near_body(n, *refs):
     xs = refs[:n]
     gain_ref, w_ref = refs[n : n + 2]
-    kv_ref, q_ref, x_scr = refs[n + 3 :]
+    kv_ref, x_scr = refs[n + 3 :]
     rows = xs[0].shape[0]
-    step = pl.program_id(0)
-
-    @pl.when(step == 0)
+
+    @pl.when(pl.program_id(0) == 0)
     def _():
         for k in range(n):
-            x_scr[k * rows : (k + 1) * rows] = (normalize(xs[k][...].astype(F32))[0] * gain_ref[...]).astype(BF16)
-
-    @pl.when(step > 0)
-    def _():
-        kv_ref[...] = dot(x_scr[...], w_ref[...]).astype(BF16).reshape(q_ref.shape)
-
-    @pl.when(step == 0)
-    def _():
-        q_ref[...] = dot(x_scr[...], w_ref[...]).astype(BF16).reshape(q_ref.shape)
+            x_scr[k * rows : (k + 1) * rows] = (normalize(xs[k][...].astype(F32))[0] * gain_of(gain_ref)).astype(BF16)
+
+    kv_ref[...] = dot(x_scr[...], w_ref[...]).astype(BF16).reshape(kv_ref.shape)
 
 
 def whole(a):
@@ -96,15 +93,12 @@
     feats = w.shape[2]
     return pl.pallas_call(
         functools.partial(project_near_body, n),
-        grid=(3,),
+        grid=(2,),
         in_specs=[whole(b) for b in blocks]
-        + [whole(gain), pl.BlockSpec((pl.squeezed, width, feats), lambda i: (i, 0, 0))]
+        + [whole(gain), pl.BlockSpec((pl.squeezed, width, feats), lambda i: (i + 1, 0, 0))]
         + [pl.BlockSpec(memory_space=pl.ANY)],
-        out_specs=[
-            pl.BlockSpec((n, rows, feats), lambda i: (first // n, 0, jnp.maximum(i - 1, 0))),
-            pl.BlockSpec((n, rows, feats), lambda i: (0, 0, 0)),
-        ],
-        out_shape=[jax.ShapeDtypeStruct(buf.shape, BF16), jax.ShapeDtypeStruct((n, rows, feats), BF16)],
+        out_specs=pl.BlockSpec((n, rows, feats), lambda i: (first // n, 0, i)),
+        out_shape=jax.ShapeDtypeStruct(buf.shape, BF16),
         scratch_shapes=[pltpu.VMEM((n * rows, width), BF16)],
         input_output_aliases={n + 2: 0},
         compiler_params=pltpu.CompilerParams(vmem_limit_bytes=VMEM_LIMIT),
@@ -118,7 +112,7 @@
 
     @pl.when(step == 0)
     def _():
-        x_scr[...] = (normalize(x_ref[...].astype(F32))[0] * gain_ref[...]).astype(BF16)
+        x_scr[...] = (normalize(x_ref[...].astype(F32))[0] * gain_of(gain_ref)).astype(BF16)
 
     @pl.when(step < 2)
     def _():
@@ -161,7 +155,7 @@
         def _():
             x_scr[...] = xs[k][...]
 
-    normed = (normalize(x_scr[...].astype(F32))[0] * gain_ref[...]).astype(BF16)
+    normed = (normalize(x_scr[...].astype(F32))[0] * gain_of(gain_ref)).astype(BF16)
     out_ref[0] = dot(normed, w_ref[...]).astype(BF16)
 
 
@@ -185,21 +179,19 @@
 def lay_out_keys(local_ref, all_scr, kv_scr, i):
     nb = kv_scr.shape[1] // 64
     for n in range(nb):
-        kv_scr[i, n * 64 : (n + 1) * 64, :] = all_scr[local_ref[i * nb + n]]
+        kv_scr[i, n * 64 : (n + 1) * 64, :] = all_scr[local_ref[i, n]]
 
 
 def forward_body(
     local_ref, count_ref, x0_ref, x1_ref, gain_ref, w_ref, kv_ref, q_ref, w_out_ref,
     part_ref, o_ref, lse_ref, p_ref, far_ref,
-    x_scr, n_scr, w_scr, wo_scr, q_scr, all_scr, kv_scr, p_scr, sem, p_sem,
+    n_scr, w_scr, wo_scr, q_scr, all_scr, kv_scr, p_scr, sem, p_sem,
 ):
     tubes, keys, feats2 = kv_scr.shape
     feats = feats2 // 2
     nb = keys // 64
     rows = tubes * 64
     copies = [
-        pltpu.make_async_copy(x0_ref, x_scr.at[:rows], sem.at[0]),
-        pltpu.make_async_copy(x1_ref, x_scr.at[rows:], sem.at[1]),
         pltpu.make_async_copy(w_ref.at[1], w_scr.at[0], sem.at[2]),
         pltpu.make_async_copy(w_ref.at[2], w_scr.at[1], sem.at[3]),
         pltpu.make_async_copy(q_ref, q_scr, sem.at[4]),
@@ -207,19 +199,17 @@
         pltpu.make_async_copy(kv_ref.at[:tubes], all_scr.at[:tubes], sem.at[6]),
         pltpu.make_async_copy(kv_ref.at[6 * tubes :], all_scr.at[tubes : 7 * tubes], sem.at[7]),
     ]
-    for k in (0, 1, 2, 3, 6, 7, 4, 5):
+    for k in (0, 1, 4, 5, 2, 3):
         copies[k].start()
+    for k, x_ref in enumerate((x0_ref, x1_ref)):
+        n_scr[k * rows : (k + 1) * rows] = (normalize(x_ref[...].astype(F32))[0] * gain_of(gain_ref)).astype(BF16)
     for k in range(2):
         copies[k].wait()
-        half = slice(k * rows, (k + 1) * rows)
-        n_scr[half] = (normalize(x_scr[half].astype(F32))[0] * gain_ref[...]).astype(BF16)
-    for k in range(2):
-        copies[2 + k].wait()
         out = dot(n_scr[...], w_scr[k]).astype(BF16).reshape(2 * tubes, 64, feats)
         all_scr[7 * tubes :, :, k * feats : (k + 1) * feats] = out
     far_copy = pltpu.make_async_copy(all_scr.at[7 * tubes :], far_ref, sem.at[8])
     far_copy.start()
-    for k in (6, 7, 4):
+    for k in (4, 5, 2):
         copies[k].wait()
     lane = lax.broadcasted_iota(jnp.int32, (1, keys), 1)
     slot, place = lane // 64, lane % 64
@@ -229,7 +219,7 @@
     def tube(i):
         limit = jnp.zeros((1, keys), jnp.int32)
         for n in range(nb):
-            limit = jnp.where(slot == n, count_ref[local_ref[i * nb + n]], limit)
+            limit = jnp.where(slot == n, count_ref[local_ref[i, n] // tubes, local_ref[i, n] % tubes], limit)
         live = place < limit
         here = slice(i * 64, (i + 1) * 64)
         lay_out_keys(local_ref, all_scr, kv_scr, i)
@@ -254,7 +244,7 @@
 
     for i in range(tubes):
         tube(i)
-    copies[5].wait()
+    copies[3].wait()
     part_ref[...] = dot(o_ref[...].astype(BF16), wo_scr[...]).astype(BF16)
     far_copy.wait()
     for i in range(tubes):
@@ -264,8 +254,7 @@
 def attend_forward(local, counts, x0, x1, gain, w, kv, q, w_out):
     rows, feats = q.shape
     tubes = rows // 64
-    nb = local.shape[0] // tubes
-    keys = nb * 64
+    keys = local.shape[1] * 64
     heads = feats // HEAD_DIM
     width = w_out.shape[1]
     vmem = pl.BlockSpec(memory_space=pltpu.VMEM)
@@ -273,7 +262,7 @@
     hbm = pl.BlockSpec(memory_space=pl.ANY)
     return pl.pallas_call(
         forward_body,
-        in_specs=[smem, smem, hbm, hbm, vmem, hbm, hbm, hbm, hbm],
+        in_specs=[smem, smem, vmem, vmem, vmem, hbm, hbm, hbm, hbm],
         out_specs=[vmem, vmem, vmem, hbm, hbm],
         out_shape=[
             jax.ShapeDtypeStruct((rows, width), BF16),
@@ -283,7 +272,6 @@
             jax.ShapeDtypeStruct((2 * tubes, 64, 2 * feats), BF16),
         ],
         scratch_shapes=[
-            pltpu.VMEM((2 * rows, width), BF16),
             pltpu.VMEM((2 * rows, width), BF16),
             pltpu.VMEM((2, width, feats), BF16),
             pltpu.VMEM((feats, width), BF16),
@@ -310,14 +298,13 @@
 
 
 def middle_body(
-    count_ref, sec_ref, mine_hbm, other_hbm, video_hbm, target_hbm, w_out_hbm, o_hbm, lse_ref, pay_ref, g_ref,
-    mine_ref, other_ref, video_ref, target_ref, w_out_ref, o_ref, sem,
+    count_ref, sec_ref, mine_hbm, other_ref, video_hbm, target_hbm, w_out_hbm, o_hbm, lse_ref, pay_ref, g_ref,
+    mine_ref, video_ref, target_ref, w_out_ref, o_ref, sem,
 ):
     rows, width = video_ref.shape
     feats = w_out_ref.shape[0]
     pairs = [
         (mine_hbm, mine_ref),
-        (other_hbm, other_ref),
         (video_hbm, video_ref),
         (target_hbm, target_ref),
         (w_out_hbm, w_out_ref),
@@ -333,15 +320,15 @@
     for i in range(tubes):
         limit = jnp.where(row // 64 == i, count_ref[i], limit)
     valid = row % 64 < limit
-    for c in copies[:4]:
+    for c in copies[:3]:
         c.wait()
     mixed = mine_ref[...].astype(F32) + other_ref[...].astype(F32)
     g = jnp.where(valid, 2.0 * (video_ref[...].astype(F32) + mixed - target_ref[...].astype(F32)), 0.0)
     half = width // 2
     g_ref[...] = jnp.where(sec_ref[0] == 0, g[:, :half], g[:, half:])
+    copies[3].wait()
+    d_att = dot_nt(g.astype(BF16), w_out_ref[...]).astype(BF16)
     copies[4].wait()
-    d_att = dot_nt(g.astype(BF16), w_out_ref[...]).astype(BF16)
-    copies[5].wait()
     pay_ref[:rows] = d_att
     prod = d_att.astype(F32) * o_ref[...]
     head = lax.broadcasted_iota(jnp.int32, (heads, feats), 0)
@@ -372,14 +359,14 @@
     smem = pl.BlockSpec(memory_space=pltpu.SMEM)
     return pl.pallas_call(
         middle_body,
-        in_specs=[smem, smem] + [pl.BlockSpec(memory_space=pl.ANY)] * 6 + [vmem],
+        in_specs=[smem, smem] + [pl.BlockSpec(memory_space=pl.ANY), vmem] + [pl.BlockSpec(memory_space=pl.ANY)] * 4 + [vmem],
         out_specs=[vmem, vmem],
         out_shape=[
             jax.ShapeDtypeStruct((rows + STAT_ROWS, feats), BF16),
             jax.ShapeDtypeStruct((rows, width // 2), F32),
         ],
-        scratch_shapes=[pltpu.VMEM((rows, width), BF16)] * 4
-        + [pltpu.VMEM((feats, width), BF16), pltpu.VMEM((rows, feats), F32), pltpu.SemaphoreType.DMA((6,))],
+        scratch_shapes=[pltpu.VMEM((rows, width), BF16)] * 3
+        + [pltpu.VMEM((feats, width), BF16), pltpu.VMEM((rows, feats), F32), pltpu.SemaphoreType.DMA((5,))],
         compiler_params=pltpu.CompilerParams(vmem_limit_bytes=VMEM_LIMIT),
         cost_estimate=SMALL,
         name="middle",
@@ -387,12 +374,12 @@
 
 
 def key_pass(
-    list_ref, n_ref, count_ref, q_scr, kv_scr, pay_scr, lse_scr, inner_scr, qc_scr, dc_scr, km_scr, vm_scr, dk_scr, dv_scr, grad_scr
+    list_ref, count_ref, q_scr, kv_scr, pay_scr, lse_scr, inner_scr, qc_scr, dc_scr, km_scr, vm_scr, dk_scr, dv_scr, grad_scr
 ):
     tubes = kv_scr.shape[0]
     size = qc_scr.shape[0] // 64
     feats = q_scr.shape[2]
-    most = list_ref.shape[0] // tubes
+    most = list_ref.shape[1] - 1
     low = lax.broadcasted_iota(jnp.int32, (8, 128), 1) < 64
     key_row = lax.broadcasted_iota(jnp.int32, (64, 1), 0)
 
@@ -411,11 +398,11 @@
             lses, inners = [], []
             for t in range(size):
                 place = c * size + t
-                i = list_ref[j * most + jnp.minimum(place, most - 1)]
+                i = list_ref[j, jnp.minimum(place, most - 1)]
                 slot, w = i // tubes, i % tubes
                 qc_scr[t * 64 : (t + 1) * 64, :] = q_scr[i]
                 dc_scr[t * 64 : (t + 1) * 64, :] = pay_scr[slot, pl.ds(pl.multiple_of(w * 64, 64), 64), :]
-                lses.append(jnp.where(place < n_ref[j], lse_scr[i], 1e30))
+                lses.append(jnp.where(place < list_ref[j, most], lse_scr[i], 1e30))
                 inners.append(inner_scr[i])
             lse = jnp.concatenate([jnp.where(low, lses[t], lses[t + 1]) for t in range(0, size, 2)], axis=1)
             inner = jnp.concatenate([jnp.where(low, inners[t], inners[t + 1]) for t in range(0, size, 2)], axis=1)
@@ -437,7 +424,7 @@
                 dv_scr[these, :wd] += dot(jnp.concatenate(p, axis=0), dc)
             return carry
 
-        lax.fori_loop(0, (n_ref[j] + size - 1) // size, chunk, carry)
+        lax.fori_loop(0, (list_ref[j, most] + size - 1) // size, chunk, carry)
         for group in GROUPS:
             h0, nh, l0, wd = group
             these = slice(h0 * 64, (h0 + nh) * 64)
@@ -512,7 +499,7 @@
     )(local, pay, kv, far, p)
 
 
-def key_near_body(n, list_ref, n_ref, count_ref, own_q_ref, q_ref, kv_ref, w_ref, dq_ref, *rest):
+def key_near_body(n, list_ref, count_ref, own_q_ref, q_ref, kv_ref, w_ref, dq_ref, *rest):
     pays = rest[:n]
     grad_ref, base_ref, w_scr, dq_scr, q_scr, kv_scr, pay_scr, *scr, sem = rest[n:]
     lse_scr, inner_scr = scr[:2]
@@ -539,7 +526,7 @@
         stats_of(pay_scr, k, rows, tubes, lse_scr, inner_scr)
     for c in copies:
         c.wait()
-    key_pass(list_ref, n_ref, count_ref, q_scr, kv_scr, pay_scr, *scr, grad_ref)
+    key_pass(list_ref, count_ref, q_scr, kv_scr, pay_scr, *scr, grad_ref)
 
 
 def key_scratch(n, tubes, feats, size):
@@ -560,7 +547,7 @@
     ]
 
 
-def key_near(lists, lengths, counts, own_q, q, kv, w, dq, pays):
+def key_near(lists, counts, own_q, q, kv, w, dq, pays):
     rows, feats = dq.shape
     width = w.shape[1]
     tubes = rows // 64
@@ -570,7 +557,7 @@
     hbm = pl.BlockSpec(memory_space=pl.ANY)
     return pl.pallas_call(
         functools.partial(key_near_body, n),
-        in_specs=[smem] * 3 + [hbm] * (5 + n),
+        in_specs=[smem] * 2 + [hbm] * 5 + [vmem] * n,
         out_specs=[vmem, vmem],
         out_shape=[
             jax.ShapeDtypeStruct((rows, 2 * feats), F32),
@@ -582,10 +569,10 @@
         compiler_params=pltpu.CompilerParams(vmem_limit_bytes=VMEM_LIMIT),
         cost_estimate=SMALL,
         name="key_near",
-    )(lists, lengths, counts, own_q, q, kv, w, dq, *pays)
-
-
-def key_last_body(n, first, list_ref, n_ref, count_ref, sec_ref, q_ref, kv_ref, w_ref, acc_ref, *rest):
+    )(lists, counts, own_q, q, kv, w, dq, *pays)
+
+
+def key_last_body(n, first, list_ref, count_ref, sec_ref, q_ref, kv_ref, w_ref, acc_ref, *rest):
     pays = rest[:n]
     video_ref, gain_ref, base_ref, g_ref, send_ref, keep_ref = rest[n : n + 6]
     q_scr, kv_scr, pay_scr, *scr, w_scr, grad_scr, x_scr, base_scr, g_scr, sem = rest[n + 6 :]
@@ -609,7 +596,7 @@
     q_copy.wait()
     kv_copy.wait()
     acc_copy.wait()
-    key_pass(list_ref, n_ref, count_ref, q_scr, kv_scr, pay_scr, *scr, grad_scr)
+    key_pass(list_ref, count_ref, q_scr, kv_scr, pay_scr, *scr, grad_scr)
     d_proj = grad_scr[...].astype(BF16)
     x_copy.wait()
     xhat, inverse = normalize(x_scr[...].astype(F32))
@@ -617,7 +604,7 @@
     base_copy.wait()
     g_copy.wait()
     d_normed = base_scr[...] + dot_nt(d_proj[:, :feats], w_scr[0]) + dot_nt(d_proj[:, feats:], w_scr[1])
-    scaled = d_normed * gain_ref[...]
+    scaled = d_normed * gain_of(gain_ref)
     out = (
         scaled
         - jnp.mean(scaled, axis=-1, keepdims=True)
@@ -629,7 +616,7 @@
     keep_ref[...] = jnp.where(lower, out[:, :half], out[:, half:]) + g_scr[...]
 
 
-def key_last(first, lists, lengths, counts, sec, q, kv, w, acc, pays, video, gain, base, g):
+def key_last(first, lists, counts, sec, q, kv, w, acc, pays, video, gain, base, g):
     rows, width = video.shape
     feats = q.shape[2]
     tubes = rows // 64
@@ -639,7 +626,7 @@
     hbm = pl.BlockSpec(memory_space=pl.ANY)
     return pl.pallas_call(
         functools.partial(key_last_body, n, first),
-        in_specs=[smem] * 4 + [hbm] * (5 + n) + [vmem] + [hbm] * 2,
+        in_specs=[smem] * 3 + [hbm] * 4 + [vmem] * n + [hbm] + [vmem] + [hbm] * 2,
         out_specs=[vmem, vmem],
         out_shape=[
             jax.ShapeDtypeStruct((rows, width // 2), BF16),
@@ -657,7 +644,7 @@
         compiler_params=pltpu.CompilerParams(vmem_limit_bytes=VMEM_LIMIT),
         cost_estimate=SMALL,
         name="key_last",
-    )(lists, lengths, counts, sec, q, kv, w, acc, *pays, video, gain, base, g)
+    )(lists, counts, sec, q, kv, w, acc, *pays, video, gain, base, g)
 
 
 def per_device(video, target, gain, w_qkv, w_out, neighbours, counts):
@@ -687,27 +674,27 @@
 
     video = video.reshape(rows, width)
     target = target.reshape(rows, width)
-    gain = gain.reshape(1, width)
     w = jnp.transpose(w_qkv, (1, 0, 2))
 
     off, mate, pair, other = from_off(video), from_mate(video), from_pair(video), from_other(video)
     meta = jnp.concatenate(
-        [neighbours.reshape(tw, nb) + 1, counts.reshape(tw, 1), jnp.zeros((tw, 16 - nb - 1), jnp.int32)], axis=1
+        [neighbours.reshape(tw, nb) + 1, jnp.pad(counts.reshape(1, tw), ((0, 0), (0, nb - tw)))], axis=0
     )
     own_video, meta, _ = lax.optimization_barrier((video, meta, mate))
     kv, own_q = project_own(own_video, gain, w)
+    pair, other, kv = lax.optimization_barrier((pair, other, kv))
     three = jnp.stack([meta, from_pair(meta), from_other(meta)])
     off_meta, mate_meta = from_off(three), from_mate(three)
     off, off_meta, mate_meta, kv = lax.optimization_barrier((off, off_meta, mate_meta, kv))
     corners = from_pair(off), from_other(off)
     mates = mate, from_mate(pair), from_mate(other)
-    kv, near_q = project_near((pair, other, off, *mates), 6, gain, w, kv)
+    rest = (pair, other, off, *mates)
+    kv = project_near((pair, other, off, *mates), 6, gain, w, kv)
     kv = kv.reshape(BLOCKS * tw, tube, 2 * feats)
 
-    meta = jnp.concatenate([three, off_meta[:1], mate_meta, off_meta[1:]]).reshape(9 * tw, 16)
-    listed = meta[:, :nb] - 1
-    count_q = meta[:, nb].reshape(9, tw)
-    count_all = count_q.reshape(9 * tw)
+    meta = jnp.concatenate([three, off_meta[:1], mate_meta, off_meta[1:]])
+    listed = (meta[:, :tw] - 1).reshape(9 * tw, nb)
+    count_all = meta[:, tw, :tw]
 
     ids = neighbours.reshape(tw, nb)
     t_of, h_of, w_of = ids // (n_h * tw), ids // tw % n_h, ids % tw
@@ -717,7 +704,7 @@
         step,
         jnp.where(h_of == h_here + 1 - 2 * (h_here % 2), 4 + step, jnp.where(step == 0, 3, 6 + step)),
     )
-    local = (slot * tw + w_of).reshape(tw * nb)
+    local = slot * tw + w_of
     own_ids = (t_here * n_h + h_here) * tw + jnp.arange(tw, dtype=jnp.int32)
     names = jnp.any(listed[None] == own_ids[:, None, None], axis=2)
 
@@ -726,21 +713,19 @@
         where = jnp.arange(last - first, dtype=jnp.int32)
         rank = jnp.sum(named[:, None, :] & (where[None, :] < where[:, None])[None], axis=2)
         hit = named[:, None, :] & (rank[:, None, :] == jnp.arange(most)[None, :, None])
-        places = jnp.sum(jnp.where(hit, where, 0), axis=2).astype(jnp.int32).reshape(tw * most)
-        return places, jnp.sum(named, axis=1).astype(jnp.int32)
-
-    near_list, near_n = listing(0, 7 * tw, 24)
-    last_list, last_n = listing(7 * tw, 9 * tw, 8)
+        places = jnp.sum(jnp.where(hit, where, 0), axis=2).astype(jnp.int32)
+        return jnp.concatenate([places, jnp.sum(named, axis=1, keepdims=True).astype(jnp.int32)], axis=1)
+
+    near_list = listing(0, 7 * tw, 24)
+    last_list = listing(7 * tw, 9 * tw, 8)
     sec = sec.reshape(1).astype(jnp.int32)
     own_counts = counts.reshape(tw)
 
     part, o, lse, p, far = attend_forward(local, count_all, *corners, gain, w, kv, own_q, w_out)
     other = lax.ppermute(part, "section", swap)
-    part, videos = lax.optimization_barrier((part, corners))
-    far_q = project_queries(videos, gain, w).reshape(2 * tw, tube, feats)
-    other, far_q, near_list, near_n, last_list, last_n = lax.optimization_barrier(
-        (other, far_q, near_list, near_n, last_list, last_n)
-    )
+    part, videos = lax.optimization_barrier((part, (*rest, *corners)))
+    far_q = project_queries(videos, gain, w).reshape(8 * tw, tube, feats)
+    other, far_q, near_list, last_list = lax.optimization_barrier((other, far_q, near_list, last_list))
     pay, g = middle(own_counts, sec, part, other, video, target, w_out, o, lse)
     off, mate = from_off(pay), from_mate(pay)
     pair, after = from_pair(pay), from_other(pay)
@@ -748,9 +733,9 @@
     dq, off = lax.optimization_barrier((dq, off))
     near, mates, corners = (pay, pair, after, off), (mate, from_mate(pair), from_mate(after)), (from_pair(off), from_other(off))
     acc, base = key_near(
-        near_list, near_n, own_counts, own_q.reshape(tw, tube, feats), near_q.reshape(6 * tw, tube, feats), kv, w, dq, [*near, *mates]
+        near_list, own_counts, own_q.reshape(tw, tube, feats), far_q, kv, w, dq, [*near, *mates]
     )
-    send, keep = key_last(0, last_list, last_n, own_counts, sec, far_q, kv, w, acc, corners, video, gain, base, g)
+    send, keep = key_last(6, last_list, own_counts, sec, far_q, kv, w, acc, corners, video, gain, base, g)
     got = lax.ppermute(send, "section", swap)
     return (keep + got.astype(F32)).astype(BF16).reshape(tt, th, tw, tube, width // 2)
 

time: 156 us -> 143 us (0.917)
  local copies, waits for them, and re-layouts: 9.79 us -> 5.09 us
  waiting for transfers between devices: 29.4 us -> 25.1 us
  starting transfers between devices: 29.7 us -> 27.6 us
  other arithmetic: 5.69 us -> 3.75 us
    pallas_call x1, Pallas kernels: 4.62 us -> 11.8 us  [project_queries(): pl.pallas_call(functools.partial(project_queries_body, n), grid=(n,), in_...]
    ppermute x1, waiting for transfers between devices: 9.01 us -> 3.3 us  [per_device(): other = lax.ppermute(part, 'section', swap)]
    reshape x6 -> x0, local copies, waits for them, and re-layouts: 4.14 us -> none  [the longest x2 1.33 us: listing(): jnp.sum(jnp.where(hit, where, 0), axis=2).astype(jnp.int32)]
    pallas_call x3, Pallas kernels: 42 us -> 38.6 us  [the longest x1 14.9 us: key_near(): pl.pallas_call(functools.partial(key_near_body, n), in_specs=[smem] * 2 +...]
    pallas_call x1, Pallas kernels: 12.1 us -> 9.49 us  [key_last(): pl.pallas_call(functools.partial(key_last_body, n, first), in_specs=[smem...]
    unnamed x36 -> x31, local copies, waits for them, and re-layouts: 4.68 us -> 4.45 us
  transfers between devices with their start and end apart: 22 -> 22, of which waited for: 7 -> 8; matrix products, arithmetic and copies ran while one was open for 6% -> 3% of each run, Pallas kernels for 32% -> 38%
where the time goes in v3:
time: 143 us; the launch traced here: 141 us
  Pallas kernels  79.2 us (55%)
  starting transfers between devices  27.6 us (19%)
  waiting for transfers between devices  25.1 us (18%)
  local copies, waits for them, and re-layouts  5.09 us (4%)
  other arithmetic  3.75 us (3%)
    pallas_call x1, Pallas kernels, key_near(): pl.pallas_call(functools.partial(key_near_body, n), in_specs=[smem] * 2 +...  14.9 us
    ppermute x5, starting transfers between devices, from_other(): return lax.ppermute(x, 'tm', other_times)  13.3 us
    pallas_call x1, Pallas kernels, project_near(): pl.pallas_call(functools.partial(project_near_body, n), grid=(2,), in_spe...  12.3 us
    pallas_call x1, Pallas kernels, project_queries(): pl.pallas_call(functools.partial(project_queries_body, n), grid=(n,), in_...  11.8 us
    pallas_call x1, Pallas kernels, attend_forward(): pl.pallas_call(forward_body, in_specs=[smem, smem, vmem, vmem, vmem, hbm,...  11.4 us
    ppermute x1, waiting for transfers between devices, per_device(): got = lax.ppermute(send, 'section', swap)  10.2 us
    pallas_call x1, Pallas kernels, key_last(): pl.pallas_call(functools.partial(key_last_body, n, first), in_specs=[smem...  9.49 us
    pallas_call x1, Pallas kernels, query_grad(): pl.pallas_call(query_body, in_specs=[smem] + [hbm] * 4, out_specs=vmem, o...  8.46 us
  transfers between devices with their start and end apart: 22, of which 8 were waited for; matrix products, arithmetic and copies ran while one was open for 3% of the time, Pallas kernels for 38%

profile of v3, /device:TPU:54, one launch (start us, length us, event | category | flops | bytes accessed | tf_op | source)
XLA Modules:
  0.0 141.1 jit_solution(12530176763112715922)
XLA Ops:
  1.3 1.9 %collective-permute-start.7 = (bf16[256,1280]{1,0:T(8,128)(2,1)}, bf16[256,1280]{1,0:T(8,128)(2,1)S(1)}, u32[]{:S(2)}, u32[]{:S(2)}) collective-permute-start(bf16[256,1280]{1,0:T(8,128)(2,1)} %bitcast.37), channel_id=1, source_target_pairs={{32,64},{64,32},{33,65},{65,33},{34,66},{66,34},{35,67},{67,35},{3... | collective-permute-start | bytes 1966088 | tf_op jit(solution)/shard_map/ppermute | solution.py:667
  3.2 3.1 %collective-permute-start.3 = (bf16[256,1280]{1,0:T(8,128)(2,1)}, bf16[256,1280]{1,0:T(8,128)(2,1)S(1)}, u32[]{:S(2)}, u32[]{:S(2)}) collective-permute-start(bf16[256,1280]{1,0:T(8,128)(2,1)} %bitcast.38), channel_id=1, source_target_pairs={{2,4},{4,2},{6,8},{8,6},{10,12},{12,10},{14,16},{16,14},{18,20},{2... | collective-permute-start | bytes 1966088 | tf_op jit(solution)/shard_map/ppermute | solution.py:670
  7.9 3.6 %collective-permute-start.2 = (s32[5,8]{1,0:T(8,128)S(1)}, s32[5,8]{1,0:T(8,128)S(1)}, u32[]{:S(2)}, u32[]{:S(2)}) collective-permute-start(s32[5,8]{1,0:T(8,128)S(1)} %pad_add_fusion.1), channel_id=1, source_target_pairs={{32,64},{64,32},{33,65},{65,33},{34,66},{66,34},{35,67},{67,35},{3... | collective-permute-start | bytes 488 | tf_op jit(solution)/shard_map/ppermute | solution.py:667
  13.4 5.5 %project_own.1 = (bf16[12,256,1280]{2,1,0:T(8,128)(2,1)}, bf16[256,640]{1,0:T(8,128)(2,1)S(1)}) custom-call(bf16[256,1280]{1,0:T(8,128)(2,1)S(1)} %bitcast.41, f32[1280]{0:T(1024)S(1)} %copy-done.4, bf16[3,1280,640]{2,1,0:T(8,128)(2,1)} %bitcast.51), custom_call_target="tpu_custom_call" | custom-call | flops 1 | bytes 1 | tf_op jit(solution)/shard_map/project_own/pallas_call | solution.py:129
  18.9 1.4 collective-permute-done.7.refs_1_
  20.8 2.9 %collective-permute-start.4 = (s32[3,5,8]{2,1,0:T(8,128)S(1)}, s32[3,5,8]{2,1,0:T(8,128)S(1)}, u32[]{:S(2)}, u32[]{:S(2)}) collective-permute-start(s32[3,5,8]{2,1,0:T(8,128)S(1)} %pad_add_fusion), channel_id=1, source_target_pairs={{2,4},{4,2},{6,8},{8,6},{10,12},{12,10},{14,16},{16,14},{18,20},{2... | collective-permute-start | bytes 1448 | tf_op jit(solution)/shard_map/ppermute | solution.py:670
  23.8 1.9 %collective-permute-start.5 = (s32[3,5,8]{2,1,0:T(8,128)S(1)}, s32[3,5,8]{2,1,0:T(8,128)S(1)}, u32[]{:S(2)}, u32[]{:S(2)}) collective-permute-start(s32[3,5,8]{2,1,0:T(8,128)S(1)} %pad_add_fusion), channel_id=1, source_target_pairs={{0,2},{2,0},{4,6},{6,4},{8,10},{10,8},{12,14},{14,12},{16,18},{18,... | collective-permute-start | bytes 1448 | tf_op jit(solution)/shard_map/ppermute | solution.py:673
  25.7 1.7 %collective-permute-done.4 = s32[3,5,8]{2,1,0:T(8,128)S(1)} collective-permute-done((s32[3,5,8]{2,1,0:T(8,128)S(1)}, s32[3,5,8]{2,1,0:T(8,128)S(1)}, u32[]{:S(2)}, u32[]{:S(2)}) %collective-permute-start.4) | collective-permute-done | bytes 512 | tf_op jit(solution)/shard_map/ppermute | solution.py:670
  27.4 2.5 %collective-permute-start.9 = (bf16[256,1280]{1,0:T(8,128)(2,1)S(1)}, bf16[256,1280]{1,0:T(8,128)(2,1)}, u32[]{:S(2)}, u32[]{:S(2)}) collective-permute-start(bf16[256,1280]{1,0:T(8,128)(2,1)S(1)} %collective-permute-done.3.refs_2_), channel_id=1, source_target_pairs={{32,64},{64,32},{33,65},{65,33},{34,66},{66,34},{35,67},{67,35},{3... | collective-permute-start | bytes 1966088 | tf_op jit(solution)/shard_map/ppermute | solution.py:667
  32.2 12.3 %project_near.1 = bf16[12,256,1280]{2,1,0:T(8,128)(2,1)} custom-call(bf16[256,1280]{1,0:T(8,128)(2,1)S(1)} %collective-permute-done.6.refs_0_, bf16[256,1280]{1,0:T(8,128)(2,1)S(1)} %collective-permute-done.7.refs_1_, bf16[256,1280]{1,0:T(8,128)(2,1)S(1)} %collective-permute-done.3.refs_2_, ...), custom_call_target="tpu_custom_call", output_to_operand_aliasing={{}: (8, {})} | custom-call | flops 1 | bytes 1 | tf_op jit(solution)/shard_map/project_near/pallas_call | solution.py:94
  44.8 1.9 %collective-permute-done.9.x1_ref.refs_7_ = bf16[256,1280]{1,0:T(8,128)(2,1)} collective-permute-done((bf16[256,1280]{1,0:T(8,128)(2,1)S(1)}, bf16[256,1280]{1,0:T(8,128)(2,1)}, u32[]{:S(2)}, u32[]{:S(2)}) %collective-permute-start.9) | collective-permute-done | bytes 655392 | tf_op jit(solution)/shard_map/ppermute | solution.py:667
  46.7 11.4 %attend_forward.1 = (bf16[256,1280]{1,0:T(8,128)(2,1)S(1)}, f32[256,640]{1,0:T(8,128)S(1)}, f32[4,8,128]{2,1,0:T(8,128)S(1)}, bf16[4,512,512]{2,1,0:T(8,128)(2,1)}, bf16[8,64,1280]{2,1,0:T(8,128)(2,1)}) custom-call(s32[4,8]{1,0:T(4,128)S(1)} %get-tuple-element.80.local_ref, s32[9,4]{1,0:T(8,128)S(1)} %copy.18.count_ref, ...), custom_call_target="tpu_custom_call" | custom-call | flops 1 | bytes 1 | tf_op jit(solution)/shard_map/attend_forward/pallas_call | solution.py:263
  60.8 11.8 %project_queries.1 = bf16[8,256,640]{2,1,0:T(8,128)(2,1)} custom-call(bf16[256,1280]{1,0:T(8,128)(2,1)S(1)} %collective-permute-done.6.refs_0_, bf16[256,1280]{1,0:T(8,128)(2,1)S(1)} %collective-permute-done.7.refs_1_, bf16[256,1280]{1,0:T(8,128)(2,1)S(1)} %collective-permute-done.3.refs_2_, bf16[256,1280]{1,0:T(8,128)(2,1)} %copy-done.7, ...), custom_call_target="tpu_custom_call" | custom-call | flops 1 | bytes 1 | tf_op jit(solution)/shard_map/project_queries/pallas_call | solution.py:166
  72.5 3.3 %collective-permute-done.12.other_ref = bf16[256,1280]{1,0:T(8,128)(2,1)} collective-permute-done((bf16[256,1280]{1,0:T(8,128)(2,1)S(1)}, bf16[256,1280]{1,0:T(8,128)(2,1)}, u32[]{:S(2)}, u32[]{:S(2)}) %collective-permute-start.12) | collective-permute-done | bytes 655392 | tf_op jit(solution)/shard_map/ppermute | solution.py:725
  75.8 5.4 %middle.1 = (bf16[288,640]{1,0:T(8,128)(2,1)S(1)}, f32[256,640]{1,0:T(8,128)S(1)}) custom-call(s32[4]{0:T(128)S(1)} %bitcast.44, s32[1]{0:T(128)} %bitcast.13.sec_ref, bf16[256,1280]{1,0:T(8,128)(2,1)S(1)} %get-tuple-element.65.mine_hbm, bf16[256,1280]{1,0:T(8,128)(2,1)} %collective-permute-done.12.other_ref, bf16[256,1280]{1,0:T(8,128)(2,1)} %bitcast.39, ...), custom_call_target="tpu_custom_call" | custom-call | flops 1 | bytes 1 | tf_op jit(solution)/shard_map/middle/pallas_call | solution.py:360
  81.3 2.7 %collective-permute-start.15 = (bf16[288,640]{1,0:T(8,128)(2,1)S(1)}, bf16[288,640]{1,0:T(8,128)(2,1)S(1)}, u32[]{:S(2)}, u32[]{:S(2)}) collective-permute-start(bf16[288,640]{1,0:T(8,128)(2,1)S(1)} %get-tuple-element.69.pay_ref.rest_0_), channel_id=1, source_target_pairs={{32,64},{64,32},{33,65},{65,33},{34,66},{66,34},{35,67},{67,35},{3... | collective-permute-start | bytes 1105928 | tf_op jit(solution)/shard_map/ppermute | solution.py:667
  84.1 1.9 %collective-permute-start.13 = (bf16[288,640]{1,0:T(8,128)(2,1)S(1)}, bf16[288,640]{1,0:T(8,128)(2,1)S(1)}, u32[]{:S(2)}, u32[]{:S(2)}) collective-permute-start(bf16[288,640]{1,0:T(8,128)(2,1)S(1)} %get-tuple-element.69.pay_ref.rest_0_), channel_id=1, source_target_pairs={{2,4},{4,2},{6,8},{8,6},{10,12},{12,10},{14,16},{16,14},{18,20},{2... | collective-permute-start | bytes 1105928 | tf_op jit(solution)/shard_map/ppermute | solution.py:670
  86.9 4.2 %collective-permute-done.14.rest_1_ = bf16[288,640]{1,0:T(8,128)(2,1)S(1)} collective-permute-done((bf16[288,640]{1,0:T(8,128)(2,1)S(1)}, bf16[288,640]{1,0:T(8,128)(2,1)S(1)}, u32[]{:S(2)}, u32[]{:S(2)}) %collective-permute-start.14) | collective-permute-done | bytes 368672 | tf_op jit(solution)/shard_map/ppermute | solution.py:664
  91.1 2.1 %collective-permute-done.15.rest_2_ = bf16[288,640]{1,0:T(8,128)(2,1)S(1)} collective-permute-done((bf16[288,640]{1,0:T(8,128)(2,1)S(1)}, bf16[288,640]{1,0:T(8,128)(2,1)S(1)}, u32[]{:S(2)}, u32[]{:S(2)}) %collective-permute-start.15) | collective-permute-done | bytes 368672 | tf_op jit(solution)/shard_map/ppermute | solution.py:667
  93.2 8.5 %query_grad.1.dq_ref = bf16[256,640]{1,0:T(8,128)(2,1)S(1)} custom-call(s32[4,8]{1,0:T(4,128)S(1)} %get-tuple-element.80.local_ref, bf16[288,640]{1,0:T(8,128)(2,1)S(1)} %get-tuple-element.69.pay_ref.rest_0_, bf16[48,64,1280]{2,1,0:T(8,128)(2,1)} %bitcast.48, bf16[8,64,1280]{2,1,0:T(8,128)(2,1)S(1)} %copy-done.1, bf16[4,512,512]{2,1,0:T(8,128)(2,1)} %get-tuple-element.71.p_ref), custom_call_target="tpu_custom_call" | custom-call | flops 1 | bytes 1 | tf_op jit(solution)/shard_map/query_grad/pallas_call | solution.py:482
  101.8 2.6 %collective-permute-start.20 = (bf16[288,640]{1,0:T(8,128)(2,1)S(1)}, bf16[288,640]{1,0:T(8,128)(2,1)S(1)}, u32[]{:S(2)}, u32[]{:S(2)}) collective-permute-start(bf16[288,640]{1,0:T(8,128)(2,1)S(1)} %collective-permute-done.13.rest_3_), channel_id=1, source_target_pairs={{32,64},{64,32},{33,65},{65,33},{34,66},{66,34},{35,67},{67,35},{3... | collective-permute-start | bytes 1105928 | tf_op jit(solution)/shard_map/ppermute | solution.py:667
  105.3 14.9 %key_near.1 = (f32[256,1280]{1,0:T(8,128)}, f32[256,1280]{1,0:T(8,128)}) custom-call(s32[4,25]{1,0:T(4,128)S(1)} %pad_add_fusion.2.list_ref, s32[4]{0:T(128)S(1)} %bitcast.45, bf16[4,64,640]{2,1,0:T(8,128)(2,1)S(1)} %bitcast.42, bf16[32,64,640]{2,1,0:T(8,128)(2,1)} %bitcast.57, bf16[48,64,1280]{2,1,0:T(8,128)(2,1)} %bitcast.49, ...), custom_call_target="tpu_custom_call" | custom-call | flops 1 | bytes 1 | tf_op jit(solution)/shard_map/key_near/pallas_call | solution.py:558
  120.2 9.5 %key_last.1 = (bf16[256,640]{1,0:T(8,128)(2,1)S(1)}, f32[256,640]{1,0:T(8,128)S(1)}) custom-call(s32[4,9]{1,0:T(4,128)S(1)} %pad_add_fusion.3.list_ref, s32[4]{0:T(128)S(1)} %bitcast.46, s32[1]{0:T(128)} %bitcast.13.sec_ref, bf16[32,64,640]{2,1,0:T(8,128)(2,1)} %bitcast.58, bf16[48,64,1280]{2,1,0:T(8,128)(2,1)} %bitcast.50, bf16[3,1280,640]{2,1,0:T(8,128)(2,1)} %bitcast.56, ...), custom_call_target="tpu_custom_call" | custom-call | flops 1 | bytes 1 | tf_op jit(solution)/shard_map/key_last/pallas_call | solution.py:627
  130.1 10.2 %collective-permute-done.21 = bf16[256,640]{1,0:T(8,128)(2,1)S(1)} collective-permute-done((bf16[256,640]{1,0:T(8,128)(2,1)S(1)}, bf16[256,640]{1,0:T(8,128)(2,1)S(1)}, u32[]{:S(2)}, u32[]{:S(2)}) %collective-permute-start.21) | collective-permute-done | bytes 327712 | tf_op jit(solution)/shard_map/ppermute | solution.py:739
  (86 shorter events, 13.5 us)
Async XLA Ops:
  0.0 7.8 %collective-permute-start = (bf16[256,1280]{1,0:T(8,128)(2,1)}, bf16[256,1280]{1,0:T(8,128)(2,1)S(1)}, u32[]{:S(2)}, u32[]{:S(2)}) collective-permute-start(bf16[256,1280]{1,0:T(8,128)(2,1)} %bitcast.35), channel_id=1, source_target_pairs={{0,2},{2,0},{4,6},{6,4},{8,10},{10,8},{12,14},{14,12},{16,18},{18,... | collective-permute-start | bytes 1966088 | tf_op jit(solution)/shard_map/ppermute | solution.py:673
  0.0 18.9 %collective-permute-start.6 = (bf16[256,1280]{1,0:T(8,128)(2,1)}, bf16[256,1280]{1,0:T(8,128)(2,1)S(1)}, u32[]{:S(2)}, u32[]{:S(2)}) collective-permute-start(bf16[256,1280]{1,0:T(8,128)(2,1)} %bitcast.36), channel_id=1, source_target_pairs={{0,32},{32,0},{64,96},{96,64},{1,33},{33,1},{65,97},{97,65},{2,34}... | collective-permute-start | bytes 1966088 | tf_op jit(solution)/shard_map/ppermute | solution.py:664
  1.3 19.0 %collective-permute-start.7 = (bf16[256,1280]{1,0:T(8,128)(2,1)}, bf16[256,1280]{1,0:T(8,128)(2,1)S(1)}, u32[]{:S(2)}, u32[]{:S(2)}) collective-permute-start(bf16[256,1280]{1,0:T(8,128)(2,1)} %bitcast.37), channel_id=1, source_target_pairs={{32,64},{64,32},{33,65},{65,33},{34,66},{66,34},{35,67},{67,35},{3... | collective-permute-start | bytes 1966088 | tf_op jit(solution)/shard_map/ppermute | solution.py:667
  3.2 22.5 %collective-permute-start.3 = (bf16[256,1280]{1,0:T(8,128)(2,1)}, bf16[256,1280]{1,0:T(8,128)(2,1)S(1)}, u32[]{:S(2)}, u32[]{:S(2)}) collective-permute-start(bf16[256,1280]{1,0:T(8,128)(2,1)} %bitcast.38), channel_id=1, source_target_pairs={{2,4},{4,2},{6,8},{8,6},{10,12},{12,10},{14,16},{16,14},{18,20},{2... | collective-permute-start | bytes 1966088 | tf_op jit(solution)/shard_map/ppermute | solution.py:670
  7.8 13.0 %collective-permute-start.1 = (s32[5,8]{1,0:T(8,128)S(1)}, s32[5,8]{1,0:T(8,128)S(1)}, u32[]{:S(2)}, u32[]{:S(2)}) collective-permute-start(s32[5,8]{1,0:T(8,128)S(1)} %pad_add_fusion.1), channel_id=1, source_target_pairs={{0,32},{32,0},{64,96},{96,64},{1,33},{33,1},{65,97},{97,65},{2,34}... | collective-permute-start | bytes 488 | tf_op jit(solution)/shard_map/ppermute | solution.py:664
  7.9 12.9 %collective-permute-start.2 = (s32[5,8]{1,0:T(8,128)S(1)}, s32[5,8]{1,0:T(8,128)S(1)}, u32[]{:S(2)}, u32[]{:S(2)}) collective-permute-start(s32[5,8]{1,0:T(8,128)S(1)} %pad_add_fusion.1), channel_id=1, source_target_pairs={{32,64},{64,32},{33,65},{65,33},{34,66},{66,34},{35,67},{67,35},{3... | collective-permute-start | bytes 488 | tf_op jit(solution)/shard_map/ppermute | solution.py:667
  13.4 18.8 %copy-start.5 = (f32[1280]{0:T(1024)S(1)}, f32[1280]{0:T(1024)}, u32[]{:S(2)}) copy-start(f32[1280]{0:T(1024)} %rest_3_.1) | copy-start | bytes 15364
  20.3 11.1 %collective-permute-start.10 = (bf16[256,1280]{1,0:T(8,128)(2,1)S(1)}, bf16[256,1280]{1,0:T(8,128)(2,1)S(1)}, u32[]{:S(2)}, u32[]{:S(2)}) collective-permute-start(bf16[256,1280]{1,0:T(8,128)(2,1)S(1)} %collective-permute-done.6.refs_0_), channel_id=1, source_target_pairs={{0,2},{2,0},{4,6},{6,4},{8,10},{10,8},{12,14},{14,12},{16,18},{18,... | collective-permute-start | bytes 1966088 | tf_op jit(solution)/shard_map/ppermute | solution.py:673
  20.6 10.7 %collective-permute-start.11 = (bf16[256,1280]{1,0:T(8,128)(2,1)S(1)}, bf16[256,1280]{1,0:T(8,128)(2,1)}, u32[]{:S(2)}, u32[]{:S(2)}) collective-permute-start(bf16[256,1280]{1,0:T(8,128)(2,1)S(1)} %collective-permute-done.7.refs_1_), channel_id=1, source_target_pairs={{0,2},{2,0},{4,6},{6,4},{8,10},{10,8},{12,14},{14,12},{16,18},{18,... | collective-permute-start | bytes 1966088 | tf_op jit(solution)/shard_map/ppermute | solution.py:673
  20.8 6.6 %collective-permute-start.4 = (s32[3,5,8]{2,1,0:T(8,128)S(1)}, s32[3,5,8]{2,1,0:T(8,128)S(1)}, u32[]{:S(2)}, u32[]{:S(2)}) collective-permute-start(s32[3,5,8]{2,1,0:T(8,128)S(1)} %pad_add_fusion), channel_id=1, source_target_pairs={{2,4},{4,2},{6,8},{8,6},{10,12},{12,10},{14,16},{16,14},{18,20},{2... | collective-permute-start | bytes 1448 | tf_op jit(solution)/shard_map/ppermute | solution.py:670
  23.8 3.7 %collective-permute-start.5 = (s32[3,5,8]{2,1,0:T(8,128)S(1)}, s32[3,5,8]{2,1,0:T(8,128)S(1)}, u32[]{:S(2)}, u32[]{:S(2)}) collective-permute-start(s32[3,5,8]{2,1,0:T(8,128)S(1)} %pad_add_fusion), channel_id=1, source_target_pairs={{0,2},{2,0},{4,6},{6,4},{8,10},{10,8},{12,14},{14,12},{16,18},{18,... | collective-permute-start | bytes 1448 | tf_op jit(solution)/shard_map/ppermute | solution.py:673
  27.4 17.4 %collective-permute-start.8 = (bf16[256,1280]{1,0:T(8,128)(2,1)S(1)}, bf16[256,1280]{1,0:T(8,128)(2,1)}, u32[]{:S(2)}, u32[]{:S(2)}) collective-permute-start(bf16[256,1280]{1,0:T(8,128)(2,1)S(1)} %collective-permute-done.3.refs_2_), channel_id=1, source_target_pairs={{0,32},{32,0},{64,96},{96,64},{1,33},{33,1},{65,97},{97,65},{2,34}... | collective-permute-start | bytes 1966088 | tf_op jit(solution)/shard_map/ppermute | solution.py:664
  27.4 19.3 %collective-permute-start.9 = (bf16[256,1280]{1,0:T(8,128)(2,1)S(1)}, bf16[256,1280]{1,0:T(8,128)(2,1)}, u32[]{:S(2)}, u32[]{:S(2)}) collective-permute-start(bf16[256,1280]{1,0:T(8,128)(2,1)S(1)} %collective-permute-done.3.refs_2_), channel_id=1, source_target_pairs={{32,64},{64,32},{33,65},{65,33},{34,66},{66,34},{35,67},{67,35},{3... | collective-permute-start | bytes 1966088 | tf_op jit(solution)/shard_map/ppermute | solution.py:667
  59.0 16.9 %collective-permute-start.12 = (bf16[256,1280]{1,0:T(8,128)(2,1)S(1)}, bf16[256,1280]{1,0:T(8,128)(2,1)}, u32[]{:S(2)}, u32[]{:S(2)}) collective-permute-start(bf16[256,1280]{1,0:T(8,128)(2,1)S(1)} %get-tuple-element.65.mine_hbm), channel_id=1, source_target_pairs={{0,1},{1,0},{2,3},{3,2},{4,5},{5,4},{6,7},{7,6},{8,9},{9,8},{10,11... | collective-permute-start | bytes 1966088 | tf_op jit(solution)/shard_map/ppermute | solution.py:725
  81.2 20.4 %copy-start.2 = (f32[256,640]{1,0:T(8,128)}, f32[256,640]{1,0:T(8,128)S(1)}, u32[]{:S(2)}) copy-start(f32[256,640]{1,0:T(8,128)S(1)} %get-tuple-element.76.rest_5_) | copy-start | bytes 1966084
  81.2 9.9 %collective-permute-start.14 = (bf16[288,640]{1,0:T(8,128)(2,1)S(1)}, bf16[288,640]{1,0:T(8,128)(2,1)S(1)}, u32[]{:S(2)}, u32[]{:S(2)}) collective-permute-start(bf16[288,640]{1,0:T(8,128)(2,1)S(1)} %get-tuple-element.69.pay_ref.rest_0_), channel_id=1, source_target_pairs={{0,32},{32,0},{64,96},{96,64},{1,33},{33,1},{65,97},{97,65},{2,34}... | collective-permute-start | bytes 1105928 | tf_op jit(solution)/shard_map/ppermute | solution.py:664
  81.3 11.8 %collective-permute-start.15 = (bf16[288,640]{1,0:T(8,128)(2,1)S(1)}, bf16[288,640]{1,0:T(8,128)(2,1)S(1)}, u32[]{:S(2)}, u32[]{:S(2)}) collective-permute-start(bf16[288,640]{1,0:T(8,128)(2,1)S(1)} %get-tuple-element.69.pay_ref.rest_0_), channel_id=1, source_target_pairs={{32,64},{64,32},{33,65},{65,33},{34,66},{66,34},{35,67},{67,35},{3... | collective-permute-start | bytes 1105928 | tf_op jit(solution)/shard_map/ppermute | solution.py:667
  84.1 17.6 %collective-permute-start.13 = (bf16[288,640]{1,0:T(8,128)(2,1)S(1)}, bf16[288,640]{1,0:T(8,128)(2,1)S(1)}, u32[]{:S(2)}, u32[]{:S(2)}) collective-permute-start(bf16[288,640]{1,0:T(8,128)(2,1)S(1)} %get-tuple-element.69.pay_ref.rest_0_), channel_id=1, source_target_pairs={{2,4},{4,2},{6,8},{8,6},{10,12},{12,10},{14,16},{16,14},{18,20},{2... | collective-permute-start | bytes 1105928 | tf_op jit(solution)/shard_map/ppermute | solution.py:670
  86.0 18.3 %collective-permute-start.16 = (bf16[288,640]{1,0:T(8,128)(2,1)S(1)}, bf16[288,640]{1,0:T(8,128)(2,1)S(1)}, u32[]{:S(2)}, u32[]{:S(2)}) collective-permute-start(bf16[288,640]{1,0:T(8,128)(2,1)S(1)} %get-tuple-element.69.pay_ref.rest_0_), channel_id=1, source_target_pairs={{0,2},{2,0},{4,6},{6,4},{8,10},{10,8},{12,14},{14,12},{16,18},{18,... | collective-permute-start | bytes 1105928 | tf_op jit(solution)/shard_map/ppermute | solution.py:673
  91.1 13.2 %collective-permute-start.17 = (bf16[288,640]{1,0:T(8,128)(2,1)S(1)}, bf16[288,640]{1,0:T(8,128)(2,1)S(1)}, u32[]{:S(2)}, u32[]{:S(2)}) collective-permute-start(bf16[288,640]{1,0:T(8,128)(2,1)S(1)} %collective-permute-done.14.rest_1_), channel_id=1, source_target_pairs={{0,2},{2,0},{4,6},{6,4},{8,10},{10,8},{12,14},{14,12},{16,18},{18,... | collective-permute-start | bytes 1105928 | tf_op jit(solution)/shard_map/ppermute | solution.py:673
  93.2 11.2 %collective-permute-start.18 = (bf16[288,640]{1,0:T(8,128)(2,1)S(1)}, bf16[288,640]{1,0:T(8,128)(2,1)S(1)}, u32[]{:S(2)}, u32[]{:S(2)}) collective-permute-start(bf16[288,640]{1,0:T(8,128)(2,1)S(1)} %collective-permute-done.15.rest_2_), channel_id=1, source_target_pairs={{0,2},{2,0},{4,6},{6,4},{8,10},{10,8},{12,14},{14,12},{16,18},{18,... | collective-permute-start | bytes 1105928 | tf_op jit(solution)/shard_map/ppermute | solution.py:673
  101.7 18.5 %collective-permute-start.19 = (bf16[288,640]{1,0:T(8,128)(2,1)S(1)}, bf16[288,640]{1,0:T(8,128)(2,1)S(1)}, u32[]{:S(2)}, u32[]{:S(2)}) collective-permute-start(bf16[288,640]{1,0:T(8,128)(2,1)S(1)} %collective-permute-done.13.rest_3_), channel_id=1, source_target_pairs={{0,32},{32,0},{64,96},{96,64},{1,33},{33,1},{65,97},{97,65},{2,34}... | collective-permute-start | bytes 1105928 | tf_op jit(solution)/shard_map/ppermute | solution.py:664
  101.8 18.5 %collective-permute-start.20 = (bf16[288,640]{1,0:T(8,128)(2,1)S(1)}, bf16[288,640]{1,0:T(8,128)(2,1)S(1)}, u32[]{:S(2)}, u32[]{:S(2)}) collective-permute-start(bf16[288,640]{1,0:T(8,128)(2,1)S(1)} %collective-permute-done.13.rest_3_), channel_id=1, source_target_pairs={{32,64},{64,32},{33,65},{65,33},{34,66},{66,34},{35,67},{67,35},{3... | collective-permute-start | bytes 1105928 | tf_op jit(solution)/shard_map/ppermute | solution.py:667
  129.7 10.6 %collective-permute-start.21 = (bf16[256,640]{1,0:T(8,128)(2,1)S(1)}, bf16[256,640]{1,0:T(8,128)(2,1)S(1)}, u32[]{:S(2)}, u32[]{:S(2)}) collective-permute-start(bf16[256,640]{1,0:T(8,128)(2,1)S(1)} %get-tuple-element.78), channel_id=1, source_target_pairs={{0,1},{1,0},{2,3},{3,2},{4,5},{5,4},{6,7},{7,6},{8,9},{9,8},{10,11... | collective-permute-start | bytes 983048 | tf_op jit(solution)/shard_map/ppermute | solution.py:739
  (11 other events, 52.3 us)

commit v4 on v3

--- a/solution.py
+++ b/solution.py
@@ -730,7 +730,7 @@
     off, mate = from_off(pay), from_mate(pay)
     pair, after = from_pair(pay), from_other(pay)
     dq = query_grad(local, pay, kv, far, p)
-    dq, off = lax.optimization_barrier((dq, off))
+    dq, off, pair, after = lax.optimization_barrier((dq, off, pair, after))
     near, mates, corners = (pay, pair, after, off), (mate, from_mate(pair), from_mate(after)), (from_pair(off), from_other(off))
     acc, base = key_near(
         near_list, own_counts, own_q.reshape(tw, tube, feats), far_q, kv, w, dq, [*near, *mates]

time: 143 us -> 138 us (0.965)
  waiting for transfers between devices: 25.1 us -> 19.7 us
  Pallas kernels: 79.2 us -> 80.8 us
    ppermute x5, waiting for transfers between devices: 4.52 us -> 0.33 us  [from_pair(): return lax.ppermute(x, 'tm', pair_times)]
    pallas_call x1, Pallas kernels: 9.49 us -> 11.1 us  [key_last(): pl.pallas_call(functools.partial(key_last_body, n, first), in_specs=[smem...]
  transfers between devices with their start and end apart: 22 -> 22, of which waited for: 8 -> 7; matrix products, arithmetic and copies ran while one was open for 3% -> 3% of each run, Pallas kernels for 38% -> 39%
where the time goes in v4:
time: 138 us; the launch traced here: 137 us
  Pallas kernels  80.8 us (59%)
  starting transfers between devices  27.7 us (20%)
  waiting for transfers between devices  19.7 us (14%)
  local copies, waits for them, and re-layouts  5.09 us (4%)
  other arithmetic  3.75 us (3%)
    pallas_call x1, Pallas kernels, key_near(): pl.pallas_call(functools.partial(key_near_body, n), in_specs=[smem] * 2 +...  14.9 us
    ppermute x5, starting transfers between devices, from_other(): return lax.ppermute(x, 'tm', other_times)  13.4 us
    pallas_call x1, Pallas kernels, project_near(): pl.pallas_call(functools.partial(project_near_body, n), grid=(2,), in_spe...  12.3 us
    pallas_call x1, Pallas kernels, project_queries(): pl.pallas_call(functools.partial(project_queries_body, n), grid=(n,), in_...  11.8 us
    pallas_call x1, Pallas kernels, attend_forward(): pl.pallas_call(forward_body, in_specs=[smem, smem, vmem, vmem, vmem, hbm,...  11.4 us
    pallas_call x1, Pallas kernels, key_last(): pl.pallas_call(functools.partial(key_last_body, n, first), in_specs=[smem...  11.1 us
    ppermute x1, waiting for transfers between devices, per_device(): got = lax.ppermute(send, 'section', swap)  9.67 us
    pallas_call x1, Pallas kernels, query_grad(): pl.pallas_call(query_body, in_specs=[smem] + [hbm] * 4, out_specs=vmem, o...  8.46 us
  transfers between devices with their start and end apart: 22, of which 7 were waited for; matrix products, arithmetic and copies ran while one was open for 3% of the time, Pallas kernels for 39%

profile of v4, /device:TPU:54, one launch (start us, length us, event | category | flops | bytes accessed | tf_op | source)
XLA Modules:
  0.0 137.5 jit_solution(9886943985691182114)
XLA Ops:
  0.0 1.3 collective-permute-start.6
  1.3 1.9 %collective-permute-start.7 = (bf16[256,1280]{1,0:T(8,128)(2,1)}, bf16[256,1280]{1,0:T(8,128)(2,1)S(1)}, u32[]{:S(2)}, u32[]{:S(2)}) collective-permute-start(bf16[256,1280]{1,0:T(8,128)(2,1)} %bitcast.37), channel_id=1, source_target_pairs={{32,64},{64,32},{33,65},{65,33},{34,66},{66,34},{35,67},{67,35},{3... | collective-permute-start | bytes 1966088 | tf_op jit(solution)/shard_map/ppermute | solution.py:667
  3.2 3.1 %collective-permute-start.3 = (bf16[256,1280]{1,0:T(8,128)(2,1)}, bf16[256,1280]{1,0:T(8,128)(2,1)S(1)}, u32[]{:S(2)}, u32[]{:S(2)}) collective-permute-start(bf16[256,1280]{1,0:T(8,128)(2,1)} %bitcast.38), channel_id=1, source_target_pairs={{2,4},{4,2},{6,8},{8,6},{10,12},{12,10},{14,16},{16,14},{18,20},{2... | collective-permute-start | bytes 1966088 | tf_op jit(solution)/shard_map/ppermute | solution.py:670
  7.9 3.6 %collective-permute-start.2 = (s32[5,8]{1,0:T(8,128)S(1)}, s32[5,8]{1,0:T(8,128)S(1)}, u32[]{:S(2)}, u32[]{:S(2)}) collective-permute-start(s32[5,8]{1,0:T(8,128)S(1)} %pad_add_fusion.1), channel_id=1, source_target_pairs={{32,64},{64,32},{33,65},{65,33},{34,66},{66,34},{35,67},{67,35},{3... | collective-permute-start | bytes 488 | tf_op jit(solution)/shard_map/ppermute | solution.py:667
  13.4 5.5 %project_own.1 = (bf16[12,256,1280]{2,1,0:T(8,128)(2,1)}, bf16[256,640]{1,0:T(8,128)(2,1)S(1)}) custom-call(bf16[256,1280]{1,0:T(8,128)(2,1)S(1)} %bitcast.41, f32[1280]{0:T(1024)S(1)} %copy-done.4, bf16[3,1280,640]{2,1,0:T(8,128)(2,1)} %bitcast.51), custom_call_target="tpu_custom_call" | custom-call | flops 1 | bytes 1 | tf_op jit(solution)/shard_map/project_own/pallas_call | solution.py:129
  18.9 1.4 %collective-permute-done.7.refs_1_ = bf16[256,1280]{1,0:T(8,128)(2,1)S(1)} collective-permute-done((bf16[256,1280]{1,0:T(8,128)(2,1)}, bf16[256,1280]{1,0:T(8,128)(2,1)S(1)}, u32[]{:S(2)}, u32[]{:S(2)}) %collective-permute-start.7) | collective-permute-done | bytes 655392 | tf_op jit(solution)/shard_map/ppermute | solution.py:667
  20.8 2.9 %collective-permute-start.4 = (s32[3,5,8]{2,1,0:T(8,128)S(1)}, s32[3,5,8]{2,1,0:T(8,128)S(1)}, u32[]{:S(2)}, u32[]{:S(2)}) collective-permute-start(s32[3,5,8]{2,1,0:T(8,128)S(1)} %pad_add_fusion), channel_id=1, source_target_pairs={{2,4},{4,2},{6,8},{8,6},{10,12},{12,10},{14,16},{16,14},{18,20},{2... | collective-permute-start | bytes 1448 | tf_op jit(solution)/shard_map/ppermute | solution.py:670
  23.8 1.9 %collective-permute-start.5 = (s32[3,5,8]{2,1,0:T(8,128)S(1)}, s32[3,5,8]{2,1,0:T(8,128)S(1)}, u32[]{:S(2)}, u32[]{:S(2)}) collective-permute-start(s32[3,5,8]{2,1,0:T(8,128)S(1)} %pad_add_fusion), channel_id=1, source_target_pairs={{0,2},{2,0},{4,6},{6,4},{8,10},{10,8},{12,14},{14,12},{16,18},{18,... | collective-permute-start | bytes 1448 | tf_op jit(solution)/shard_map/ppermute | solution.py:673
  25.7 1.7 %collective-permute-done.4 = s32[3,5,8]{2,1,0:T(8,128)S(1)} collective-permute-done((s32[3,5,8]{2,1,0:T(8,128)S(1)}, s32[3,5,8]{2,1,0:T(8,128)S(1)}, u32[]{:S(2)}, u32[]{:S(2)}) %collective-permute-start.4) | collective-permute-done | bytes 512 | tf_op jit(solution)/shard_map/ppermute | solution.py:670
  27.4 2.5 %collective-permute-start.9 = (bf16[256,1280]{1,0:T(8,128)(2,1)S(1)}, bf16[256,1280]{1,0:T(8,128)(2,1)}, u32[]{:S(2)}, u32[]{:S(2)}) collective-permute-start(bf16[256,1280]{1,0:T(8,128)(2,1)S(1)} %collective-permute-done.3.refs_2_), channel_id=1, source_target_pairs={{32,64},{64,32},{33,65},{65,33},{34,66},{66,34},{35,67},{67,35},{3... | collective-permute-start | bytes 1966088 | tf_op jit(solution)/shard_map/ppermute | solution.py:667
  32.2 12.3 %project_near.1 = bf16[12,256,1280]{2,1,0:T(8,128)(2,1)} custom-call(bf16[256,1280]{1,0:T(8,128)(2,1)S(1)} %collective-permute-done.6.refs_0_, bf16[256,1280]{1,0:T(8,128)(2,1)S(1)} %collective-permute-done.7.refs_1_, bf16[256,1280]{1,0:T(8,128)(2,1)S(1)} %collective-permute-done.3.refs_2_, ...), custom_call_target="tpu_custom_call", output_to_operand_aliasing={{}: (8, {})} | custom-call | flops 1 | bytes 1 | tf_op jit(solution)/shard_map/project_near/pallas_call | solution.py:94
  44.8 1.9 %collective-permute-done.9.x1_ref.refs_7_ = bf16[256,1280]{1,0:T(8,128)(2,1)} collective-permute-done((bf16[256,1280]{1,0:T(8,128)(2,1)S(1)}, bf16[256,1280]{1,0:T(8,128)(2,1)}, u32[]{:S(2)}, u32[]{:S(2)}) %collective-permute-start.9) | collective-permute-done | bytes 655392 | tf_op jit(solution)/shard_map/ppermute | solution.py:667
  46.7 11.4 %attend_forward.1 = (bf16[256,1280]{1,0:T(8,128)(2,1)S(1)}, f32[256,640]{1,0:T(8,128)S(1)}, f32[4,8,128]{2,1,0:T(8,128)S(1)}, bf16[4,512,512]{2,1,0:T(8,128)(2,1)}, bf16[8,64,1280]{2,1,0:T(8,128)(2,1)}) custom-call(s32[4,8]{1,0:T(4,128)S(1)} %get-tuple-element.84.local_ref, s32[9,4]{1,0:T(8,128)S(1)} %copy.18.count_ref, ...), custom_call_target="tpu_custom_call" | custom-call | flops 1 | bytes 1 | tf_op jit(solution)/shard_map/attend_forward/pallas_call | solution.py:263
  60.8 11.8 %project_queries.1 = bf16[8,256,640]{2,1,0:T(8,128)(2,1)} custom-call(bf16[256,1280]{1,0:T(8,128)(2,1)S(1)} %collective-permute-done.6.refs_0_, bf16[256,1280]{1,0:T(8,128)(2,1)S(1)} %collective-permute-done.7.refs_1_, bf16[256,1280]{1,0:T(8,128)(2,1)S(1)} %collective-permute-done.3.refs_2_, bf16[256,1280]{1,0:T(8,128)(2,1)} %copy-done.7, ...), custom_call_target="tpu_custom_call" | custom-call | flops 1 | bytes 1 | tf_op jit(solution)/shard_map/project_queries/pallas_call | solution.py:166
  72.5 3.3 %collective-permute-done.12.other_ref = bf16[256,1280]{1,0:T(8,128)(2,1)} collective-permute-done((bf16[256,1280]{1,0:T(8,128)(2,1)S(1)}, bf16[256,1280]{1,0:T(8,128)(2,1)}, u32[]{:S(2)}, u32[]{:S(2)}) %collective-permute-start.12) | collective-permute-done | bytes 655392 | tf_op jit(solution)/shard_map/ppermute | solution.py:725
  75.8 5.4 %middle.1 = (bf16[288,640]{1,0:T(8,128)(2,1)S(1)}, f32[256,640]{1,0:T(8,128)S(1)}) custom-call(s32[4]{0:T(128)S(1)} %bitcast.44, s32[1]{0:T(128)} %bitcast.13.sec_ref, bf16[256,1280]{1,0:T(8,128)(2,1)S(1)} %get-tuple-element.67.mine_hbm, bf16[256,1280]{1,0:T(8,128)(2,1)} %collective-permute-done.12.other_ref, bf16[256,1280]{1,0:T(8,128)(2,1)} %bitcast.39, ...), custom_call_target="tpu_custom_call" | custom-call | flops 1 | bytes 1 | tf_op jit(solution)/shard_map/middle/pallas_call | solution.py:360
  81.2 1.9 %collective-permute-start.13 = (bf16[288,640]{1,0:T(8,128)(2,1)S(1)}, bf16[288,640]{1,0:T(8,128)(2,1)S(1)}, u32[]{:S(2)}, u32[]{:S(2)}) collective-permute-start(bf16[288,640]{1,0:T(8,128)(2,1)S(1)} %get-tuple-element.71.pay_ref.rest_0_), channel_id=1, source_target_pairs={{2,4},{4,2},{6,8},{8,6},{10,12},{12,10},{14,16},{16,14},{18,20},{2... | collective-permute-start | bytes 1105928 | tf_op jit(solution)/shard_map/ppermute | solution.py:670
  83.3 2.7 %collective-permute-start.15 = (bf16[288,640]{1,0:T(8,128)(2,1)S(1)}, bf16[288,640]{1,0:T(8,128)(2,1)S(1)}, u32[]{:S(2)}, u32[]{:S(2)}) collective-permute-start(bf16[288,640]{1,0:T(8,128)(2,1)S(1)} %get-tuple-element.71.pay_ref.rest_0_), channel_id=1, source_target_pairs={{32,64},{64,32},{33,65},{65,33},{34,66},{66,34},{35,67},{67,35},{3... | collective-permute-start | bytes 1105928 | tf_op jit(solution)/shard_map/ppermute | solution.py:667
  86.6 8.5 %query_grad.1.dq_ref = bf16[256,640]{1,0:T(8,128)(2,1)S(1)} custom-call(s32[4,8]{1,0:T(4,128)S(1)} %get-tuple-element.84.local_ref, bf16[288,640]{1,0:T(8,128)(2,1)S(1)} %get-tuple-element.71.pay_ref.rest_0_, bf16[48,64,1280]{2,1,0:T(8,128)(2,1)} %bitcast.48, bf16[8,64,1280]{2,1,0:T(8,128)(2,1)S(1)} %copy-done.1, bf16[4,512,512]{2,1,0:T(8,128)(2,1)} %get-tuple-element.73.p_ref), custom_call_target="tpu_custom_call" | custom-call | flops 1 | bytes 1 | tf_op jit(solution)/shard_map/query_grad/pallas_call | solution.py:482
  95.1 1.4 %collective-permute-done.15.rest_2_ = bf16[288,640]{1,0:T(8,128)(2,1)S(1)} collective-permute-done((bf16[288,640]{1,0:T(8,128)(2,1)S(1)}, bf16[288,640]{1,0:T(8,128)(2,1)S(1)}, u32[]{:S(2)}, u32[]{:S(2)}) %collective-permute-start.15) | collective-permute-done | bytes 368672 | tf_op jit(solution)/shard_map/ppermute | solution.py:667
  97.1 2.6 %collective-permute-start.20 = (bf16[288,640]{1,0:T(8,128)(2,1)S(1)}, bf16[288,640]{1,0:T(8,128)(2,1)S(1)}, u32[]{:S(2)}, u32[]{:S(2)}) collective-permute-start(bf16[288,640]{1,0:T(8,128)(2,1)S(1)} %collective-permute-done.13.rest_3_), channel_id=1, source_target_pairs={{32,64},{64,32},{33,65},{65,33},{34,66},{66,34},{35,67},{67,35},{3... | collective-permute-start | bytes 1105928 | tf_op jit(solution)/shard_map/ppermute | solution.py:667
  100.7 14.9 %key_near.1 = (f32[256,1280]{1,0:T(8,128)}, f32[256,1280]{1,0:T(8,128)}) custom-call(s32[4,25]{1,0:T(4,128)S(1)} %pad_add_fusion.2.list_ref, s32[4]{0:T(128)S(1)} %bitcast.45, bf16[4,64,640]{2,1,0:T(8,128)(2,1)S(1)} %bitcast.42, bf16[32,64,640]{2,1,0:T(8,128)(2,1)} %bitcast.57, bf16[48,64,1280]{2,1,0:T(8,128)(2,1)} %bitcast.49, ...), custom_call_target="tpu_custom_call" | custom-call | flops 1 | bytes 1 | tf_op jit(solution)/shard_map/key_near/pallas_call | solution.py:558
  115.6 11.1 %key_last.1 = (bf16[256,640]{1,0:T(8,128)(2,1)S(1)}, f32[256,640]{1,0:T(8,128)S(1)}) custom-call(s32[4,9]{1,0:T(4,128)S(1)} %pad_add_fusion.3.list_ref, s32[4]{0:T(128)S(1)} %bitcast.46, s32[1]{0:T(128)} %bitcast.13.sec_ref, bf16[32,64,640]{2,1,0:T(8,128)(2,1)} %bitcast.58, bf16[48,64,1280]{2,1,0:T(8,128)(2,1)} %bitcast.50, bf16[3,1280,640]{2,1,0:T(8,128)(2,1)} %bitcast.56, ...), custom_call_target="tpu_custom_call" | custom-call | flops 1 | bytes 1 | tf_op jit(solution)/shard_map/key_last/pallas_call | solution.py:627
  127.0 9.7 %collective-permute-done.21 = bf16[256,640]{1,0:T(8,128)(2,1)S(1)} collective-permute-done((bf16[256,640]{1,0:T(8,128)(2,1)S(1)}, bf16[256,640]{1,0:T(8,128)(2,1)S(1)}, u32[]{:S(2)}, u32[]{:S(2)}) %collective-permute-start.21) | collective-permute-done | bytes 327712 | tf_op jit(solution)/shard_map/ppermute | solution.py:739
  (86 shorter events, 12.3 us)
Async XLA Ops:
  0.0 7.8 %collective-permute-start = (bf16[256,1280]{1,0:T(8,128)(2,1)}, bf16[256,1280]{1,0:T(8,128)(2,1)S(1)}, u32[]{:S(2)}, u32[]{:S(2)}) collective-permute-start(bf16[256,1280]{1,0:T(8,128)(2,1)} %bitcast.35), channel_id=1, source_target_pairs={{0,2},{2,0},{4,6},{6,4},{8,10},{10,8},{12,14},{14,12},{16,18},{18,... | collective-permute-start | bytes 1966088 | tf_op jit(solution)/shard_map/ppermute | solution.py:673
  0.0 18.9 %collective-permute-start.6 = (bf16[256,1280]{1,0:T(8,128)(2,1)}, bf16[256,1280]{1,0:T(8,128)(2,1)S(1)}, u32[]{:S(2)}, u32[]{:S(2)}) collective-permute-start(bf16[256,1280]{1,0:T(8,128)(2,1)} %bitcast.36), channel_id=1, source_target_pairs={{0,32},{32,0},{64,96},{96,64},{1,33},{33,1},{65,97},{97,65},{2,34}... | collective-permute-start | bytes 1966088 | tf_op jit(solution)/shard_map/ppermute | solution.py:664
  1.3 19.0 %collective-permute-start.7 = (bf16[256,1280]{1,0:T(8,128)(2,1)}, bf16[256,1280]{1,0:T(8,128)(2,1)S(1)}, u32[]{:S(2)}, u32[]{:S(2)}) collective-permute-start(bf16[256,1280]{1,0:T(8,128)(2,1)} %bitcast.37), channel_id=1, source_target_pairs={{32,64},{64,32},{33,65},{65,33},{34,66},{66,34},{35,67},{67,35},{3... | collective-permute-start | bytes 1966088 | tf_op jit(solution)/shard_map/ppermute | solution.py:667
  3.2 22.5 %collective-permute-start.3 = (bf16[256,1280]{1,0:T(8,128)(2,1)}, bf16[256,1280]{1,0:T(8,128)(2,1)S(1)}, u32[]{:S(2)}, u32[]{:S(2)}) collective-permute-start(bf16[256,1280]{1,0:T(8,128)(2,1)} %bitcast.38), channel_id=1, source_target_pairs={{2,4},{4,2},{6,8},{8,6},{10,12},{12,10},{14,16},{16,14},{18,20},{2... | collective-permute-start | bytes 1966088 | tf_op jit(solution)/shard_map/ppermute | solution.py:670
  7.8 13.0 %collective-permute-start.1 = (s32[5,8]{1,0:T(8,128)S(1)}, s32[5,8]{1,0:T(8,128)S(1)}, u32[]{:S(2)}, u32[]{:S(2)}) collective-permute-start(s32[5,8]{1,0:T(8,128)S(1)} %pad_add_fusion.1), channel_id=1, source_target_pairs={{0,32},{32,0},{64,96},{96,64},{1,33},{33,1},{65,97},{97,65},{2,34}... | collective-permute-start | bytes 488 | tf_op jit(solution)/shard_map/ppermute | solution.py:664
  7.9 12.9 %collective-permute-start.2 = (s32[5,8]{1,0:T(8,128)S(1)}, s32[5,8]{1,0:T(8,128)S(1)}, u32[]{:S(2)}, u32[]{:S(2)}) collective-permute-start(s32[5,8]{1,0:T(8,128)S(1)} %pad_add_fusion.1), channel_id=1, source_target_pairs={{32,64},{64,32},{33,65},{65,33},{34,66},{66,34},{35,67},{67,35},{3... | collective-permute-start | bytes 488 | tf_op jit(solution)/shard_map/ppermute | solution.py:667
  13.4 18.8 %copy-start.5 = (f32[1280]{0:T(1024)S(1)}, f32[1280]{0:T(1024)}, u32[]{:S(2)}) copy-start(f32[1280]{0:T(1024)} %rest_3_.1) | copy-start | bytes 15364
  20.3 11.1 %collective-permute-start.10 = (bf16[256,1280]{1,0:T(8,128)(2,1)S(1)}, bf16[256,1280]{1,0:T(8,128)(2,1)S(1)}, u32[]{:S(2)}, u32[]{:S(2)}) collective-permute-start(bf16[256,1280]{1,0:T(8,128)(2,1)S(1)} %collective-permute-done.6.refs_0_), channel_id=1, source_target_pairs={{0,2},{2,0},{4,6},{6,4},{8,10},{10,8},{12,14},{14,12},{16,18},{18,... | collective-permute-start | bytes 1966088 | tf_op jit(solution)/shard_map/ppermute | solution.py:673
  20.6 10.7 %collective-permute-start.11 = (bf16[256,1280]{1,0:T(8,128)(2,1)S(1)}, bf16[256,1280]{1,0:T(8,128)(2,1)}, u32[]{:S(2)}, u32[]{:S(2)}) collective-permute-start(bf16[256,1280]{1,0:T(8,128)(2,1)S(1)} %collective-permute-done.7.refs_1_), channel_id=1, source_target_pairs={{0,2},{2,0},{4,6},{6,4},{8,10},{10,8},{12,14},{14,12},{16,18},{18,... | collective-permute-start | bytes 1966088 | tf_op jit(solution)/shard_map/ppermute | solution.py:673
  20.8 6.6 %collective-permute-start.4 = (s32[3,5,8]{2,1,0:T(8,128)S(1)}, s32[3,5,8]{2,1,0:T(8,128)S(1)}, u32[]{:S(2)}, u32[]{:S(2)}) collective-permute-start(s32[3,5,8]{2,1,0:T(8,128)S(1)} %pad_add_fusion), channel_id=1, source_target_pairs={{2,4},{4,2},{6,8},{8,6},{10,12},{12,10},{14,16},{16,14},{18,20},{2... | collective-permute-start | bytes 1448 | tf_op jit(solution)/shard_map/ppermute | solution.py:670
  23.8 3.7 %collective-permute-start.5 = (s32[3,5,8]{2,1,0:T(8,128)S(1)}, s32[3,5,8]{2,1,0:T(8,128)S(1)}, u32[]{:S(2)}, u32[]{:S(2)}) collective-permute-start(s32[3,5,8]{2,1,0:T(8,128)S(1)} %pad_add_fusion), channel_id=1, source_target_pairs={{0,2},{2,0},{4,6},{6,4},{8,10},{10,8},{12,14},{14,12},{16,18},{18,... | collective-permute-start | bytes 1448 | tf_op jit(solution)/shard_map/ppermute | solution.py:673
  27.4 17.4 %collective-permute-start.8 = (bf16[256,1280]{1,0:T(8,128)(2,1)S(1)}, bf16[256,1280]{1,0:T(8,128)(2,1)}, u32[]{:S(2)}, u32[]{:S(2)}) collective-permute-start(bf16[256,1280]{1,0:T(8,128)(2,1)S(1)} %collective-permute-done.3.refs_2_), channel_id=1, source_target_pairs={{0,32},{32,0},{64,96},{96,64},{1,33},{33,1},{65,97},{97,65},{2,34}... | collective-permute-start | bytes 1966088 | tf_op jit(solution)/shard_map/ppermute | solution.py:664
  27.4 19.3 %collective-permute-start.9 = (bf16[256,1280]{1,0:T(8,128)(2,1)S(1)}, bf16[256,1280]{1,0:T(8,128)(2,1)}, u32[]{:S(2)}, u32[]{:S(2)}) collective-permute-start(bf16[256,1280]{1,0:T(8,128)(2,1)S(1)} %collective-permute-done.3.refs_2_), channel_id=1, source_target_pairs={{32,64},{64,32},{33,65},{65,33},{34,66},{66,34},{35,67},{67,35},{3... | collective-permute-start | bytes 1966088 | tf_op jit(solution)/shard_map/ppermute | solution.py:667
  59.0 16.9 %collective-permute-start.12 = (bf16[256,1280]{1,0:T(8,128)(2,1)S(1)}, bf16[256,1280]{1,0:T(8,128)(2,1)}, u32[]{:S(2)}, u32[]{:S(2)}) collective-permute-start(bf16[256,1280]{1,0:T(8,128)(2,1)S(1)} %get-tuple-element.67.mine_hbm), channel_id=1, source_target_pairs={{0,1},{1,0},{2,3},{3,2},{4,5},{5,4},{6,7},{7,6},{8,9},{9,8},{10,11... | collective-permute-start | bytes 1966088 | tf_op jit(solution)/shard_map/ppermute | solution.py:725
  60.8 15.1 %copy-start.6 = (s32[1,1,4]{2,1,0:T(1,128)S(1)}, s32[1,1,4]{2,1,0:T(1,128)}, u32[]{:S(2)}) copy-start(s32[1,1,4]{2,1,0:T(1,128)} %param.13) | copy-start | bytes 52
  81.2 13.9 %collective-permute-start.13 = (bf16[288,640]{1,0:T(8,128)(2,1)S(1)}, bf16[288,640]{1,0:T(8,128)(2,1)S(1)}, u32[]{:S(2)}, u32[]{:S(2)}) collective-permute-start(bf16[288,640]{1,0:T(8,128)(2,1)S(1)} %get-tuple-element.71.pay_ref.rest_0_), channel_id=1, source_target_pairs={{2,4},{4,2},{6,8},{8,6},{10,12},{12,10},{14,16},{16,14},{18,20},{2... | collective-permute-start | bytes 1105928 | tf_op jit(solution)/shard_map/ppermute | solution.py:670
  83.2 12.0 %collective-permute-start.14 = (bf16[288,640]{1,0:T(8,128)(2,1)S(1)}, bf16[288,640]{1,0:T(8,128)(2,1)S(1)}, u32[]{:S(2)}, u32[]{:S(2)}) collective-permute-start(bf16[288,640]{1,0:T(8,128)(2,1)S(1)} %get-tuple-element.71.pay_ref.rest_0_), channel_id=1, source_target_pairs={{0,32},{32,0},{64,96},{96,64},{1,33},{33,1},{65,97},{97,65},{2,34}... | collective-permute-start | bytes 1105928 | tf_op jit(solution)/shard_map/ppermute | solution.py:664
  83.3 13.3 %collective-permute-start.15 = (bf16[288,640]{1,0:T(8,128)(2,1)S(1)}, bf16[288,640]{1,0:T(8,128)(2,1)S(1)}, u32[]{:S(2)}, u32[]{:S(2)}) collective-permute-start(bf16[288,640]{1,0:T(8,128)(2,1)S(1)} %get-tuple-element.71.pay_ref.rest_0_), channel_id=1, source_target_pairs={{32,64},{64,32},{33,65},{65,33},{34,66},{66,34},{35,67},{67,35},{3... | collective-permute-start | bytes 1105928 | tf_op jit(solution)/shard_map/ppermute | solution.py:667
  86.0 13.7 %collective-permute-start.16 = (bf16[288,640]{1,0:T(8,128)(2,1)S(1)}, bf16[288,640]{1,0:T(8,128)(2,1)S(1)}, u32[]{:S(2)}, u32[]{:S(2)}) collective-permute-start(bf16[288,640]{1,0:T(8,128)(2,1)S(1)} %get-tuple-element.71.pay_ref.rest_0_), channel_id=1, source_target_pairs={{0,2},{2,0},{4,6},{6,4},{8,10},{10,8},{12,14},{14,12},{16,18},{18,... | collective-permute-start | bytes 1105928 | tf_op jit(solution)/shard_map/ppermute | solution.py:673
  96.6 3.2 %collective-permute-start.17 = (bf16[288,640]{1,0:T(8,128)(2,1)S(1)}, bf16[288,640]{1,0:T(8,128)(2,1)S(1)}, u32[]{:S(2)}, u32[]{:S(2)}) collective-permute-start(bf16[288,640]{1,0:T(8,128)(2,1)S(1)} %collective-permute-done.14.rest_1_), channel_id=1, source_target_pairs={{0,2},{2,0},{4,6},{6,4},{8,10},{10,8},{12,14},{14,12},{16,18},{18,... | collective-permute-start | bytes 1105928 | tf_op jit(solution)/shard_map/ppermute | solution.py:673
  96.6 3.1 %collective-permute-start.18 = (bf16[288,640]{1,0:T(8,128)(2,1)S(1)}, bf16[288,640]{1,0:T(8,128)(2,1)S(1)}, u32[]{:S(2)}, u32[]{:S(2)}) collective-permute-start(bf16[288,640]{1,0:T(8,128)(2,1)S(1)} %collective-permute-done.15.rest_2_), channel_id=1, source_target_pairs={{0,2},{2,0},{4,6},{6,4},{8,10},{10,8},{12,14},{14,12},{16,18},{18,... | collective-permute-start | bytes 1105928 | tf_op jit(solution)/shard_map/ppermute | solution.py:673
  97.1 18.5 %collective-permute-start.19 = (bf16[288,640]{1,0:T(8,128)(2,1)S(1)}, bf16[288,640]{1,0:T(8,128)(2,1)S(1)}, u32[]{:S(2)}, u32[]{:S(2)}) collective-permute-start(bf16[288,640]{1,0:T(8,128)(2,1)S(1)} %collective-permute-done.13.rest_3_), channel_id=1, source_target_pairs={{0,32},{32,0},{64,96},{96,64},{1,33},{33,1},{65,97},{97,65},{2,34}... | collective-permute-start | bytes 1105928 | tf_op jit(solution)/shard_map/ppermute | solution.py:664
  97.1 18.5 %collective-permute-start.20 = (bf16[288,640]{1,0:T(8,128)(2,1)S(1)}, bf16[288,640]{1,0:T(8,128)(2,1)S(1)}, u32[]{:S(2)}, u32[]{:S(2)}) collective-permute-start(bf16[288,640]{1,0:T(8,128)(2,1)S(1)} %collective-permute-done.13.rest_3_), channel_id=1, source_target_pairs={{32,64},{64,32},{33,65},{65,33},{34,66},{66,34},{35,67},{67,35},{3... | collective-permute-start | bytes 1105928 | tf_op jit(solution)/shard_map/ppermute | solution.py:667
  126.7 10.0 %collective-permute-start.21 = (bf16[256,640]{1,0:T(8,128)(2,1)S(1)}, bf16[256,640]{1,0:T(8,128)(2,1)S(1)}, u32[]{:S(2)}, u32[]{:S(2)}) collective-permute-start(bf16[256,640]{1,0:T(8,128)(2,1)S(1)} %get-tuple-element.82), channel_id=1, source_target_pairs={{0,1},{1,0},{2,3},{3,2},{4,5},{5,4},{6,7},{7,6},{8,9},{9,8},{10,11... | collective-permute-start | bytes 983048 | tf_op jit(solution)/shard_map/ppermute | solution.py:739
  (11 other events, 46.5 us)

commit v5 on v4

--- a/solution.py
+++ b/solution.py
@@ -499,28 +499,21 @@
     )(local, pay, kv, far, p)
 
 
-def key_near_body(n, list_ref, count_ref, own_q_ref, q_ref, kv_ref, w_ref, dq_ref, *rest):
+def key_near_body(n, list_ref, count_ref, own_q_ref, q_ref, kv_ref, *rest):
     pays = rest[:n]
-    grad_ref, base_ref, w_scr, dq_scr, q_scr, kv_scr, pay_scr, *scr, sem = rest[n:]
+    grad_ref, q_scr, kv_scr, pay_scr, *scr, sem = rest[n:]
     lse_scr, inner_scr = scr[:2]
     tubes = kv_scr.shape[0]
     rows = tubes * 64
     pay_copies = [pltpu.make_async_copy(pays[k], pay_scr.at[k], sem.at[k]) for k in range(n)]
-    first = [
-        pltpu.make_async_copy(dq_ref, dq_scr, sem.at[n + 4]),
-        pltpu.make_async_copy(w_ref.at[0], w_scr, sem.at[n]),
+    copies = [
+        pltpu.make_async_copy(own_q_ref, q_scr.at[:tubes], sem.at[n]),
+        pltpu.make_async_copy(q_ref.at[: (n - 1) * tubes], q_scr.at[tubes:], sem.at[n + 1]),
+        pltpu.make_async_copy(kv_ref.at[:tubes], kv_scr, sem.at[n + 2]),
     ]
-    copies = [
-        pltpu.make_async_copy(own_q_ref, q_scr.at[:tubes], sem.at[n + 1]),
-        pltpu.make_async_copy(q_ref.at[: (n - 1) * tubes], q_scr.at[tubes:], sem.at[n + 2]),
-        pltpu.make_async_copy(kv_ref.at[:tubes], kv_scr, sem.at[n + 3]),
-    ]
-    for c in first + pay_copies + copies:
+    for c in pay_copies + copies:
         c.start()
     grad_ref[...] = jnp.zeros_like(grad_ref)
-    for c in first:
-        c.wait()
-    base_ref[...] = dot_nt(dq_scr[...], w_scr[...])
     for k in range(n):
         pay_copies[k].wait()
         stats_of(pay_scr, k, rows, tubes, lse_scr, inner_scr)
@@ -547,35 +540,29 @@
     ]
 
 
-def key_near(lists, counts, own_q, q, kv, w, dq, pays):
-    rows, feats = dq.shape
-    width = w.shape[1]
-    tubes = rows // 64
+def key_near(lists, counts, own_q, q, kv, pays):
+    tubes, _, feats = own_q.shape
+    rows = tubes * 64
     n = len(pays)
     vmem = pl.BlockSpec(memory_space=pltpu.VMEM)
     smem = pl.BlockSpec(memory_space=pltpu.SMEM)
     hbm = pl.BlockSpec(memory_space=pl.ANY)
     return pl.pallas_call(
         functools.partial(key_near_body, n),
-        in_specs=[smem] * 2 + [hbm] * 5 + [vmem] * n,
-        out_specs=[vmem, vmem],
-        out_shape=[
-            jax.ShapeDtypeStruct((rows, 2 * feats), F32),
-            jax.ShapeDtypeStruct((rows, width), F32),
-        ],
-        scratch_shapes=[pltpu.VMEM((width, feats), BF16), pltpu.VMEM((rows, feats), BF16)]
-        + key_scratch(n, tubes, feats, NEAR_CHUNK)
-        + [pltpu.SemaphoreType.DMA((n + 5,))],
+        in_specs=[smem] * 2 + [hbm] * 3 + [vmem] * n,
+        out_specs=vmem,
+        out_shape=jax.ShapeDtypeStruct((rows, 2 * feats), F32),
+        scratch_shapes=key_scratch(n, tubes, feats, NEAR_CHUNK) + [pltpu.SemaphoreType.DMA((n + 3,))],
         compiler_params=pltpu.CompilerParams(vmem_limit_bytes=VMEM_LIMIT),
         cost_estimate=SMALL,
         name="key_near",
-    )(lists, counts, own_q, q, kv, w, dq, *pays)
+    )(lists, counts, own_q, q, kv, *pays)
 
 
 def key_last_body(n, first, list_ref, count_ref, sec_ref, q_ref, kv_ref, w_ref, acc_ref, *rest):
     pays = rest[:n]
-    video_ref, gain_ref, base_ref, g_ref, send_ref, keep_ref = rest[n : n + 6]
-    q_scr, kv_scr, pay_scr, *scr, w_scr, grad_scr, x_scr, base_scr, g_scr, sem = rest[n + 6 :]
+    video_ref, gain_ref, dq_ref, g_ref, send_ref, keep_ref = rest[n : n + 6]
+    q_scr, kv_scr, pay_scr, *scr, w_scr, grad_scr, x_scr, dq_scr, g_scr, sem = rest[n + 6 :]
     lse_scr, inner_scr = scr[:2]
     tubes = kv_scr.shape[0]
     rows = tubes * 64
@@ -583,12 +570,12 @@
     q_copy = pltpu.make_async_copy(q_ref.at[first * tubes : (first + n) * tubes], q_scr, sem.at[0])
     kv_copy = pltpu.make_async_copy(kv_ref.at[:tubes], kv_scr, sem.at[1])
     acc_copy = pltpu.make_async_copy(acc_ref, grad_scr, sem.at[2])
-    w_copy = pltpu.make_async_copy(w_ref.at[1:], w_scr, sem.at[3])
+    w_copy = pltpu.make_async_copy(w_ref, w_scr, sem.at[3])
     x_copy = pltpu.make_async_copy(video_ref, x_scr, sem.at[4])
-    base_copy = pltpu.make_async_copy(base_ref, base_scr, sem.at[5])
+    dq_copy = pltpu.make_async_copy(dq_ref, dq_scr, sem.at[5])
     g_copy = pltpu.make_async_copy(g_ref, g_scr, sem.at[6])
     pay_copies = [pltpu.make_async_copy(pays[k], pay_scr.at[k], sem.at[7 + k]) for k in range(n)]
-    for c in pay_copies + [q_copy, kv_copy, acc_copy, w_copy, x_copy, base_copy, g_copy]:
+    for c in pay_copies + [q_copy, kv_copy, acc_copy, w_copy, x_copy, dq_copy, g_copy]:
         c.start()
     for k, c in enumerate(pay_copies):
         c.wait()
@@ -601,9 +588,9 @@
     x_copy.wait()
     xhat, inverse = normalize(x_scr[...].astype(F32))
     w_copy.wait()
-    base_copy.wait()
+    dq_copy.wait()
     g_copy.wait()
-    d_normed = base_scr[...] + dot_nt(d_proj[:, :feats], w_scr[0]) + dot_nt(d_proj[:, feats:], w_scr[1])
+    d_normed = dot_nt(dq_scr[...], w_scr[0]) + dot_nt(d_proj[:, :feats], w_scr[1]) + dot_nt(d_proj[:, feats:], w_scr[2])
     scaled = d_normed * gain_of(gain_ref)
     out = (
         scaled
@@ -616,7 +603,7 @@
     keep_ref[...] = jnp.where(lower, out[:, :half], out[:, half:]) + g_scr[...]
 
 
-def key_last(first, lists, counts, sec, q, kv, w, acc, pays, video, gain, base, g):
+def key_last(first, lists, counts, sec, q, kv, w, acc, pays, video, gain, dq, g):
     rows, width = video.shape
     feats = q.shape[2]
     tubes = rows // 64
@@ -634,17 +621,17 @@
         ],
         scratch_shapes=key_scratch(n, tubes, feats, LAST_CHUNK)
         + [
-            pltpu.VMEM((2, width, feats), BF16),
+            pltpu.VMEM((3, width, feats), BF16),
             pltpu.VMEM((rows, 2 * feats), F32),
             pltpu.VMEM((rows, width), BF16),
-            pltpu.VMEM((rows, width), F32),
+            pltpu.VMEM((rows, feats), BF16),
             pltpu.VMEM((rows, width // 2), F32),
             pltpu.SemaphoreType.DMA((7 + n,)),
         ],
         compiler_params=pltpu.CompilerParams(vmem_limit_bytes=VMEM_LIMIT),
         cost_estimate=SMALL,
         name="key_last",
-    )(lists, counts, sec, q, kv, w, acc, *pays, video, gain, base, g)
+    )(lists, counts, sec, q, kv, w, acc, *pays, video, gain, dq, g)
 
 
 def per_device(video, target, gain, w_qkv, w_out, neighbours, counts):
@@ -732,10 +719,8 @@
     dq = query_grad(local, pay, kv, far, p)
     dq, off, pair, after = lax.optimization_barrier((dq, off, pair, after))
     near, mates, corners = (pay, pair, after, off), (mate, from_mate(pair), from_mate(after)), (from_pair(off), from_other(off))
-    acc, base = key_near(
-        near_list, own_counts, own_q.reshape(tw, tube, feats), far_q, kv, w, dq, [*near, *mates]
-    )
-    send, keep = key_last(6, last_list, own_counts, sec, far_q, kv, w, acc, corners, video, gain, base, g)
+    acc = key_near(near_list, own_counts, own_q.reshape(tw, tube, feats), far_q, kv, [*near, *mates])
+    send, keep = key_last(6, last_list, own_counts, sec, far_q, kv, w, acc, corners, video, gain, dq, g)
     got = lax.ppermute(send, "section", swap)
     return (keep + got.astype(F32)).astype(BF16).reshape(tt, th, tw, tube, width // 2)
 

time: 138 us -> 140 us (1.014)
  the two profiles are of different devices: /device:TPU:54 before, /device:TPU:49 now
where the time goes in v5:
time: 140 us; the launch traced here: 137 us
  Pallas kernels  82.1 us (59%)
  starting transfers between devices  32.9 us (24%)
  waiting for transfers between devices  12 us (9%)
  local copies, waits for them, and re-layouts  5.16 us (4%)
  other arithmetic  4.82 us (3%)
    ppermute x3, starting transfers between devices, from_off(): return lax.ppermute(x, 'height', off_chip)  17.4 us
    pallas_call x1, Pallas kernels, key_near(): pl.pallas_call(functools.partial(key_near_body, n), in_specs=[smem] * 2 +...  14.2 us
    pallas_call x1, Pallas kernels, key_last(): pl.pallas_call(functools.partial(key_last_body, n, first), in_specs=[smem...  13.2 us
    pallas_call x1, Pallas kernels, project_near(): pl.pallas_call(functools.partial(project_near_body, n), grid=(2,), in_spe...  12.3 us
    ppermute x5, starting transfers between devices, from_other(): return lax.ppermute(x, 'tm', other_times)  12.2 us
    pallas_call x1, Pallas kernels, project_queries(): pl.pallas_call(functools.partial(project_queries_body, n), grid=(n,), in_...  11.8 us
    pallas_call x1, Pallas kernels, attend_forward(): pl.pallas_call(forward_body, in_specs=[smem, smem, vmem, vmem, vmem, hbm,...  11.4 us
    pallas_call x1, Pallas kernels, query_grad(): pl.pallas_call(query_body, in_specs=[smem] + [hbm] * 4, out_specs=vmem, o...  8.46 us
  transfers between devices with their start and end apart: 22, of which 5 were waited for; matrix products, arithmetic and copies ran while one was open for 3% of the time, Pallas kernels for 38%

profile of v5, /device:TPU:49, one launch (start us, length us, event | category | flops | bytes accessed | tf_op | source)
XLA Modules:
  0.0 137.5 jit_solution(12740851645920579496)
XLA Ops:
  0.7 1.0 collective-permute-start.6
  1.7 1.9 %collective-permute-start.7 = (bf16[256,1280]{1,0:T(8,128)(2,1)}, bf16[256,1280]{1,0:T(8,128)(2,1)S(1)}, u32[]{:S(2)}, u32[]{:S(2)}) collective-permute-start(bf16[256,1280]{1,0:T(8,128)(2,1)} %bitcast.37), channel_id=1, source_target_pairs={{32,64},{64,32},{33,65},{65,33},{34,66},{66,34},{35,67},{67,35},{3... | collective-permute-start | bytes 1966088 | tf_op jit(solution)/shard_map/ppermute | solution.py:654
  3.6 4.8 %collective-permute-start.3 = (bf16[256,1280]{1,0:T(8,128)(2,1)}, bf16[256,1280]{1,0:T(8,128)(2,1)S(1)}, u32[]{:S(2)}, u32[]{:S(2)}) collective-permute-start(bf16[256,1280]{1,0:T(8,128)(2,1)} %bitcast.38), channel_id=1, source_target_pairs={{2,4},{4,2},{6,8},{8,6},{10,12},{12,10},{14,16},{16,14},{18,20},{2... | collective-permute-start | bytes 1966088 | tf_op jit(solution)/shard_map/ppermute | solution.py:657
  10.0 3.6 %collective-permute-start.2 = (s32[5,8]{1,0:T(8,128)S(1)}, s32[5,8]{1,0:T(8,128)S(1)}, u32[]{:S(2)}, u32[]{:S(2)}) collective-permute-start(s32[5,8]{1,0:T(8,128)S(1)} %pad_add_fusion.1), channel_id=1, source_target_pairs={{32,64},{64,32},{33,65},{65,33},{34,66},{66,34},{35,67},{67,35},{3... | collective-permute-start | bytes 488 | tf_op jit(solution)/shard_map/ppermute | solution.py:654
  13.7 1.1 copy-done
  15.4 5.6 %project_own.1 = (bf16[12,256,1280]{2,1,0:T(8,128)(2,1)}, bf16[256,640]{1,0:T(8,128)(2,1)S(1)}) custom-call(bf16[256,1280]{1,0:T(8,128)(2,1)S(1)} %bitcast.41, f32[1280]{0:T(1024)S(1)} %copy-done.4, bf16[3,1280,640]{2,1,0:T(8,128)(2,1)} %bitcast.51), custom_call_target="tpu_custom_call" | custom-call | flops 1 | bytes 1 | tf_op jit(solution)/shard_map/project_own/pallas_call | solution.py:129
  21.6 4.4 %collective-permute-start.4 = (s32[3,5,8]{2,1,0:T(8,128)S(1)}, s32[3,5,8]{2,1,0:T(8,128)S(1)}, u32[]{:S(2)}, u32[]{:S(2)}) collective-permute-start(s32[3,5,8]{2,1,0:T(8,128)S(1)} %pad_add_fusion), channel_id=1, source_target_pairs={{2,4},{4,2},{6,8},{8,6},{10,12},{12,10},{14,16},{16,14},{18,20},{2... | collective-permute-start | bytes 1448 | tf_op jit(solution)/shard_map/ppermute | solution.py:657
  26.2 2.3 %collective-permute-done.4 = s32[3,5,8]{2,1,0:T(8,128)S(1)} collective-permute-done((s32[3,5,8]{2,1,0:T(8,128)S(1)}, s32[3,5,8]{2,1,0:T(8,128)S(1)}, u32[]{:S(2)}, u32[]{:S(2)}) %collective-permute-start.4) | collective-permute-done | bytes 512 | tf_op jit(solution)/shard_map/ppermute | solution.py:657
  28.4 2.1 %collective-permute-start.9 = (bf16[256,1280]{1,0:T(8,128)(2,1)S(1)}, bf16[256,1280]{1,0:T(8,128)(2,1)}, u32[]{:S(2)}, u32[]{:S(2)}) collective-permute-start(bf16[256,1280]{1,0:T(8,128)(2,1)S(1)} %collective-permute-done.3.refs_2_), channel_id=1, source_target_pairs={{32,64},{64,32},{33,65},{65,33},{34,66},{66,34},{35,67},{67,35},{3... | collective-permute-start | bytes 1966088 | tf_op jit(solution)/shard_map/ppermute | solution.py:654
  32.8 12.3 %project_near.1 = bf16[12,256,1280]{2,1,0:T(8,128)(2,1)} custom-call(bf16[256,1280]{1,0:T(8,128)(2,1)S(1)} %collective-permute-done.6.refs_0_, bf16[256,1280]{1,0:T(8,128)(2,1)S(1)} %collective-permute-done.7.refs_1_, bf16[256,1280]{1,0:T(8,128)(2,1)S(1)} %collective-permute-done.3.refs_2_, ...), custom_call_target="tpu_custom_call", output_to_operand_aliasing={{}: (8, {})} | custom-call | flops 1 | bytes 1 | tf_op jit(solution)/shard_map/project_near/pallas_call | solution.py:94
  45.1 0.9 collective-permute-done.9.x1_ref.refs_7_
  46.0 11.4 %attend_forward.1 = (bf16[256,1280]{1,0:T(8,128)(2,1)S(1)}, f32[256,640]{1,0:T(8,128)S(1)}, f32[4,8,128]{2,1,0:T(8,128)S(1)}, bf16[4,512,512]{2,1,0:T(8,128)(2,1)}, bf16[8,64,1280]{2,1,0:T(8,128)(2,1)}) custom-call(s32[4,8]{1,0:T(4,128)S(1)} %get-tuple-element.80.local_ref, s32[9,4]{1,0:T(8,128)S(1)} %copy.18.count_ref, ...), custom_call_target="tpu_custom_call" | custom-call | flops 1 | bytes 1 | tf_op jit(solution)/shard_map/attend_forward/pallas_call | solution.py:263
  59.1 11.8 %project_queries.1 = bf16[8,256,640]{2,1,0:T(8,128)(2,1)} custom-call(bf16[256,1280]{1,0:T(8,128)(2,1)S(1)} %collective-permute-done.6.refs_0_, bf16[256,1280]{1,0:T(8,128)(2,1)S(1)} %collective-permute-done.7.refs_1_, bf16[256,1280]{1,0:T(8,128)(2,1)S(1)} %collective-permute-done.3.refs_2_, bf16[256,1280]{1,0:T(8,128)(2,1)} %copy-done.7, ...), custom_call_target="tpu_custom_call" | custom-call | flops 1 | bytes 1 | tf_op jit(solution)/shard_map/project_queries/pallas_call | solution.py:166
  70.9 2.2 %collective-permute-done.12.other_ref = bf16[256,1280]{1,0:T(8,128)(2,1)} collective-permute-done((bf16[256,1280]{1,0:T(8,128)(2,1)S(1)}, bf16[256,1280]{1,0:T(8,128)(2,1)}, u32[]{:S(2)}, u32[]{:S(2)}) %collective-permute-start.12) | collective-permute-done | bytes 655392 | tf_op jit(solution)/shard_map/ppermute | solution.py:712
  73.0 5.3 %middle.1 = (bf16[288,640]{1,0:T(8,128)(2,1)S(1)}, f32[256,640]{1,0:T(8,128)S(1)}) custom-call(s32[4]{0:T(128)S(1)} %bitcast.44, s32[1]{0:T(128)} %bitcast.13.sec_ref, bf16[256,1280]{1,0:T(8,128)(2,1)S(1)} %get-tuple-element.65.mine_hbm, bf16[256,1280]{1,0:T(8,128)(2,1)} %collective-permute-done.12.other_ref, bf16[256,1280]{1,0:T(8,128)(2,1)} %bitcast.39, ...), custom_call_target="tpu_custom_call" | custom-call | flops 1 | bytes 1 | tf_op jit(solution)/shard_map/middle/pallas_call | solution.py:360
  78.3 8.1 %collective-permute-start.13 = (bf16[288,640]{1,0:T(8,128)(2,1)S(1)}, bf16[288,640]{1,0:T(8,128)(2,1)S(1)}, u32[]{:S(2)}, u32[]{:S(2)}) collective-permute-start(bf16[288,640]{1,0:T(8,128)(2,1)S(1)} %get-tuple-element.69.pay_ref.rest_0_), channel_id=1, source_target_pairs={{2,4},{4,2},{6,8},{8,6},{10,12},{12,10},{14,16},{16,14},{18,20},{2... | collective-permute-start | bytes 1105928 | tf_op jit(solution)/shard_map/ppermute | solution.py:657
  86.6 1.9 %collective-permute-start.15 = (bf16[288,640]{1,0:T(8,128)(2,1)S(1)}, bf16[288,640]{1,0:T(8,128)(2,1)S(1)}, u32[]{:S(2)}, u32[]{:S(2)}) collective-permute-start(bf16[288,640]{1,0:T(8,128)(2,1)S(1)} %get-tuple-element.69.pay_ref.rest_0_), channel_id=1, source_target_pairs={{32,64},{64,32},{33,65},{65,33},{34,66},{66,34},{35,67},{67,35},{3... | collective-permute-start | bytes 1105928 | tf_op jit(solution)/shard_map/ppermute | solution.py:654
  88.6 8.5 %query_grad.1.rest_4_ = bf16[256,640]{1,0:T(8,128)(2,1)S(1)} custom-call(s32[4,8]{1,0:T(4,128)S(1)} %get-tuple-element.80.local_ref, bf16[288,640]{1,0:T(8,128)(2,1)S(1)} %get-tuple-element.69.pay_ref.rest_0_, bf16[48,64,1280]{2,1,0:T(8,128)(2,1)} %bitcast.48, bf16[8,64,1280]{2,1,0:T(8,128)(2,1)S(1)} %copy-done.1, bf16[4,512,512]{2,1,0:T(8,128)(2,1)} %get-tuple-element.71.p_ref), custom_call_target="tpu_custom_call" | custom-call | flops 1 | bytes 1 | tf_op jit(solution)/shard_map/query_grad/pallas_call | solution.py:482
  97.1 0.9 collective-permute-done.15.rest_2_
  98.5 2.6 %collective-permute-start.20 = (bf16[288,640]{1,0:T(8,128)(2,1)S(1)}, bf16[288,640]{1,0:T(8,128)(2,1)S(1)}, u32[]{:S(2)}, u32[]{:S(2)}) collective-permute-start(bf16[288,640]{1,0:T(8,128)(2,1)S(1)} %collective-permute-done.13.rest_3_), channel_id=1, source_target_pairs={{32,64},{64,32},{33,65},{65,33},{34,66},{66,34},{35,67},{67,35},{3... | collective-permute-start | bytes 1105928 | tf_op jit(solution)/shard_map/ppermute | solution.py:654
  102.2 14.2 %key_near.1.acc_ref = f32[256,1280]{1,0:T(8,128)} custom-call(s32[4,25]{1,0:T(4,128)S(1)} %pad_add_fusion.2.list_ref, s32[4]{0:T(128)S(1)} %bitcast.45, bf16[4,64,640]{2,1,0:T(8,128)(2,1)S(1)} %bitcast.42, bf16[32,64,640]{2,1,0:T(8,128)(2,1)} %bitcast.56, bf16[48,64,1280]{2,1,0:T(8,128)(2,1)} %bitcast.49, ...), custom_call_target="tpu_custom_call" | custom-call | flops 1 | bytes 1 | tf_op jit(solution)/shard_map/key_near/pallas_call | solution.py:550
  116.4 13.2 %key_last.1 = (bf16[256,640]{1,0:T(8,128)(2,1)S(1)}, f32[256,640]{1,0:T(8,128)}) custom-call(s32[4,9]{1,0:T(4,128)S(1)} %pad_add_fusion.3.list_ref, s32[4]{0:T(128)S(1)} %bitcast.46, s32[1]{0:T(128)} %bitcast.13.sec_ref, bf16[32,64,640]{2,1,0:T(8,128)(2,1)} %bitcast.57, bf16[48,64,1280]{2,1,0:T(8,128)(2,1)} %bitcast.50, bf16[3,1280,640]{2,1,0:T(8,128)(2,1)} %bitcast.55, ...), custom_call_target="tpu_custom_call" | custom-call | flops 1 | bytes 1 | tf_op jit(solution)/shard_map/key_last/pallas_call | solution.py:614
  129.8 5.8 %collective-permute-done.21 = bf16[256,640]{1,0:T(8,128)(2,1)S(1)} collective-permute-done((bf16[256,640]{1,0:T(8,128)(2,1)S(1)}, bf16[256,640]{1,0:T(8,128)(2,1)S(1)}, u32[]{:S(2)}, u32[]{:S(2)}) %collective-permute-start.21) | collective-permute-done | bytes 327712 | tf_op jit(solution)/shard_map/ppermute | solution.py:724
  135.6 1.9 %add_convert_fusion = bf16[256,640]{1,0:T(8,128)(2,1)} fusion(f32[256,640]{1,0:T(8,128)} %get-tuple-element.77, bf16[256,640]{1,0:T(8,128)(2,1)S(1)} %collective-permute-done.21), kind=kLoop, calls=%fused_computation | loop fusion | flops 491520 | bytes 1310720 | tf_op jit(solution)/shard_map/convert_element_type | solution.py:725
  (84 shorter events, 9.4 us)
Async XLA Ops:
  0.0 9.9 %collective-permute-start = (bf16[256,1280]{1,0:T(8,128)(2,1)}, bf16[256,1280]{1,0:T(8,128)(2,1)S(1)}, u32[]{:S(2)}, u32[]{:S(2)}) collective-permute-start(bf16[256,1280]{1,0:T(8,128)(2,1)} %bitcast.35), channel_id=1, source_target_pairs={{0,2},{2,0},{4,6},{6,4},{8,10},{10,8},{12,14},{14,12},{16,18},{18,... | collective-permute-start | bytes 1966088 | tf_op jit(solution)/shard_map/ppermute | solution.py:660
  0.7 20.3 %collective-permute-start.6 = (bf16[256,1280]{1,0:T(8,128)(2,1)}, bf16[256,1280]{1,0:T(8,128)(2,1)S(1)}, u32[]{:S(2)}, u32[]{:S(2)}) collective-permute-start(bf16[256,1280]{1,0:T(8,128)(2,1)} %bitcast.36), channel_id=1, source_target_pairs={{0,32},{32,0},{64,96},{96,64},{1,33},{33,1},{65,97},{97,65},{2,34}... | collective-permute-start | bytes 1966088 | tf_op jit(solution)/shard_map/ppermute | solution.py:651
  1.7 19.3 %collective-permute-start.7 = (bf16[256,1280]{1,0:T(8,128)(2,1)}, bf16[256,1280]{1,0:T(8,128)(2,1)S(1)}, u32[]{:S(2)}, u32[]{:S(2)}) collective-permute-start(bf16[256,1280]{1,0:T(8,128)(2,1)} %bitcast.37), channel_id=1, source_target_pairs={{32,64},{64,32},{33,65},{65,33},{34,66},{66,34},{35,67},{67,35},{3... | collective-permute-start | bytes 1966088 | tf_op jit(solution)/shard_map/ppermute | solution.py:654
  3.6 22.6 %collective-permute-start.3 = (bf16[256,1280]{1,0:T(8,128)(2,1)}, bf16[256,1280]{1,0:T(8,128)(2,1)S(1)}, u32[]{:S(2)}, u32[]{:S(2)}) collective-permute-start(bf16[256,1280]{1,0:T(8,128)(2,1)} %bitcast.38), channel_id=1, source_target_pairs={{2,4},{4,2},{6,8},{8,6},{10,12},{12,10},{14,16},{16,14},{18,20},{2... | collective-permute-start | bytes 1966088 | tf_op jit(solution)/shard_map/ppermute | solution.py:657
  9.9 11.7 %collective-permute-start.1 = (s32[5,8]{1,0:T(8,128)S(1)}, s32[5,8]{1,0:T(8,128)S(1)}, u32[]{:S(2)}, u32[]{:S(2)}) collective-permute-start(s32[5,8]{1,0:T(8,128)S(1)} %pad_add_fusion.1), channel_id=1, source_target_pairs={{0,32},{32,0},{64,96},{96,64},{1,33},{33,1},{65,97},{97,65},{2,34}... | collective-permute-start | bytes 488 | tf_op jit(solution)/shard_map/ppermute | solution.py:651
  10.0 11.6 %collective-permute-start.2 = (s32[5,8]{1,0:T(8,128)S(1)}, s32[5,8]{1,0:T(8,128)S(1)}, u32[]{:S(2)}, u32[]{:S(2)}) collective-permute-start(s32[5,8]{1,0:T(8,128)S(1)} %pad_add_fusion.1), channel_id=1, source_target_pairs={{32,64},{64,32},{33,65},{65,33},{34,66},{66,34},{35,67},{67,35},{3... | collective-permute-start | bytes 488 | tf_op jit(solution)/shard_map/ppermute | solution.py:654
  21.0 11.0 %collective-permute-start.10 = (bf16[256,1280]{1,0:T(8,128)(2,1)S(1)}, bf16[256,1280]{1,0:T(8,128)(2,1)S(1)}, u32[]{:S(2)}, u32[]{:S(2)}) collective-permute-start(bf16[256,1280]{1,0:T(8,128)(2,1)S(1)} %collective-permute-done.6.refs_0_), channel_id=1, source_target_pairs={{0,2},{2,0},{4,6},{6,4},{8,10},{10,8},{12,14},{14,12},{16,18},{18,... | collective-permute-start | bytes 1966088 | tf_op jit(solution)/shard_map/ppermute | solution.py:660
  21.1 10.9 %collective-permute-start.11 = (bf16[256,1280]{1,0:T(8,128)(2,1)S(1)}, bf16[256,1280]{1,0:T(8,128)(2,1)}, u32[]{:S(2)}, u32[]{:S(2)}) collective-permute-start(bf16[256,1280]{1,0:T(8,128)(2,1)S(1)} %collective-permute-done.7.refs_1_), channel_id=1, source_target_pairs={{0,2},{2,0},{4,6},{6,4},{8,10},{10,8},{12,14},{14,12},{16,18},{18,... | collective-permute-start | bytes 1966088 | tf_op jit(solution)/shard_map/ppermute | solution.py:660
  21.6 6.8 %collective-permute-start.4 = (s32[3,5,8]{2,1,0:T(8,128)S(1)}, s32[3,5,8]{2,1,0:T(8,128)S(1)}, u32[]{:S(2)}, u32[]{:S(2)}) collective-permute-start(s32[3,5,8]{2,1,0:T(8,128)S(1)} %pad_add_fusion), channel_id=1, source_target_pairs={{2,4},{4,2},{6,8},{8,6},{10,12},{12,10},{14,16},{16,14},{18,20},{2... | collective-permute-start | bytes 1448 | tf_op jit(solution)/shard_map/ppermute | solution.py:657
  26.0 2.4 %collective-permute-start.5 = (s32[3,5,8]{2,1,0:T(8,128)S(1)}, s32[3,5,8]{2,1,0:T(8,128)S(1)}, u32[]{:S(2)}, u32[]{:S(2)}) collective-permute-start(s32[3,5,8]{2,1,0:T(8,128)S(1)} %pad_add_fusion), channel_id=1, source_target_pairs={{0,2},{2,0},{4,6},{6,4},{8,10},{10,8},{12,14},{14,12},{16,18},{18,... | collective-permute-start | bytes 1448 | tf_op jit(solution)/shard_map/ppermute | solution.py:660
  28.4 16.7 %collective-permute-start.8 = (bf16[256,1280]{1,0:T(8,128)(2,1)S(1)}, bf16[256,1280]{1,0:T(8,128)(2,1)}, u32[]{:S(2)}, u32[]{:S(2)}) collective-permute-start(bf16[256,1280]{1,0:T(8,128)(2,1)S(1)} %collective-permute-done.3.refs_2_), channel_id=1, source_target_pairs={{0,32},{32,0},{64,96},{96,64},{1,33},{33,1},{65,97},{97,65},{2,34}... | collective-permute-start | bytes 1966088 | tf_op jit(solution)/shard_map/ppermute | solution.py:651
  28.4 17.6 %collective-permute-start.9 = (bf16[256,1280]{1,0:T(8,128)(2,1)S(1)}, bf16[256,1280]{1,0:T(8,128)(2,1)}, u32[]{:S(2)}, u32[]{:S(2)}) collective-permute-start(bf16[256,1280]{1,0:T(8,128)(2,1)S(1)} %collective-permute-done.3.refs_2_), channel_id=1, source_target_pairs={{32,64},{64,32},{33,65},{65,33},{34,66},{66,34},{35,67},{67,35},{3... | collective-permute-start | bytes 1966088 | tf_op jit(solution)/shard_map/ppermute | solution.py:654
  58.3 14.8 %collective-permute-start.12 = (bf16[256,1280]{1,0:T(8,128)(2,1)S(1)}, bf16[256,1280]{1,0:T(8,128)(2,1)}, u32[]{:S(2)}, u32[]{:S(2)}) collective-permute-start(bf16[256,1280]{1,0:T(8,128)(2,1)S(1)} %get-tuple-element.65.mine_hbm), channel_id=1, source_target_pairs={{0,1},{1,0},{2,3},{3,2},{4,5},{5,4},{6,7},{7,6},{8,9},{9,8},{10,11... | collective-permute-start | bytes 1966088 | tf_op jit(solution)/shard_map/ppermute | solution.py:712
  70.9 17.7 %copy-start.1 = (bf16[8,64,1280]{2,1,0:T(8,128)(2,1)S(1)}, bf16[8,64,1280]{2,1,0:T(8,128)(2,1)}, u32[]{:S(2)}) copy-start(bf16[8,64,1280]{2,1,0:T(8,128)(2,1)} %get-tuple-element.70.far_ref) | copy-start | bytes 3932164
  78.3 18.7 %copy-start.2 = (f32[256,640]{1,0:T(8,128)}, f32[256,640]{1,0:T(8,128)S(1)}, u32[]{:S(2)}) copy-start(f32[256,640]{1,0:T(8,128)S(1)} %get-tuple-element.76.rest_5_) | copy-start | bytes 1966084
  78.3 18.7 %collective-permute-start.13 = (bf16[288,640]{1,0:T(8,128)(2,1)S(1)}, bf16[288,640]{1,0:T(8,128)(2,1)S(1)}, u32[]{:S(2)}, u32[]{:S(2)}) collective-permute-start(bf16[288,640]{1,0:T(8,128)(2,1)S(1)} %get-tuple-element.69.pay_ref.rest_0_), channel_id=1, source_target_pairs={{2,4},{4,2},{6,8},{8,6},{10,12},{12,10},{14,16},{16,14},{18,20},{2... | collective-permute-start | bytes 1105928 | tf_op jit(solution)/shard_map/ppermute | solution.py:657
  86.5 10.6 %collective-permute-start.14 = (bf16[288,640]{1,0:T(8,128)(2,1)S(1)}, bf16[288,640]{1,0:T(8,128)(2,1)S(1)}, u32[]{:S(2)}, u32[]{:S(2)}) collective-permute-start(bf16[288,640]{1,0:T(8,128)(2,1)S(1)} %get-tuple-element.69.pay_ref.rest_0_), channel_id=1, source_target_pairs={{0,32},{32,0},{64,96},{96,64},{1,33},{33,1},{65,97},{97,65},{2,34}... | collective-permute-start | bytes 1105928 | tf_op jit(solution)/shard_map/ppermute | solution.py:651
  86.6 11.4 %collective-permute-start.15 = (bf16[288,640]{1,0:T(8,128)(2,1)S(1)}, bf16[288,640]{1,0:T(8,128)(2,1)S(1)}, u32[]{:S(2)}, u32[]{:S(2)}) collective-permute-start(bf16[288,640]{1,0:T(8,128)(2,1)S(1)} %get-tuple-element.69.pay_ref.rest_0_), channel_id=1, source_target_pairs={{32,64},{64,32},{33,65},{65,33},{34,66},{66,34},{35,67},{67,35},{3... | collective-permute-start | bytes 1105928 | tf_op jit(solution)/shard_map/ppermute | solution.py:654
  88.5 12.6 %collective-permute-start.16 = (bf16[288,640]{1,0:T(8,128)(2,1)S(1)}, bf16[288,640]{1,0:T(8,128)(2,1)S(1)}, u32[]{:S(2)}, u32[]{:S(2)}) collective-permute-start(bf16[288,640]{1,0:T(8,128)(2,1)S(1)} %get-tuple-element.69.pay_ref.rest_0_), channel_id=1, source_target_pairs={{0,2},{2,0},{4,6},{6,4},{8,10},{10,8},{12,14},{14,12},{16,18},{18,... | collective-permute-start | bytes 1105928 | tf_op jit(solution)/shard_map/ppermute | solution.py:660
  98.0 3.2 %collective-permute-start.17 = (bf16[288,640]{1,0:T(8,128)(2,1)S(1)}, bf16[288,640]{1,0:T(8,128)(2,1)S(1)}, u32[]{:S(2)}, u32[]{:S(2)}) collective-permute-start(bf16[288,640]{1,0:T(8,128)(2,1)S(1)} %collective-permute-done.14.rest_1_), channel_id=1, source_target_pairs={{0,2},{2,0},{4,6},{6,4},{8,10},{10,8},{12,14},{14,12},{16,18},{18,... | collective-permute-start | bytes 1105928 | tf_op jit(solution)/shard_map/ppermute | solution.py:660
  98.0 3.2 %collective-permute-start.18 = (bf16[288,640]{1,0:T(8,128)(2,1)S(1)}, bf16[288,640]{1,0:T(8,128)(2,1)S(1)}, u32[]{:S(2)}, u32[]{:S(2)}) collective-permute-start(bf16[288,640]{1,0:T(8,128)(2,1)S(1)} %collective-permute-done.15.rest_2_), channel_id=1, source_target_pairs={{0,2},{2,0},{4,6},{6,4},{8,10},{10,8},{12,14},{14,12},{16,18},{18,... | collective-permute-start | bytes 1105928 | tf_op jit(solution)/shard_map/ppermute | solution.py:660
  98.5 17.8 %collective-permute-start.19 = (bf16[288,640]{1,0:T(8,128)(2,1)S(1)}, bf16[288,640]{1,0:T(8,128)(2,1)S(1)}, u32[]{:S(2)}, u32[]{:S(2)}) collective-permute-start(bf16[288,640]{1,0:T(8,128)(2,1)S(1)} %collective-permute-done.13.rest_3_), channel_id=1, source_target_pairs={{0,32},{32,0},{64,96},{96,64},{1,33},{33,1},{65,97},{97,65},{2,34}... | collective-permute-start | bytes 1105928 | tf_op jit(solution)/shard_map/ppermute | solution.py:651
  98.5 17.8 %collective-permute-start.20 = (bf16[288,640]{1,0:T(8,128)(2,1)S(1)}, bf16[288,640]{1,0:T(8,128)(2,1)S(1)}, u32[]{:S(2)}, u32[]{:S(2)}) collective-permute-start(bf16[288,640]{1,0:T(8,128)(2,1)S(1)} %collective-permute-done.13.rest_3_), channel_id=1, source_target_pairs={{32,64},{64,32},{33,65},{65,33},{34,66},{66,34},{35,67},{67,35},{3... | collective-permute-start | bytes 1105928 | tf_op jit(solution)/shard_map/ppermute | solution.py:654
  129.6 6.0 %collective-permute-start.21 = (bf16[256,640]{1,0:T(8,128)(2,1)S(1)}, bf16[256,640]{1,0:T(8,128)(2,1)S(1)}, u32[]{:S(2)}, u32[]{:S(2)}) collective-permute-start(bf16[256,640]{1,0:T(8,128)(2,1)S(1)} %get-tuple-element.78), channel_id=1, source_target_pairs={{0,1},{1,0},{2,3},{3,2},{4,5},{5,4},{6,7},{7,6},{8,9},{9,8},{10,11... | collective-permute-start | bytes 983048 | tf_op jit(solution)/shard_map/ppermute | solution.py:724
  (10 other events, 48.5 us)

commit v6 on v4

--- a/solution.py
+++ b/solution.py
@@ -684,8 +684,8 @@
     kv, own_q = project_own(own_video, gain, w)
     pair, other, kv = lax.optimization_barrier((pair, other, kv))
     three = jnp.stack([meta, from_pair(meta), from_other(meta)])
+    off, kv, three = lax.optimization_barrier((off, kv, three))
     off_meta, mate_meta = from_off(three), from_mate(three)
-    off, off_meta, mate_meta, kv = lax.optimization_barrier((off, off_meta, mate_meta, kv))
     corners = from_pair(off), from_other(off)
     mates = mate, from_mate(pair), from_mate(other)
     rest = (pair, other, off, *mates)

time: 138 us -> 142 us (1.029)
  the two profiles are of different devices: /device:TPU:54 before, /device:TPU:40 now
where the time goes in v6:
time: 142 us; the launch traced here: 141 us
  Pallas kernels  78.6 us (55%)
  starting transfers between devices  34.6 us (24%)
  waiting for transfers between devices  18.8 us (13%)
  local copies, waits for them, and re-layouts  5.07 us (4%)
  other arithmetic  3.76 us (3%)
    ppermute x5, starting transfers between devices, from_other(): return lax.ppermute(x, 'tm', other_times)  14.7 us
    pallas_call x1, Pallas kernels, key_near(): pl.pallas_call(functools.partial(key_near_body, n), in_specs=[smem] * 2 +...  13.5 us
    ppermute x3, starting transfers between devices, from_off(): return lax.ppermute(x, 'height', off_chip)  12.9 us
    pallas_call x1, Pallas kernels, project_near(): pl.pallas_call(functools.partial(project_near_body, n), grid=(2,), in_spe...  12.3 us
    pallas_call x1, Pallas kernels, project_queries(): pl.pallas_call(functools.partial(project_queries_body, n), grid=(n,), in_...  11.8 us
    pallas_call x1, Pallas kernels, attend_forward(): pl.pallas_call(forward_body, in_specs=[smem, smem, vmem, vmem, vmem, hbm,...  11.4 us
    pallas_call x1, Pallas kernels, key_last(): pl.pallas_call(functools.partial(key_last_body, n, first), in_specs=[smem...  10.3 us
    ppermute x1, waiting for transfers between devices, per_device(): got = lax.ppermute(send, 'section', swap)  9.61 us
  transfers between devices with their start and end apart: 22, of which 6 were waited for; matrix products, arithmetic and copies ran while one was open for 3% of the time, Pallas kernels for 37%

profile of v6, /device:TPU:40, one launch (start us, length us, event | category | flops | bytes accessed | tf_op | source)
XLA Modules:
  0.0 141.3 jit_solution(11671630268411468966)
XLA Ops:
  0.5 4.3 %collective-permute-start.2 = (bf16[256,1280]{1,0:T(8,128)(2,1)}, bf16[256,1280]{1,0:T(8,128)(2,1)S(1)}, u32[]{:S(2)}, u32[]{:S(2)}) collective-permute-start(bf16[256,1280]{1,0:T(8,128)(2,1)} %bitcast.34), channel_id=1, source_target_pairs={{32,64},{64,32},{33,65},{65,33},{34,66},{66,34},{35,67},{67,35},{3... | collective-permute-start | bytes 1966088 | tf_op jit(solution)/shard_map/ppermute | solution.py:667
  4.8 4.0 %collective-permute-start = (bf16[256,1280]{1,0:T(8,128)(2,1)}, bf16[256,1280]{1,0:T(8,128)(2,1)S(1)}, u32[]{:S(2)}, u32[]{:S(2)}) collective-permute-start(bf16[256,1280]{1,0:T(8,128)(2,1)} %bitcast.35), channel_id=1, source_target_pairs={{2,4},{4,2},{6,8},{8,6},{10,12},{12,10},{14,16},{16,14},{18,20},{2... | collective-permute-start | bytes 1966088 | tf_op jit(solution)/shard_map/ppermute | solution.py:670
  10.3 2.2 %collective-permute-start.5 = (s32[5,8]{1,0:T(8,128)S(1)}, s32[5,8]{1,0:T(8,128)S(1)}, u32[]{:S(2)}, u32[]{:S(2)}) collective-permute-start(s32[5,8]{1,0:T(8,128)S(1)} %pad_add_fusion.5), channel_id=1, source_target_pairs={{32,64},{64,32},{33,65},{65,33},{34,66},{66,34},{35,67},{67,35},{3... | collective-permute-start | bytes 488 | tf_op jit(solution)/shard_map/ppermute | solution.py:667
  12.6 1.1 copy-done
  14.3 5.5 %project_own.1 = (bf16[12,256,1280]{2,1,0:T(8,128)(2,1)}, bf16[256,640]{1,0:T(8,128)(2,1)S(1)}) custom-call(bf16[256,1280]{1,0:T(8,128)(2,1)S(1)} %bitcast.38, f32[1280]{0:T(1024)S(1)} %copy-done.4, bf16[3,1280,640]{2,1,0:T(8,128)(2,1)} %bitcast.48), custom_call_target="tpu_custom_call" | custom-call | flops 1 | bytes 1 | tf_op jit(solution)/shard_map/project_own/pallas_call | solution.py:129
  20.2 4.9 %collective-permute-done.refs_2_ = bf16[256,1280]{1,0:T(8,128)(2,1)S(1)} collective-permute-done((bf16[256,1280]{1,0:T(8,128)(2,1)}, bf16[256,1280]{1,0:T(8,128)(2,1)S(1)}, u32[]{:S(2)}, u32[]{:S(2)}) %collective-permute-start) | collective-permute-done | bytes 655392 | tf_op jit(solution)/shard_map/ppermute | solution.py:670
  25.1 4.9 %collective-permute-start.6 = (s32[3,5,8]{2,1,0:T(8,128)S(1)}, s32[3,5,8]{2,1,0:T(8,128)S(1)}, u32[]{:S(2)}, u32[]{:S(2)}) collective-permute-start(s32[3,5,8]{2,1,0:T(8,128)S(1)} %pad_add_fusion.3), channel_id=1, source_target_pairs={{2,4},{4,2},{6,8},{8,6},{10,12},{12,10},{14,16},{16,14},{18,20},{2... | collective-permute-start | bytes 1448 | tf_op jit(solution)/shard_map/ppermute | solution.py:670
  30.7 1.8 %collective-permute-done.6 = s32[3,5,8]{2,1,0:T(8,128)S(1)} collective-permute-done((s32[3,5,8]{2,1,0:T(8,128)S(1)}, s32[3,5,8]{2,1,0:T(8,128)S(1)}, u32[]{:S(2)}, u32[]{:S(2)}) %collective-permute-start.6) | collective-permute-done | bytes 512 | tf_op jit(solution)/shard_map/ppermute | solution.py:670
  32.5 2.2 %collective-permute-start.9 = (bf16[256,1280]{1,0:T(8,128)(2,1)S(1)}, bf16[256,1280]{1,0:T(8,128)(2,1)}, u32[]{:S(2)}, u32[]{:S(2)}) collective-permute-start(bf16[256,1280]{1,0:T(8,128)(2,1)S(1)} %collective-permute-done.refs_2_), channel_id=1, source_target_pairs={{32,64},{64,32},{33,65},{65,33},{34,66},{66,34},{35,67},{67,35},{3... | collective-permute-start | bytes 1966088 | tf_op jit(solution)/shard_map/ppermute | solution.py:667
  37.0 12.3 %project_near.1 = bf16[12,256,1280]{2,1,0:T(8,128)(2,1)} custom-call(bf16[256,1280]{1,0:T(8,128)(2,1)S(1)} %collective-permute-done.1.refs_0_, bf16[256,1280]{1,0:T(8,128)(2,1)S(1)} %collective-permute-done.2.refs_1_, bf16[256,1280]{1,0:T(8,128)(2,1)S(1)} %collective-permute-done.refs_2_, ...), custom_call_target="tpu_custom_call", output_to_operand_aliasing={{}: (8, {})} | custom-call | flops 1 | bytes 1 | tf_op jit(solution)/shard_map/project_near/pallas_call | solution.py:94
  50.1 11.4 %attend_forward.1 = (bf16[256,1280]{1,0:T(8,128)(2,1)S(1)}, f32[256,640]{1,0:T(8,128)S(1)}, f32[4,8,128]{2,1,0:T(8,128)S(1)}, bf16[4,512,512]{2,1,0:T(8,128)(2,1)}, bf16[8,64,1280]{2,1,0:T(8,128)(2,1)}) custom-call(s32[4,8]{1,0:T(4,128)S(1)} %get-tuple-element.82.local_ref, s32[9,4]{1,0:T(8,128)S(1)} %copy.18.count_ref, ...), custom_call_target="tpu_custom_call" | custom-call | flops 1 | bytes 1 | tf_op jit(solution)/shard_map/attend_forward/pallas_call | solution.py:263
  61.5 0.8 copy-done.3
  62.4 0.9 collective-permute-start.12
  64.1 11.8 %project_queries.1 = bf16[8,256,640]{2,1,0:T(8,128)(2,1)} custom-call(bf16[256,1280]{1,0:T(8,128)(2,1)S(1)} %collective-permute-done.1.refs_0_, bf16[256,1280]{1,0:T(8,128)(2,1)S(1)} %collective-permute-done.2.refs_1_, bf16[256,1280]{1,0:T(8,128)(2,1)S(1)} %collective-permute-done.refs_2_, bf16[256,1280]{1,0:T(8,128)(2,1)} %copy-done.7, ...), custom_call_target="tpu_custom_call" | custom-call | flops 1 | bytes 1 | tf_op jit(solution)/shard_map/project_queries/pallas_call | solution.py:166
  75.9 1.3 collective-permute-done.12.other_ref
  77.2 5.4 %middle.1 = (bf16[288,640]{1,0:T(8,128)(2,1)S(1)}, f32[256,640]{1,0:T(8,128)S(1)}) custom-call(s32[4]{0:T(128)S(1)} %bitcast.41, s32[1]{0:T(128)} %bitcast.13.sec_ref, bf16[256,1280]{1,0:T(8,128)(2,1)S(1)} %get-tuple-element.65.mine_hbm, bf16[256,1280]{1,0:T(8,128)(2,1)} %collective-permute-done.12.other_ref, bf16[256,1280]{1,0:T(8,128)(2,1)} %bitcast.36, ...), custom_call_target="tpu_custom_call" | custom-call | flops 1 | bytes 1 | tf_op jit(solution)/shard_map/middle/pallas_call | solution.py:360
  82.6 3.9 %collective-permute-start.13 = (bf16[288,640]{1,0:T(8,128)(2,1)S(1)}, bf16[288,640]{1,0:T(8,128)(2,1)S(1)}, u32[]{:S(2)}, u32[]{:S(2)}) collective-permute-start(bf16[288,640]{1,0:T(8,128)(2,1)S(1)} %get-tuple-element.69.pay_ref.rest_0_), channel_id=1, source_target_pairs={{2,4},{4,2},{6,8},{8,6},{10,12},{12,10},{14,16},{16,14},{18,20},{2... | collective-permute-start | bytes 1105928 | tf_op jit(solution)/shard_map/ppermute | solution.py:670
  86.6 2.8 %collective-permute-start.15 = (bf16[288,640]{1,0:T(8,128)(2,1)S(1)}, bf16[288,640]{1,0:T(8,128)(2,1)S(1)}, u32[]{:S(2)}, u32[]{:S(2)}) collective-permute-start(bf16[288,640]{1,0:T(8,128)(2,1)S(1)} %get-tuple-element.69.pay_ref.rest_0_), channel_id=1, source_target_pairs={{32,64},{64,32},{33,65},{65,33},{34,66},{66,34},{35,67},{67,35},{3... | collective-permute-start | bytes 1105928 | tf_op jit(solution)/shard_map/ppermute | solution.py:667
  89.5 3.1 %collective-permute-start.16 = (bf16[288,640]{1,0:T(8,128)(2,1)S(1)}, bf16[288,640]{1,0:T(8,128)(2,1)S(1)}, u32[]{:S(2)}, u32[]{:S(2)}) collective-permute-start(bf16[288,640]{1,0:T(8,128)(2,1)S(1)} %get-tuple-element.69.pay_ref.rest_0_), channel_id=1, source_target_pairs={{0,2},{2,0},{4,6},{6,4},{8,10},{10,8},{12,14},{14,12},{16,18},{18,... | collective-permute-start | bytes 1105928 | tf_op jit(solution)/shard_map/ppermute | solution.py:673
  92.6 8.5 %query_grad.1.dq_ref = bf16[256,640]{1,0:T(8,128)(2,1)S(1)} custom-call(s32[4,8]{1,0:T(4,128)S(1)} %get-tuple-element.82.local_ref, bf16[288,640]{1,0:T(8,128)(2,1)S(1)} %get-tuple-element.69.pay_ref.rest_0_, bf16[48,64,1280]{2,1,0:T(8,128)(2,1)} %bitcast.45, bf16[8,64,1280]{2,1,0:T(8,128)(2,1)S(1)} %copy-done.1, bf16[4,512,512]{2,1,0:T(8,128)(2,1)} %get-tuple-element.71.p_ref), custom_call_target="tpu_custom_call" | custom-call | flops 1 | bytes 1 | tf_op jit(solution)/shard_map/query_grad/pallas_call | solution.py:482
  102.2 3.1 %collective-permute-start.20 = (bf16[288,640]{1,0:T(8,128)(2,1)S(1)}, bf16[288,640]{1,0:T(8,128)(2,1)S(1)}, u32[]{:S(2)}, u32[]{:S(2)}) collective-permute-start(bf16[288,640]{1,0:T(8,128)(2,1)S(1)} %collective-permute-done.13.rest_3_), channel_id=1, source_target_pairs={{32,64},{64,32},{33,65},{65,33},{34,66},{66,34},{35,67},{67,35},{3... | collective-permute-start | bytes 1105928 | tf_op jit(solution)/shard_map/ppermute | solution.py:667
  106.3 13.5 %key_near.1 = (f32[256,1280]{1,0:T(8,128)}, f32[256,1280]{1,0:T(8,128)}) custom-call(s32[4,25]{1,0:T(4,128)S(1)} %pad_add_fusion.6.list_ref, s32[4]{0:T(128)S(1)} %bitcast.42, bf16[4,64,640]{2,1,0:T(8,128)(2,1)S(1)} %bitcast.39, bf16[32,64,640]{2,1,0:T(8,128)(2,1)} %bitcast.54, bf16[48,64,1280]{2,1,0:T(8,128)(2,1)} %bitcast.46, ...), custom_call_target="tpu_custom_call" | custom-call | flops 1 | bytes 1 | tf_op jit(solution)/shard_map/key_near/pallas_call | solution.py:558
  119.9 10.3 %key_last.1 = (bf16[256,640]{1,0:T(8,128)(2,1)S(1)}, f32[256,640]{1,0:T(8,128)S(1)}) custom-call(s32[4,9]{1,0:T(4,128)S(1)} %pad_add_fusion.7.list_ref, s32[4]{0:T(128)S(1)} %bitcast.43, s32[1]{0:T(128)} %bitcast.13.sec_ref, bf16[32,64,640]{2,1,0:T(8,128)(2,1)} %bitcast.55, bf16[48,64,1280]{2,1,0:T(8,128)(2,1)} %bitcast.47, bf16[3,1280,640]{2,1,0:T(8,128)(2,1)} %bitcast.53, ...), custom_call_target="tpu_custom_call" | custom-call | flops 1 | bytes 1 | tf_op jit(solution)/shard_map/key_last/pallas_call | solution.py:627
  130.8 9.6 %collective-permute-done.21 = bf16[256,640]{1,0:T(8,128)(2,1)S(1)} collective-permute-done((bf16[256,640]{1,0:T(8,128)(2,1)S(1)}, bf16[256,640]{1,0:T(8,128)(2,1)S(1)}, u32[]{:S(2)}, u32[]{:S(2)}) %collective-permute-start.21) | collective-permute-done | bytes 327712 | tf_op jit(solution)/shard_map/ppermute | solution.py:739
  (82 shorter events, 11.1 us)
Async XLA Ops:
  0.0 10.2 %collective-permute-start.3 = (bf16[256,1280]{1,0:T(8,128)(2,1)}, bf16[256,1280]{1,0:T(8,128)(2,1)S(1)}, u32[]{:S(2)}, u32[]{:S(2)}) collective-permute-start(bf16[256,1280]{1,0:T(8,128)(2,1)} %bitcast.32), channel_id=1, source_target_pairs={{0,2},{2,0},{4,6},{6,4},{8,10},{10,8},{12,14},{14,12},{16,18},{18,... | collective-permute-start | bytes 1966088 | tf_op jit(solution)/shard_map/ppermute | solution.py:673
  0.0 19.9 %collective-permute-start.1 = (bf16[256,1280]{1,0:T(8,128)(2,1)}, bf16[256,1280]{1,0:T(8,128)(2,1)S(1)}, u32[]{:S(2)}, u32[]{:S(2)}) collective-permute-start(bf16[256,1280]{1,0:T(8,128)(2,1)} %bitcast.33), channel_id=1, source_target_pairs={{0,32},{32,0},{64,96},{96,64},{1,33},{33,1},{65,97},{97,65},{2,34}... | collective-permute-start | bytes 1966088 | tf_op jit(solution)/shard_map/ppermute | solution.py:664
  0.5 19.7 %collective-permute-start.2 = (bf16[256,1280]{1,0:T(8,128)(2,1)}, bf16[256,1280]{1,0:T(8,128)(2,1)S(1)}, u32[]{:S(2)}, u32[]{:S(2)}) collective-permute-start(bf16[256,1280]{1,0:T(8,128)(2,1)} %bitcast.34), channel_id=1, source_target_pairs={{32,64},{64,32},{33,65},{65,33},{34,66},{66,34},{35,67},{67,35},{3... | collective-permute-start | bytes 1966088 | tf_op jit(solution)/shard_map/ppermute | solution.py:667
  4.8 20.3 %collective-permute-start = (bf16[256,1280]{1,0:T(8,128)(2,1)}, bf16[256,1280]{1,0:T(8,128)(2,1)S(1)}, u32[]{:S(2)}, u32[]{:S(2)}) collective-permute-start(bf16[256,1280]{1,0:T(8,128)(2,1)} %bitcast.35), channel_id=1, source_target_pairs={{2,4},{4,2},{6,8},{8,6},{10,12},{12,10},{14,16},{16,14},{18,20},{2... | collective-permute-start | bytes 1966088 | tf_op jit(solution)/shard_map/ppermute | solution.py:670
  10.3 9.9 %collective-permute-start.4 = (s32[5,8]{1,0:T(8,128)S(1)}, s32[5,8]{1,0:T(8,128)S(1)}, u32[]{:S(2)}, u32[]{:S(2)}) collective-permute-start(s32[5,8]{1,0:T(8,128)S(1)} %pad_add_fusion.5), channel_id=1, source_target_pairs={{0,32},{32,0},{64,96},{96,64},{1,33},{33,1},{65,97},{97,65},{2,34}... | collective-permute-start | bytes 488 | tf_op jit(solution)/shard_map/ppermute | solution.py:664
  10.3 9.8 %collective-permute-start.5 = (s32[5,8]{1,0:T(8,128)S(1)}, s32[5,8]{1,0:T(8,128)S(1)}, u32[]{:S(2)}, u32[]{:S(2)}) collective-permute-start(s32[5,8]{1,0:T(8,128)S(1)} %pad_add_fusion.5), channel_id=1, source_target_pairs={{32,64},{64,32},{33,65},{65,33},{34,66},{66,34},{35,67},{67,35},{3... | collective-permute-start | bytes 488 | tf_op jit(solution)/shard_map/ppermute | solution.py:667
  14.3 22.6 %copy-start.5 = (f32[1280]{0:T(1024)S(1)}, f32[1280]{0:T(1024)}, u32[]{:S(2)}) copy-start(f32[1280]{0:T(1024)} %rest_3_.1) | copy-start | bytes 15364
  25.1 7.4 %collective-permute-start.6 = (s32[3,5,8]{2,1,0:T(8,128)S(1)}, s32[3,5,8]{2,1,0:T(8,128)S(1)}, u32[]{:S(2)}, u32[]{:S(2)}) collective-permute-start(s32[3,5,8]{2,1,0:T(8,128)S(1)} %pad_add_fusion.3), channel_id=1, source_target_pairs={{2,4},{4,2},{6,8},{8,6},{10,12},{12,10},{14,16},{16,14},{18,20},{2... | collective-permute-start | bytes 1448 | tf_op jit(solution)/shard_map/ppermute | solution.py:670
  30.0 6.1 %collective-permute-start.10 = (bf16[256,1280]{1,0:T(8,128)(2,1)S(1)}, bf16[256,1280]{1,0:T(8,128)(2,1)S(1)}, u32[]{:S(2)}, u32[]{:S(2)}) collective-permute-start(bf16[256,1280]{1,0:T(8,128)(2,1)S(1)} %collective-permute-done.1.refs_0_), channel_id=1, source_target_pairs={{0,2},{2,0},{4,6},{6,4},{8,10},{10,8},{12,14},{14,12},{16,18},{18,... | collective-permute-start | bytes 1966088 | tf_op jit(solution)/shard_map/ppermute | solution.py:673
  30.2 5.9 %collective-permute-start.11 = (bf16[256,1280]{1,0:T(8,128)(2,1)S(1)}, bf16[256,1280]{1,0:T(8,128)(2,1)}, u32[]{:S(2)}, u32[]{:S(2)}) collective-permute-start(bf16[256,1280]{1,0:T(8,128)(2,1)S(1)} %collective-permute-done.2.refs_1_), channel_id=1, source_target_pairs={{0,2},{2,0},{4,6},{6,4},{8,10},{10,8},{12,14},{14,12},{16,18},{18,... | collective-permute-start | bytes 1966088 | tf_op jit(solution)/shard_map/ppermute | solution.py:673
  30.6 4.1 %collective-permute-start.7 = (s32[3,5,8]{2,1,0:T(8,128)S(1)}, s32[3,5,8]{2,1,0:T(8,128)S(1)}, u32[]{:S(2)}, u32[]{:S(2)}) collective-permute-start(s32[3,5,8]{2,1,0:T(8,128)S(1)} %pad_add_fusion.3), channel_id=1, source_target_pairs={{0,2},{2,0},{4,6},{6,4},{8,10},{10,8},{12,14},{14,12},{16,18},{18,... | collective-permute-start | bytes 1448 | tf_op jit(solution)/shard_map/ppermute | solution.py:673
  30.7 18.6 %collective-permute-start.8 = (bf16[256,1280]{1,0:T(8,128)(2,1)S(1)}, bf16[256,1280]{1,0:T(8,128)(2,1)}, u32[]{:S(2)}, u32[]{:S(2)}) collective-permute-start(bf16[256,1280]{1,0:T(8,128)(2,1)S(1)} %collective-permute-done.refs_2_), channel_id=1, source_target_pairs={{0,32},{32,0},{64,96},{96,64},{1,33},{33,1},{65,97},{97,65},{2,34}... | collective-permute-start | bytes 1966088 | tf_op jit(solution)/shard_map/ppermute | solution.py:664
  32.5 17.6 %collective-permute-start.9 = (bf16[256,1280]{1,0:T(8,128)(2,1)S(1)}, bf16[256,1280]{1,0:T(8,128)(2,1)}, u32[]{:S(2)}, u32[]{:S(2)}) collective-permute-start(bf16[256,1280]{1,0:T(8,128)(2,1)S(1)} %collective-permute-done.refs_2_), channel_id=1, source_target_pairs={{32,64},{64,32},{33,65},{65,33},{34,66},{66,34},{35,67},{67,35},{3... | collective-permute-start | bytes 1966088 | tf_op jit(solution)/shard_map/ppermute | solution.py:667
  62.4 14.8 %collective-permute-start.12 = (bf16[256,1280]{1,0:T(8,128)(2,1)S(1)}, bf16[256,1280]{1,0:T(8,128)(2,1)}, u32[]{:S(2)}, u32[]{:S(2)}) collective-permute-start(bf16[256,1280]{1,0:T(8,128)(2,1)S(1)} %get-tuple-element.65.mine_hbm), channel_id=1, source_target_pairs={{0,1},{1,0},{2,3},{3,2},{4,5},{5,4},{6,7},{7,6},{8,9},{9,8},{10,11... | collective-permute-start | bytes 1966088 | tf_op jit(solution)/shard_map/ppermute | solution.py:725
  82.6 18.4 %copy-start.2 = (f32[256,640]{1,0:T(8,128)}, f32[256,640]{1,0:T(8,128)S(1)}, u32[]{:S(2)}) copy-start(f32[256,640]{1,0:T(8,128)S(1)} %get-tuple-element.78.rest_5_) | copy-start | bytes 1966084
  82.6 18.4 %collective-permute-start.13 = (bf16[288,640]{1,0:T(8,128)(2,1)S(1)}, bf16[288,640]{1,0:T(8,128)(2,1)S(1)}, u32[]{:S(2)}, u32[]{:S(2)}) collective-permute-start(bf16[288,640]{1,0:T(8,128)(2,1)S(1)} %get-tuple-element.69.pay_ref.rest_0_), channel_id=1, source_target_pairs={{2,4},{4,2},{6,8},{8,6},{10,12},{12,10},{14,16},{16,14},{18,20},{2... | collective-permute-start | bytes 1105928 | tf_op jit(solution)/shard_map/ppermute | solution.py:670
  86.5 14.5 %collective-permute-start.14 = (bf16[288,640]{1,0:T(8,128)(2,1)S(1)}, bf16[288,640]{1,0:T(8,128)(2,1)S(1)}, u32[]{:S(2)}, u32[]{:S(2)}) collective-permute-start(bf16[288,640]{1,0:T(8,128)(2,1)S(1)} %get-tuple-element.69.pay_ref.rest_0_), channel_id=1, source_target_pairs={{0,32},{32,0},{64,96},{96,64},{1,33},{33,1},{65,97},{97,65},{2,34}... | collective-permute-start | bytes 1105928 | tf_op jit(solution)/shard_map/ppermute | solution.py:664
  86.6 14.4 %collective-permute-start.15 = (bf16[288,640]{1,0:T(8,128)(2,1)S(1)}, bf16[288,640]{1,0:T(8,128)(2,1)S(1)}, u32[]{:S(2)}, u32[]{:S(2)}) collective-permute-start(bf16[288,640]{1,0:T(8,128)(2,1)S(1)} %get-tuple-element.69.pay_ref.rest_0_), channel_id=1, source_target_pairs={{32,64},{64,32},{33,65},{65,33},{34,66},{66,34},{35,67},{67,35},{3... | collective-permute-start | bytes 1105928 | tf_op jit(solution)/shard_map/ppermute | solution.py:667
  89.5 15.8 %collective-permute-start.16 = (bf16[288,640]{1,0:T(8,128)(2,1)S(1)}, bf16[288,640]{1,0:T(8,128)(2,1)S(1)}, u32[]{:S(2)}, u32[]{:S(2)}) collective-permute-start(bf16[288,640]{1,0:T(8,128)(2,1)S(1)} %get-tuple-element.69.pay_ref.rest_0_), channel_id=1, source_target_pairs={{0,2},{2,0},{4,6},{6,4},{8,10},{10,8},{12,14},{14,12},{16,18},{18,... | collective-permute-start | bytes 1105928 | tf_op jit(solution)/shard_map/ppermute | solution.py:673
  101.1 4.3 %collective-permute-start.17 = (bf16[288,640]{1,0:T(8,128)(2,1)S(1)}, bf16[288,640]{1,0:T(8,128)(2,1)S(1)}, u32[]{:S(2)}, u32[]{:S(2)}) collective-permute-start(bf16[288,640]{1,0:T(8,128)(2,1)S(1)} %collective-permute-done.14.rest_1_), channel_id=1, source_target_pairs={{0,2},{2,0},{4,6},{6,4},{8,10},{10,8},{12,14},{14,12},{16,18},{18,... | collective-permute-start | bytes 1105928 | tf_op jit(solution)/shard_map/ppermute | solution.py:673
  101.2 4.2 %collective-permute-start.18 = (bf16[288,640]{1,0:T(8,128)(2,1)S(1)}, bf16[288,640]{1,0:T(8,128)(2,1)S(1)}, u32[]{:S(2)}, u32[]{:S(2)}) collective-permute-start(bf16[288,640]{1,0:T(8,128)(2,1)S(1)} %collective-permute-done.15.rest_2_), channel_id=1, source_target_pairs={{0,2},{2,0},{4,6},{6,4},{8,10},{10,8},{12,14},{14,12},{16,18},{18,... | collective-permute-start | bytes 1105928 | tf_op jit(solution)/shard_map/ppermute | solution.py:673
  101.7 18.2 %collective-permute-start.19 = (bf16[288,640]{1,0:T(8,128)(2,1)S(1)}, bf16[288,640]{1,0:T(8,128)(2,1)S(1)}, u32[]{:S(2)}, u32[]{:S(2)}) collective-permute-start(bf16[288,640]{1,0:T(8,128)(2,1)S(1)} %collective-permute-done.13.rest_3_), channel_id=1, source_target_pairs={{0,32},{32,0},{64,96},{96,64},{1,33},{33,1},{65,97},{97,65},{2,34}... | collective-permute-start | bytes 1105928 | tf_op jit(solution)/shard_map/ppermute | solution.py:664
  102.2 17.7 %collective-permute-start.20 = (bf16[288,640]{1,0:T(8,128)(2,1)S(1)}, bf16[288,640]{1,0:T(8,128)(2,1)S(1)}, u32[]{:S(2)}, u32[]{:S(2)}) collective-permute-start(bf16[288,640]{1,0:T(8,128)(2,1)S(1)} %collective-permute-done.13.rest_3_), channel_id=1, source_target_pairs={{32,64},{64,32},{33,65},{65,33},{34,66},{66,34},{35,67},{67,35},{3... | collective-permute-start | bytes 1105928 | tf_op jit(solution)/shard_map/ppermute | solution.py:667
  130.2 10.3 %collective-permute-start.21 = (bf16[256,640]{1,0:T(8,128)(2,1)S(1)}, bf16[256,640]{1,0:T(8,128)(2,1)S(1)}, u32[]{:S(2)}, u32[]{:S(2)}) collective-permute-start(bf16[256,640]{1,0:T(8,128)(2,1)S(1)} %get-tuple-element.80), channel_id=1, source_target_pairs={{0,1},{1,0},{2,3},{3,2},{4,5},{5,4},{6,7},{7,6},{8,9},{9,8},{10,11... | collective-permute-start | bytes 983048 | tf_op jit(solution)/shard_map/ppermute | solution.py:739
  (11 other events, 48.5 us)
